TPU v7x, 32 devices: a whole 2x2x4 slice. The times are simulated.
32 devices in a mesh: rep: 4 (over z), fsdp: 8 (over y, x, core).
Axes of the slice: x: 2, y: 2, z: 4, core: 2. Of those that a mesh axis runs over, the one named last changes fastest.
Arguments:
- inputs: bfloat16 [32, 1024, 1024], P(('rep', 'fsdp')), may hold values from -6 to 6
- lengths: int32 [32], P(('rep', 'fsdp')), may hold values from 800 to 1024
- bucket_table: int32 [1024], replicated, may hold values from 0 to 31, as said below
- ln1_gain: bfloat16 [1024], P('fsdp'), may hold values from 0.099609375 to 1.8984375
- ln1_shift: bfloat16 [1024], P('fsdp'), may hold values from -3 to 3
- w_qkv: bfloat16 [1024, 3072], P('fsdp'), may hold values from -0.1875 to 0.1875
- rel_bias: bfloat16 [512], P('fsdp'), may hold values from -4 to 4
- w_out: bfloat16 [1024, 1024], P('fsdp'), may hold values from -3 to 3
- ln2_gain: bfloat16 [1024], P('fsdp'), may hold values from 0.099609375 to 1.8984375
- ln2_shift: bfloat16 [1024], P('fsdp'), may hold values from -3 to 3
- w_in: bfloat16 [1024, 4096], P('fsdp'), may hold values from -0.1875 to 0.1875
- w_down: bfloat16 [4096, 1024], P('fsdp'), may hold values from -0.09375 to 0.09375
- cotangent: bfloat16 [32, 1024, 1024], P(('rep', 'fsdp')), may hold values from -6 to 6
Outputs:
- outputs: bfloat16 [32, 1024, 1024], P(('rep', 'fsdp'))
- input_grad: float32 [32, 1024, 1024], P(('rep', 'fsdp'))
- ln1_gain_grad: float32 [1024], P('fsdp')
- ln1_shift_grad: float32 [1024], P('fsdp')
- w_qkv_grad: float32 [1024, 3072], P('fsdp')
- rel_bias_grad: float32 [512], P('fsdp')
- w_out_grad: float32 [1024, 1024], P('fsdp')
- ln2_gain_grad: float32 [1024], P('fsdp')
- ln2_shift_grad: float32 [1024], P('fsdp')
- w_in_grad: float32 [1024, 4096], P('fsdp')
- w_down_grad: float32 [4096, 1024], P('fsdp')
Inputs may be any that keep to these rules, and one draw needn't show every extreme that they name: bucket_table[k] = k for k < 16; it never falls as k grows and takes every value from 0 to 31.
All inputs are finite; a program needn't handle non-finite values.
Results may differ from a plain program's by a relative error of at most 0.017.
Values may be sent and summed in bfloat16 or wider, within the bound.
No kernel may reach another device: no remote copies, remote signals or barrier semaphores. Data moves between devices by JAX's collectives and lax.ppermute only.
A program may use at most 512 MiB of HBM per device.

v0:
```python
import jax
import jax.numpy as jnp
from jax import lax
from jax.sharding import PartitionSpec as P

HEADS = 16
HEAD_DIM = 64
BUCKETS = 32


def layer_norm(values, gain_row, shift_row):
    average = jnp.mean(values, axis=-1, keepdims=True)
    centred = values - average
    spread = jnp.mean(centred * centred, axis=-1, keepdims=True)
    return centred * lax.rsqrt(spread + 1e-05) * gain_row + shift_row


def gelu_exact(values):
    return jax.nn.gelu(values, approximate=False)


def bucket_onehot(bucket_table, bucket_count):
    return (bucket_table[:, None] == lax.iota(jnp.int32, bucket_count)[None, :]).astype(
        jnp.bfloat16
    )


def distance_bias(bucket_table, table_heads, margin):
    onehot = bucket_onehot(bucket_table, table_heads.shape[1])
    by_distance = jnp.einsum(
        "hb,sb->hs", table_heads, onehot, preferred_element_type=jnp.float32
    ).astype(jnp.bfloat16)
    return jnp.pad(by_distance, ((0, 0), (margin, 0)))


def bias_tile(bias_ext, margin, first_row, first_col, row_count, col_count):
    span_len = row_count + col_count - 1
    low_dist = first_row - first_col - (col_count - 1)
    window = bias_ext[:, margin + low_dist : margin + low_dist + span_len]
    turned = jnp.roll(window[:, ::-1], -(row_count - 1), axis=1)
    head_count = window.shape[0]
    flat = jnp.broadcast_to(turned[:, None, :], (head_count, row_count, span_len)).reshape(
        head_count, row_count * span_len
    )
    skewed = flat[:, : row_count * (span_len - 1)].reshape(head_count, row_count, span_len - 1)
    return skewed[:, :, :col_count]


def tile_scores(
    query_block, key_tile, first_row, first_col, clip_length, bias_ext, margin, score_scale
):
    row_count = query_block.shape[0]
    col_count = key_tile.shape[0]
    row_ids = first_row + lax.iota(jnp.int32, row_count)
    col_ids = first_col + lax.iota(jnp.int32, col_count)
    distance = row_ids[:, None] - col_ids[None, :]
    bias_part = bias_tile(bias_ext, margin, first_row, first_col, row_count, col_count)
    raw_scores = jnp.einsum(
        "ihd,jhd->hij", query_block, key_tile, preferred_element_type=jnp.float32
    )
    allowed = (distance >= 0) & (col_ids[None, :] < clip_length)
    return jnp.where(allowed[None], raw_scores * score_scale + bias_part, -1e30)


def diagonal_sums(tile):
    head_count, row_count, col_count = tile.shape
    wide = col_count + row_count
    padded = jnp.pad(tile, ((0, 0), (0, 0), (row_count, 0)))
    flat = jnp.pad(padded.reshape(head_count, row_count * wide), ((0, 0), (0, row_count)))
    skewed = flat.reshape(head_count, row_count, wide + 1)
    sums = jnp.sum(skewed.astype(jnp.float32), axis=1)
    return sums[:, 1:wide][:, ::-1]


def block_sizes(slot_count):
    return (min(512, slot_count), min(256, slot_count))


def attend_forward(queries, key_rows, value_rows, clip_length, bias_ext, margin):
    slot_count, head_count, head_size = queries.shape
    query_rows, key_cols = block_sizes(slot_count)
    score_scale = head_size ** (-0.5)
    pieces = []
    totals = []
    for first_row in range(0, slot_count, query_rows):
        query_block = queries[first_row : first_row + query_rows]
        starts = [
            first_col
            for first_col in range(0, slot_count, key_cols)
            if first_col <= first_row + query_rows - 1
        ]
        running_max = jnp.full((head_count, query_rows), -1e30, jnp.float32)
        running_total = jnp.zeros((head_count, query_rows), jnp.float32)
        for first_col in starts:
            scores = tile_scores(
                query_block,
                key_rows[first_col : first_col + key_cols],
                first_row,
                first_col,
                clip_length,
                bias_ext,
                margin,
                score_scale,
            )
            new_max = jnp.maximum(running_max, jnp.max(scores, axis=-1))
            running_total = running_total * jnp.exp(running_max - new_max) + jnp.sum(
                jnp.exp(scores - new_max[..., None]), axis=-1
            )
            running_max = new_max
        log_total = running_max + jnp.log(running_total)
        attended = jnp.zeros((query_rows, head_count, head_size), jnp.float32)
        for first_col in starts:
            value_tile = value_rows[first_col : first_col + key_cols]
            scores = tile_scores(
                query_block,
                key_rows[first_col : first_col + key_cols],
                first_row,
                first_col,
                clip_length,
                bias_ext,
                margin,
                score_scale,
            )
            prob_low = jnp.exp(scores - log_total[..., None]).astype(jnp.bfloat16)
            attended = attended + jnp.einsum(
                "hij,jhd->ihd", prob_low, value_tile, preferred_element_type=jnp.float32
            )
        pieces.append(attended)
        totals.append(log_total)
    return (jnp.concatenate(pieces, axis=0), jnp.concatenate(totals, axis=1))


def attend_backward(
    queries,
    key_rows,
    value_rows,
    attended_grad,
    log_totals,
    attended_out,
    clip_length,
    bias_ext,
    margin,
):
    slot_count, head_count, head_size = queries.shape
    query_rows, key_cols = block_sizes(slot_count)
    score_scale = head_size ** (-0.5)
    key_grad = jnp.zeros(key_rows.shape, jnp.float32)
    value_grad = jnp.zeros(value_rows.shape, jnp.float32)
    edge = query_rows + key_cols
    distance_grad = jnp.zeros((head_count, slot_count + 2 * edge), jnp.float32)
    query_parts = []
    for first_row in range(0, slot_count, query_rows):
        query_block = queries[first_row : first_row + query_rows]
        grad_block = attended_grad[first_row : first_row + query_rows]
        log_total = log_totals[:, first_row : first_row + query_rows]
        inner = jnp.einsum(
            "ihd,ihd->hi",
            grad_block.astype(jnp.float32),
            attended_out[first_row : first_row + query_rows],
        )
        query_grad = jnp.zeros(query_block.shape, jnp.float32)
        for first_col in range(0, slot_count, key_cols):
            if first_col > first_row + query_rows - 1:
                continue
            key_tile = key_rows[first_col : first_col + key_cols]
            value_tile = value_rows[first_col : first_col + key_cols]
            scores = tile_scores(
                query_block,
                key_tile,
                first_row,
                first_col,
                clip_length,
                bias_ext,
                margin,
                score_scale,
            )
            probs = jnp.exp(scores - log_total[..., None])
            prob_low = probs.astype(jnp.bfloat16)
            value_grad = value_grad.at[first_col : first_col + key_cols].add(
                jnp.einsum("hij,ihd->jhd", prob_low, grad_block, preferred_element_type=jnp.float32)
            )
            prob_grad = jnp.einsum(
                "ihd,jhd->hij", grad_block, value_tile, preferred_element_type=jnp.float32
            )
            score_grad = (probs * (prob_grad - inner[..., None])).astype(jnp.bfloat16)
            query_grad = (
                query_grad
                + jnp.einsum(
                    "hij,jhd->ihd", score_grad, key_tile, preferred_element_type=jnp.float32
                )
                * score_scale
            )
            key_grad = key_grad.at[first_col : first_col + key_cols].add(
                jnp.einsum(
                    "hij,ihd->jhd", score_grad, query_block, preferred_element_type=jnp.float32
                )
                * score_scale
            )
            offset = first_row - first_col - (key_cols - 1) + edge
            distance_grad = distance_grad.at[:, offset : offset + query_rows + key_cols - 1].add(
                diagonal_sums(score_grad)
            )
        query_parts.append(query_grad)
    return (
        jnp.concatenate(query_parts, axis=0),
        key_grad,
        value_grad,
        distance_grad[:, edge : edge + slot_count],
    )


def per_device(
    inputs,
    lengths,
    bucket_table,
    ln1_gain,
    ln1_shift,
    w_qkv,
    rel_bias,
    w_out,
    ln2_gain,
    ln2_shift,
    w_in,
    w_down,
    cotangent,
):
    gain_one, shift_one, qkv_full, table_flat, out_full = (
        lax.all_gather(ln1_gain, "fsdp", axis=0, tiled=True),
        lax.all_gather(ln1_shift, "fsdp", axis=0, tiled=True),
        lax.all_gather(w_qkv, "fsdp", axis=0, tiled=True),
        lax.all_gather(rel_bias, "fsdp", axis=0, tiled=True),
        lax.all_gather(w_out, "fsdp", axis=0, tiled=True),
    )
    gain_two, shift_two, in_full, down_full = (
        lax.all_gather(ln2_gain, "fsdp", axis=0, tiled=True),
        lax.all_gather(ln2_shift, "fsdp", axis=0, tiled=True),
        lax.all_gather(w_in, "fsdp", axis=0, tiled=True),
        lax.all_gather(w_down, "fsdp", axis=0, tiled=True),
    )
    clip_count, slot_count, width = inputs.shape
    row_count = clip_count * slot_count
    margin = block_sizes(slot_count)[0] + block_sizes(slot_count)[1]
    table_heads = table_flat.reshape(HEADS, BUCKETS)
    bias_ext = distance_bias(bucket_table, table_heads, margin)
    gain_one_f = gain_one.astype(jnp.float32)
    shift_one_f = shift_one.astype(jnp.float32)
    gain_two_f = gain_two.astype(jnp.float32)
    shift_two_f = shift_two.astype(jnp.float32)
    residual = inputs.reshape(row_count, width).astype(jnp.float32)
    normed_one = layer_norm(residual, gain_one_f, shift_one_f).astype(jnp.bfloat16)
    projected = jnp.dot(normed_one, qkv_full, preferred_element_type=jnp.float32).astype(
        jnp.bfloat16
    )
    shaped = projected.reshape(clip_count, slot_count, 3, HEADS, HEAD_DIM)
    queries = shaped[:, :, 0]
    key_rows = shaped[:, :, 1]
    value_rows = shaped[:, :, 2]

    def forward_clip(clip_item):
        return attend_forward(
            clip_item[0], clip_item[1], clip_item[2], clip_item[3], bias_ext, margin
        )

    attended, log_totals = lax.map(forward_clip, (queries, key_rows, value_rows, lengths))
    attended_low = attended.reshape(row_count, width).astype(jnp.bfloat16)
    middle = residual + jnp.dot(attended_low, out_full, preferred_element_type=jnp.float32)
    normed_two = layer_norm(middle, gain_two_f, shift_two_f).astype(jnp.bfloat16)
    hidden_pre = jnp.dot(normed_two, in_full, preferred_element_type=jnp.float32)
    hidden = gelu_exact(hidden_pre).astype(jnp.bfloat16)
    ffn_out = jnp.dot(hidden, down_full, preferred_element_type=jnp.float32)
    slot_ids = lax.iota(jnp.int32, slot_count)
    valid = (slot_ids[None, :] < lengths[:, None]).astype(jnp.float32).reshape(row_count, 1)
    outputs = (
        ((middle + ffn_out) * valid).astype(jnp.bfloat16).reshape(clip_count, slot_count, width)
    )
    gain_back, shift_back, in_back, down_back = (
        lax.all_gather(ln2_gain, "fsdp", axis=0, tiled=True),
        lax.all_gather(ln2_shift, "fsdp", axis=0, tiled=True),
        lax.all_gather(w_in, "fsdp", axis=0, tiled=True),
        lax.all_gather(w_down, "fsdp", axis=0, tiled=True),
    )
    gain_two_b = gain_back.astype(jnp.float32)
    out_grad_rows = cotangent.reshape(row_count, width).astype(jnp.float32) * valid
    out_low = out_grad_rows.astype(jnp.bfloat16)
    down_grad = jnp.einsum("rf,rd->fd", hidden, out_low, preferred_element_type=jnp.float32)
    hidden_grad = jnp.einsum("rd,fd->rf", out_low, down_back, preferred_element_type=jnp.float32)
    unused, gelu_back = jax.vjp(gelu_exact, hidden_pre)
    pre_grad = gelu_back(hidden_grad)[0].astype(jnp.bfloat16)
    in_grad = jnp.einsum("rd,rf->df", normed_two, pre_grad, preferred_element_type=jnp.float32)
    normed_two_grad = jnp.einsum("rf,df->rd", pre_grad, in_back, preferred_element_type=jnp.float32)
    unused, norm_back_two = jax.vjp(layer_norm, middle, gain_two_b, shift_two_f)
    middle_part, gain_two_grad, shift_two_grad = norm_back_two(normed_two_grad)
    middle_grad = out_grad_rows + middle_part
    gain_back_one, shift_back_one, qkv_back, table_back, out_back = (
        lax.all_gather(ln1_gain, "fsdp", axis=0, tiled=True),
        lax.all_gather(ln1_shift, "fsdp", axis=0, tiled=True),
        lax.all_gather(w_qkv, "fsdp", axis=0, tiled=True),
        lax.all_gather(rel_bias, "fsdp", axis=0, tiled=True),
        lax.all_gather(w_out, "fsdp", axis=0, tiled=True),
    )
    gain_one_b = gain_back_one.astype(jnp.float32)
    bias_back = distance_bias(bucket_table, table_back.reshape(HEADS, BUCKETS), margin)
    branch_grad = middle_grad.astype(jnp.bfloat16)
    out_w_grad = jnp.einsum(
        "rk,rd->kd", attended_low, branch_grad, preferred_element_type=jnp.float32
    )
    attended_grad = jnp.einsum(
        "rd,kd->rk", branch_grad, out_back, preferred_element_type=jnp.float32
    ).astype(jnp.bfloat16)
    attended_grad = attended_grad.reshape(clip_count, slot_count, HEADS, HEAD_DIM)

    def backward_clip(clip_item):
        return attend_backward(
            clip_item[0],
            clip_item[1],
            clip_item[2],
            clip_item[3],
            clip_item[4],
            clip_item[5],
            clip_item[6],
            bias_back,
            margin,
        )

    query_grad, key_grad, value_grad, distance_grads = lax.map(
        backward_clip, (queries, key_rows, value_rows, attended_grad, log_totals, attended, lengths)
    )
    distance_total = jnp.sum(distance_grads, axis=0)
    onehot_f = bucket_onehot(bucket_table, BUCKETS).astype(jnp.float32)
    table_grad = jnp.dot(
        distance_total,
        onehot_f,
        precision=lax.Precision.HIGHEST,
        preferred_element_type=jnp.float32,
    ).reshape(HEADS * BUCKETS)
    projected_grad = (
        jnp.stack([query_grad, key_grad, value_grad], axis=2)
        .reshape(row_count, 3 * width)
        .astype(jnp.bfloat16)
    )
    qkv_grad = jnp.einsum(
        "rd,re->de", normed_one, projected_grad, preferred_element_type=jnp.float32
    )
    normed_one_grad = jnp.einsum(
        "re,de->rd", projected_grad, qkv_back, preferred_element_type=jnp.float32
    )
    unused, norm_back_one = jax.vjp(layer_norm, residual, gain_one_b, shift_one_f)
    input_part, gain_one_grad, shift_one_grad = norm_back_one(normed_one_grad)
    input_grad = (middle_grad + input_part).reshape(clip_count, slot_count, width)
    shards = (
        lax.psum_scatter(gain_one_grad, "fsdp", scatter_dimension=0, tiled=True),
        lax.psum_scatter(shift_one_grad, "fsdp", scatter_dimension=0, tiled=True),
        lax.psum_scatter(qkv_grad, "fsdp", scatter_dimension=0, tiled=True),
        lax.psum_scatter(table_grad, "fsdp", scatter_dimension=0, tiled=True),
        lax.psum_scatter(out_w_grad, "fsdp", scatter_dimension=0, tiled=True),
        lax.psum_scatter(gain_two_grad, "fsdp", scatter_dimension=0, tiled=True),
        lax.psum_scatter(shift_two_grad, "fsdp", scatter_dimension=0, tiled=True),
        lax.psum_scatter(in_grad, "fsdp", scatter_dimension=0, tiled=True),
        lax.psum_scatter(down_grad, "fsdp", scatter_dimension=0, tiled=True),
    )
    final_grads = (
        lax.psum(shards[0].astype(jnp.bfloat16), "rep").astype(jnp.float32),
        lax.psum(shards[1].astype(jnp.bfloat16), "rep").astype(jnp.float32),
        lax.psum(shards[2].astype(jnp.bfloat16), "rep").astype(jnp.float32),
        lax.psum(shards[3].astype(jnp.bfloat16), "rep").astype(jnp.float32),
        lax.psum(shards[4].astype(jnp.bfloat16), "rep").astype(jnp.float32),
        lax.psum(shards[5].astype(jnp.bfloat16), "rep").astype(jnp.float32),
        lax.psum(shards[6].astype(jnp.bfloat16), "rep").astype(jnp.float32),
        lax.psum(shards[7].astype(jnp.bfloat16), "rep").astype(jnp.float32),
        lax.psum(shards[8].astype(jnp.bfloat16), "rep").astype(jnp.float32),
    )
    return (
        outputs,
        input_grad,
        final_grads[0],
        final_grads[1],
        final_grads[2],
        final_grads[3],
        final_grads[4],
        final_grads[5],
        final_grads[6],
        final_grads[7],
        final_grads[8],
    )


def solution(mesh):
    placed = (
        P(("rep", "fsdp"), None, None),
        P(("rep", "fsdp")),
        P(),
        P("fsdp"),
        P("fsdp"),
        P("fsdp", None),
        P("fsdp"),
        P("fsdp", None),
        P("fsdp"),
        P("fsdp"),
        P("fsdp", None),
        P("fsdp", None),
        P(("rep", "fsdp"), None, None),
    )
    return jax.shard_map(
        per_device,
        mesh=mesh,
        in_specs=placed,
        out_specs=(
            P(("rep", "fsdp"), None, None),
            P(("rep", "fsdp"), None, None),
            P("fsdp"),
            P("fsdp"),
            P("fsdp", None),
            P("fsdp"),
            P("fsdp", None),
            P("fsdp"),
            P("fsdp"),
            P("fsdp", None),
            P("fsdp", None),
        ),
        check_vma=False,
    )
```

profile of v0, /device:TPU:0, one launch (start us, length us, event | category | flops | bytes accessed | tf_op | source)
XLA Modules:
  0.0 1657.6 jit_solution(15786511539205055053)
XLA Ops:
  12.9 15.3 all-reduce.17
  36.0 7.7 all-gather
  43.8 8.8 all-gather.1
  59.2 28.6 %reshape.1378 = bf16[16,392704]{1,0:T(8,128)(2,1)} reshape(bf16[16,512,767]{2,1,0:T(8,128)(2,1)} %broadcast_in_dim.473) | data formatting | bytes 25133056 | tf_op jit(solution)/shard_map/while/body/eval_jaxpr/reshape | solution.py:42
  87.9 10.5 slice.972
  98.4 43.0 %reshape.1379 = bf16[16,512,766]{2,1,0:T(8,128)(2,1)} reshape(bf16[16,392192]{1,0:T(8,128)(2,1)} %slice.972) | data formatting | bytes 25100288 | tf_op jit(solution)/shard_map/while/body/eval_jaxpr/reshape | solution.py:45
  158.2 29.8 %reshape.1380 = bf16[16,392704]{1,0:T(8,128)(2,1)} reshape(bf16[16,512,767]{2,1,0:T(8,128)(2,1)} %broadcast_in_dim.477) | data formatting | bytes 25133056 | tf_op jit(solution)/shard_map/while/body/eval_jaxpr/reshape | solution.py:42
  188.0 10.6 slice.975
  198.6 41.8 %reshape.1381 = bf16[16,512,766]{2,1,0:T(8,128)(2,1)} reshape(bf16[16,392192]{1,0:T(8,128)(2,1)} %slice.975) | data formatting | bytes 25100288 | tf_op jit(solution)/shard_map/while/body/eval_jaxpr/reshape | solution.py:45
  257.4 28.6 %reshape.1382 = bf16[16,392704]{1,0:T(8,128)(2,1)} reshape(bf16[16,512,767]{2,1,0:T(8,128)(2,1)} %broadcast_in_dim.480) | data formatting | bytes 25133056 | tf_op jit(solution)/shard_map/while/body/eval_jaxpr/reshape | solution.py:42
  286.1 10.5 slice.981
  296.6 41.9 %reshape.1383 = bf16[16,512,766]{2,1,0:T(8,128)(2,1)} reshape(bf16[16,392192]{1,0:T(8,128)(2,1)} %slice.981) | data formatting | bytes 25100288 | tf_op jit(solution)/shard_map/while/body/eval_jaxpr/reshape | solution.py:45
  355.4 28.6 %reshape.1384 = bf16[16,392704]{1,0:T(8,128)(2,1)} reshape(bf16[16,512,767]{2,1,0:T(8,128)(2,1)} %broadcast_in_dim.483) | data formatting | bytes 25133056 | tf_op jit(solution)/shard_map/while/body/eval_jaxpr/reshape | solution.py:42
  384.0 10.5 slice.985
  394.5 42.0 %reshape.1385 = bf16[16,512,766]{2,1,0:T(8,128)(2,1)} reshape(bf16[16,392192]{1,0:T(8,128)(2,1)} %slice.985) | data formatting | bytes 25100288 | tf_op jit(solution)/shard_map/while/body/eval_jaxpr/reshape | solution.py:45
  441.1 6.4 copy.221
  447.6 7.6 all-gather.2
  455.2 8.9 all-gather.3
  470.8 12.0 convolution_convert_fusion
  482.8 8.6 copy.124
  521.3 6.4 fusion.90
  537.3 6.7 fusion.134
  567.6 48.5 %multiply_convert_fusion = (bf16[1024,4096]{1,0:T(8,128)(2,1)}, f32[1024,4096]{1,0:T(8,128)}, f32[1024,4096]{1,0:T(8,128)}) fusion(bf16[1024,4096]{1,0:T(8,128)(2,1)} %all-gather.13.cloned.1.call-done, bf16[1024,1024]{0,1:T(8,128)(2,1)} %add_convert_fusion.3.clone.4), kind=kOutput, calls=%fused_computation.3 | convolution fusion | flops 8862564352 | bytes 52428800 | tf_op jit(solution)/shard_map/dot_general | solution.py:268
  616.1 23.0 %add_convert_fusion = bf16[1024,4096]{1,0:T(8,128)(2,1)} fusion(f32[1024,4096]{1,0:T(8,128)} %get-tuple-element.438, f32[1024,4096]{1,0:T(8,128)} %get-tuple-element.480, bf16[4096,1024]{1,0:T(8,128)(2,1)} %all-gather.15.cloned.1.call-done, bf16[1,1024,1024]{1,2,0:T(8,128)(2,1)S(1)} %copy-done.22, f32[1024]{0:T(1024)S(1)} %copy-done.63), kind=kOutput, calls=%fused_computation.2 | convolution fusion | flops 8651800576 | bytes 52432896 | tf_op jit(solution)/shard_map/rd,fd->rf/dot_general | solution.py:286
  639.2 15.8 fusion.137
  681.1 6.8 multiply_convert_fusion.6
  721.9 6.9 copy.223
  736.7 6.5 copy.224
  749.0 6.5 copy.225
  794.8 38.2 %copy.229 = bf16[2,8,512,768]{3,1,2,0:T(8,128)(2,1)S(1)} copy(bf16[2,8,512,768]{3,2,1,0:T(8,128)(2,1)S(1)} %bitcast.386) | data formatting | bytes 25165824
  833.0 9.2 pad_convert_fusion.4
  844.6 38.4 %copy.228 = bf16[2,8,512,768]{3,1,2,0:T(8,128)(2,1)S(1)} copy(bf16[2,8,512,768]{3,2,1,0:T(8,128)(2,1)S(1)} %bitcast.387) | data formatting | bytes 25165824
  883.0 9.2 pad_convert_fusion.5
  894.7 38.2 %copy.230 = bf16[2,8,512,768]{3,1,2,0:T(8,128)(2,1)S(1)} copy(bf16[2,8,512,768]{3,2,1,0:T(8,128)(2,1)S(1)} %bitcast.388) | data formatting | bytes 25165824
  932.9 9.2 pad_convert_fusion.3
  944.3 9.2 copy.231
  981.4 13.2 fusion.38
  994.7 15.8 pad_convert_fusion.2
  1010.4 6.7 copy.226
  1017.1 6.4 copy.227
  1028.3 9.1 copy.232
  1039.9 9.2 copy.233
  1049.2 12.6 fusion.51
  1061.8 16.8 %fusion.120 = f32[1024,4096]{1,0:T(8,128)} fusion(bf16[1024,4096]{1,0:T(8,128)(2,1)} %add_convert_fusion, f32[1024,1024]{0,1:T(8,128)} %copy-done.18, f32[1024]{0:T(1024)S(1)} %bitcast.425, f32[1024]{0:T(1024)S(1)} %bitcast.414, f32[1024]{0:T(1024)S(1)} %copy-done.59, f32[1024]{0:T(1024)S(1)} %copy-done.53), kind=kOutput, calls=%fused_computation.240 | convolution fusion | flops 8595177472 | bytes 29376512 | tf_op jit(solution)/shard_map/rd,rf->df/dot_general | solution.py:289
  1078.7 14.1 pad_convert_fusion.1
  1092.9 15.4 pad_convert_fusion
  1108.3 51.2 %reshape.1397 = f32[16,512,769]{2,1,0:T(8,128)} reshape(f32[16,393728]{1,0:T(8,128)} %pad_convert_fusion.4) | data formatting | bytes 50397184 | tf_op jit(solution)/shard_map/while/body/eval_jaxpr/convert_element_type | solution.py:71
  1159.5 11.0 reduce_sum.297
  1171.1 51.1 %reshape.1396 = f32[16,512,769]{2,1,0:T(8,128)} reshape(f32[16,393728]{1,0:T(8,128)} %pad_convert_fusion.5) | data formatting | bytes 50397184 | tf_op jit(solution)/shard_map/while/body/eval_jaxpr/convert_element_type | solution.py:71
  1222.2 15.3 reduce_sum.296
  1238.8 49.0 %reshape.1398 = f32[16,512,769]{2,1,0:T(8,128)} reshape(f32[16,393728]{1,0:T(8,128)} %pad_convert_fusion.3) | data formatting | bytes 50397184 | tf_op jit(solution)/shard_map/while/body/eval_jaxpr/convert_element_type | solution.py:71
  1287.8 10.8 reduce_sum.298
  1299.1 49.4 %reshape.1399 = f32[16,512,769]{2,1,0:T(8,128)} reshape(f32[16,393728]{1,0:T(8,128)} %pad_convert_fusion.2) | data formatting | bytes 50397184 | tf_op jit(solution)/shard_map/while/body/eval_jaxpr/convert_element_type | solution.py:71
  1348.5 10.7 reduce_sum.299
  1359.7 48.4 %reshape.1400 = f32[16,512,769]{2,1,0:T(8,128)} reshape(f32[16,393728]{1,0:T(8,128)} %pad_convert_fusion.1) | data formatting | bytes 50397184 | tf_op jit(solution)/shard_map/while/body/eval_jaxpr/convert_element_type | solution.py:71
  1408.1 10.7 reduce_sum.300
  1419.3 48.8 %reshape.1401 = f32[16,512,769]{2,1,0:T(8,128)} reshape(f32[16,393728]{1,0:T(8,128)} %pad_convert_fusion) | data formatting | bytes 50397184 | tf_op jit(solution)/shard_map/while/body/eval_jaxpr/convert_element_type | solution.py:71
  1468.1 10.7 reduce_sum.301
  1486.8 12.1 fusion.136
  1520.1 24.4 %all-reduce.23 = (bf16[1024]{0:T(1024)(128)(2,1)S(1)}, bf16[1024]{0:T(1024)(128)(2,1)S(1)}, bf16[512]{0:T(512)(128)(2,1)S(1)}, bf16[1024]{0:T(1024)(128)(2,1)S(1)}, bf16[1024]{0:T(1024)(128)(2,1)S(1)}) all-reduce(f32[1024]{0:T(1024)S(1)} %get-tuple-element.415, ...), channel_id=2, replica_groups=mesh['rep'=4,'fsdp'=8] {'fsdp'}, use_global_device_ids=true, to_apply=%region_21.22.clone | all-reduce | flops 4608 | bytes 27648
  1544.9 13.9 all-reduce.24
  1561.4 6.5 add_bitcast_fusion
  1573.3 14.5 fusion.36
  1590.3 52.8 %all-reduce.28.cloned.1.call-done = (bf16[128,3072]{1,0:T(8,128)(2,1)}, bf16[128,1024]{1,0:T(8,128)(2,1)}, bf16[128,4096]{1,0:T(8,128)(2,1)}, bf16[512,1024]{1,0:T(8,128)(2,1)}) async-done(((bf16[128,3072]{1,0:T(8,128)(2,1)}, bf16[128,1024]{1,0:T(8,128)(2,1)}, bf16[128,4096]{1,0:T(8,128)(2,1)}, bf16[512,1024]{1,0:T(8,128)(2,1)}), (bf16[128,3072]{1,0:T(8,128)(2,1)}, bf16[128,1024]{1,0:T(8,128)(2,1)}, ...) | async-done | bytes 3145744 | tf_op jit(solution)/shard_map/psum | solution.py:364
  (441 shorter events, 348.5 us)
Async XLA Ops:
  7.2 28.8 %copy-start.81 = (bf16[128]{0:T(256)(128)(2,1)S(1)}, bf16[128]{0:T(256)(128)(2,1)}, u32[]{:S(2)}) copy-start(bf16[128]{0:T(256)(128)(2,1)} %param.52) | copy-start | bytes 772
  7.2 36.6 %copy-start.82 = (bf16[128]{0:T(256)(128)(2,1)S(1)}, bf16[128]{0:T(256)(128)(2,1)}, u32[]{:S(2)}) copy-start(bf16[128]{0:T(256)(128)(2,1)} %param.53) | copy-start | bytes 772
  7.2 463.6 %all-gather.9.cloned.1.call-start = ((), (), s32[]{:S(2)}) async-start(), calls=%async_computation.4 | async-start | bytes 7077888 | tf_op jit(solution)/shard_map/all_gather | solution.py:230
  7.9 551.0 %all-gather.11.cloned.1.call-start = ((), (), s32[]{:S(2)}) async-start(), calls=%async_computation.5 | async-start | bytes 2359296 | tf_op jit(solution)/shard_map/all_gather | solution.py:232
  8.7 558.9 %all-gather.13.cloned.1.call-start = ((), (), s32[]{:S(2)}) async-start(), calls=%async_computation.6 | async-start | bytes 9437184 | tf_op jit(solution)/shard_map/all_gather | solution.py:237
  9.4 606.7 %all-gather.15.cloned.1.call-start = ((), (), s32[]{:S(2)}) async-start(), calls=%async_computation.7 | async-start | bytes 9437184 | tf_op jit(solution)/shard_map/all_gather | solution.py:238
  10.0 1500.0 %reduce-scatter.7.cloned.1.call-start = ((), (), s32[]{:S(2)}) async-start(), calls=%async_computation.9 | async-start | bytes 4718592 | tf_op jit(solution)/shard_map/reduce_scatter | solution.py:355
  35.0 523.9 %copy-start.6 = (bf16[1,1024,1024]{1,2,0:T(8,128)(2,1)}, bf16[1,1024,1024]{1,2,0:T(8,128)(2,1)S(1)}, u32[]{:S(2)}) copy-start(bf16[1,1024,1024]{1,2,0:T(8,128)(2,1)S(1)} %copy.123) | copy-start | bytes 6291460
  35.3 435.4 %copy-start.48 = (f32[1024]{0:T(1024)}, f32[1024]{0:T(1024)S(1)}, u32[]{:S(2)}) copy-start(f32[1024]{0:T(1024)S(1)} %broadcast_multiply_fusion.1) | copy-start | bytes 12292
  36.0 17.7 %copy-start.71 = (f32[1024]{0:T(1024)}, f32[1024]{0:T(1024)S(1)}, u32[]{:S(2)}) copy-start(f32[1024]{0:T(1024)S(1)} %fusion.27) | copy-start | bytes 12292
  36.0 434.8 %copy-start.68 = (f32[1024]{0:T(1024)}, f32[1024]{0:T(1024)S(1)}, u32[]{:S(2)}) copy-start(f32[1024]{0:T(1024)S(1)} %fusion.116) | copy-start | bytes 12292
  43.8 427.0 %copy-start.60 = (f32[8,1,128]{2,1,0:T(1,128)}, f32[8,1,128]{2,1,0:T(1,128)S(1)}, u32[]{:S(2)}) copy-start(f32[8,1,128]{2,1,0:T(1,128)S(1)} %convert_element_type.392) | copy-start | bytes 12292
  52.5 418.3 %copy-start.78 = (f32[8,1,128]{2,1,0:T(1,128)}, f32[8,1,128]{2,1,0:T(1,128)S(1)}, u32[]{:S(2)}) copy-start(f32[8,1,128]{2,1,0:T(1,128)S(1)} %convert_element_type.393) | copy-start | bytes 12292
  441.1 14.1 copy-start.84
  455.2 109.8 %copy-start.54 = (f32[8,1,128]{2,1,0:T(1,128)}, f32[8,1,128]{2,1,0:T(1,128)S(1)}, u32[]{:S(2)}) copy-start(f32[8,1,128]{2,1,0:T(1,128)S(1)} %convert_element_type.394) | copy-start | bytes 12292
  464.1 101.0 %copy-start.75 = (f32[8,1,128]{2,1,0:T(1,128)}, f32[8,1,128]{2,1,0:T(1,128)S(1)}, u32[]{:S(2)}) copy-start(f32[8,1,128]{2,1,0:T(1,128)S(1)} %convert_element_type.395) | copy-start | bytes 12292
  496.4 34.1 %copy-start.2 = (f32[16,512,256]{1,2,0:T(8,128)}, f32[16,512,256]{1,2,0:T(8,128)S(1)}, u32[]{:S(2)}) copy-start(f32[16,512,256]{1,2,0:T(8,128)S(1)} %get-tuple-element.465) | copy-start | bytes 25165828
  499.6 28.1 %copy-start.3 = (f32[16,512,256]{1,2,0:T(8,128)}, f32[16,512,256]{1,2,0:T(8,128)S(1)}, u32[]{:S(2)}) copy-start(f32[16,512,256]{1,2,0:T(8,128)S(1)} %get-tuple-element.469) | copy-start | bytes 25165828
  511.0 42.2 %copy-start.1 = (f32[16,512,256]{1,2,0:T(8,128)}, f32[16,512,256]{1,2,0:T(8,128)S(1)}, u32[]{:S(2)}) copy-start(f32[16,512,256]{1,2,0:T(8,128)S(1)} %get-tuple-element.463) | copy-start | bytes 25165828
  521.3 32.0 %copy-start.39 = (f32[16,512]{1,0:T(8,128)}, f32[16,512]{1,0:T(8,128)S(1)}, u32[]{:S(2)}) copy-start(f32[16,512]{1,0:T(8,128)S(1)} %log_add_fusion) | copy-start | bytes 98308
  537.3 9.5 copy-start.4
  567.6 48.5 %copy-start.22 = (bf16[1,1024,1024]{1,2,0:T(8,128)(2,1)S(1)}, bf16[1,1024,1024]{1,2,0:T(8,128)(2,1)}, u32[]{:S(2)}) copy-start(bf16[1,1024,1024]{1,2,0:T(8,128)(2,1)} %copy.136) | copy-start | bytes 6291460
  567.6 48.5 %copy-start.63 = (f32[1024]{0:T(1024)S(1)}, f32[1024]{0:T(1024)}, u32[]{:S(2)}) copy-start(f32[1024]{0:T(1024)} %fusion.115) | copy-start | bytes 12292
  667.4 8.7 copy-start.66
  680.2 7.7 slice-start
  681.1 6.8 slice-start.1
  681.1 11.7 slice-start.6
  688.0 9.7 slice-start.14
  692.8 9.6 slice-start.10
  697.7 16.3 slice-start.18
  702.4 11.6 slice-start.19
  721.9 789.9 %reduce-scatter.5.cloned.1.call-start = ((), (), s32[]{:S(2)}) async-start(), calls=%async_computation.8 | async-start | bytes 14155776 | tf_op jit(solution)/shard_map/reduce_scatter | solution.py:353
  761.0 11.9 slice-start.2
  765.1 7.8 slice-start.3
  765.1 14.6 slice-start.16
  772.9 6.8 slice-start.17
  775.5 8.1 slice-start.8
  833.0 9.2 copy-start.26
  883.0 9.2 copy-start.28
  932.9 9.2 copy-start.27
  942.0 11.5 slice-start.22
  944.3 9.2 slice-start.23
  944.3 9.2 copy-start.11
  944.3 10.1 copy-start.16
  994.6 519.6 %reduce-scatter.9.cloned.1.call-start = ((), (), s32[]{:S(2)}) async-start(), calls=%async_computation.10 | async-start | bytes 18874368 | tf_op jit(solution)/shard_map/reduce_scatter | solution.py:358
  1028.3 9.1 copy-start.30
  1037.4 11.7 slice-start.24
  1039.9 9.2 copy-start.23
  1039.9 9.2 copy-start.64
  1039.9 9.2 slice-start.25
  1049.1 12.7 copy-start.53
  1049.2 12.6 copy-start.56
  1049.2 12.6 copy-start.59
  1049.2 12.6 copy-start.76
  1078.7 438.3 %reduce-scatter.11.cloned.1.call-start = ((), (), s32[]{:S(2)}) async-start(), calls=%async_computation.11 | async-start | bytes 18874368 | tf_op jit(solution)/shard_map/reduce_scatter | solution.py:359
  1092.8 550.3 %all-reduce.28.cloned.1.call-start = ((), (), s32[]{:S(2)}) async-start(), calls=%async_computation.12 | async-start | bytes 6291456 | tf_op jit(solution)/shard_map/psum | solution.py:364
  1498.9 8.6 copy-start.72
  1498.9 8.6 copy-start.70
  1510.0 9.7 copy-start.86
  1510.0 10.2 copy-start.77
  1510.0 10.2 copy-start.80
  1510.0 51.4 %copy-start.65 = (f32[1024]{0:T(1024)S(1)}, f32[1024]{0:T(1024)}, u32[]{:S(2)}) copy-start(f32[1024]{0:T(1024)} %fusion.115) | copy-start | bytes 12292
  1510.0 51.4 %copy-start.67 = (f32[1024]{0:T(1024)S(1)}, f32[1024]{0:T(1024)}, u32[]{:S(2)}) copy-start(f32[1024]{0:T(1024)} %copy-done.66) | copy-start | bytes 12292
  1643.1 6.9 copy-start.47
  (58 other events, 264.8 us)
Sparse Core Ops, SparseCore 0:
  9.9 48.2 all-gather.8
  60.1 27.8 all-gather.10
  89.9 54.3 all-gather.12
  146.1 54.3 all-gather.14
  722.0 51.6 reduce-scatter.6
  994.7 92.4 reduce-scatter.4
  1091.2 115.9 reduce-scatter.8
  1211.2 115.9 reduce-scatter.10
  1519.8 123.2 all-reduce.27
where the time goes:
time: 1670 us; the launch traced here: 1660 us
  local copies, waits for them, and re-layouts  963 us (58%)
  matrix products  320 us (19%)
  other arithmetic  214 us (13%)
  blocking collectives  86.6 us (5%)
  waiting for transfers between devices  55.5 us (3%)
  between operations  18.2 us (1%)
    convert_element_type x6, local copies, waits for them, and re-layouts, diagonal_sums(): sums = jnp.sum(skewed.astype(jnp.float32), axis=1)  298 us
    unnamed x270, local copies, waits for them, and re-layouts  250 us
    reshape x4, local copies, waits for them, and re-layouts, bias_tile(): flat[:, :row_count * (span_len - 1)]  169 us
    reshape x4, local copies, waits for them, and re-layouts, bias_tile(): jnp.broadcast_to(turned[:, None, :], (head_count, row_count, span_len))  116 us
    convert_element_type x6, other arithmetic, diagonal_sums(): sums = jnp.sum(skewed.astype(jnp.float32), axis=1)  72.8 us
    reduce_sum x6, other arithmetic, diagonal_sums(): sums = jnp.sum(skewed.astype(jnp.float32), axis=1)  69.1 us
    psum x1, waiting for transfers between devices, per_device(): lax.psum(shards[2].astype(jnp.bfloat16), 'rep').astype(jnp.float32)  52.8 us
    dot_general x1, matrix products, per_device(): jnp.dot(normed_two, in_full, preferred_element_type=jnp.float32)  48.5 us
  transfers between devices with their start and end apart: 9, of which 1 were waited for; matrix products, arithmetic and copies ran while one was open for 83% of the time, Pallas kernels for 0%

commit v1 on v0

v1 whole, which is shorter than its diff:
```python
import jax
import jax.numpy as jnp
from jax import lax
from jax.experimental import pallas as pl
from jax.experimental.pallas import tpu as pltpu
from jax.sharding import PartitionSpec as P

HEADS = 16
HEAD_DIM = 64
BUCKETS = 32
T = 256
NEG = -1e30
F32 = jnp.float32
BF = jnp.bfloat16

def layer_norm(values, gain_row, shift_row):
    average = jnp.mean(values, axis=-1, keepdims=True)
    centred = values - average
    spread = jnp.mean(centred * centred, axis=-1, keepdims=True)
    return centred * lax.rsqrt(spread + 1e-05) * gain_row + shift_row


def gelu_exact(values):
    return jax.nn.gelu(values, approximate=False)


def bucket_onehot(bucket_table, bucket_count):
    return (bucket_table[:, None] == lax.iota(jnp.int32, bucket_count)[None, :]).astype(
        jnp.bfloat16
    )


def toeplitz(base_ref):
    row=lax.broadcasted_iota(jnp.int32,(T,T),0); col=lax.broadcasted_iota(jnp.int32,(T,T),1)
    upper = col>=row
    rolled=[]
    for U in range(4):
        a=jnp.broadcast_to(base_ref[0,U:U+1,:],(T,T))
        rolled.append(pltpu.roll(a,0,1,stride=1,stride_axis=0))
    out=[]
    for U in range(4):
        nxt = rolled[U+1] if U<3 else NEG
        out.append(jnp.where(upper,rolled[U],nxt))
    return out

def fwd_kernel(len_ref, base_ref, qT_ref, kT_ref, vT_ref, oT_ref, lt_ref, g_ref):
    for U,t in enumerate(toeplitz(base_ref)): g_ref[U*T:(U+1)*T,:]=t
    k = kT_ref[0].T
    vT= vT_ref[0]
    kid = 768+lax.broadcasted_iota(jnp.int32,(T,1),0)
    kmask = jnp.where(kid<len_ref[0],0.0,NEG).astype(F32)
    for bi in range(4):
        nk=(bi+1)*T
        qT=qT_ref[0,:,bi*T:(bi+1)*T]*BF(0.125)
        s=jnp.dot(k[:nk],qT,preferred_element_type=F32)+g_ref[(3-bi)*T:,:]
        if bi==3:
            s=jnp.concatenate([s[:768],s[768:]+kmask],axis=0)
        m=jnp.max(s,axis=0,keepdims=True)
        p=jnp.exp(s-m)
        l=jnp.sum(p,axis=0,keepdims=True)
        o=jnp.dot(vT[:,:nk],p.astype(BF),preferred_element_type=F32)
        oT_ref[0,:,bi*T:(bi+1)*T]=(o*(1.0/l)).astype(BF)
        lt_ref[0,:,bi*T:(bi+1)*T]=m+jnp.log(l)

def attn_fwd(length, base, qkvT, vmem=48<<20):
    hs=lambda off: pl.BlockSpec((1,64,1024),lambda h:(h+off,0,0))
    return pl.pallas_call(fwd_kernel, grid=(16,),
        in_specs=[pl.BlockSpec(memory_space=pltpu.SMEM), pl.BlockSpec((1,4,T),lambda h:(h,0,0)), hs(0),hs(16),hs(32)],
        out_specs=[pl.BlockSpec((1,64,1024),lambda h:(h,0,0)), pl.BlockSpec((1,1,1024),lambda h:(h,0,0))],
        out_shape=[jax.ShapeDtypeStruct((16,64,1024),BF),jax.ShapeDtypeStruct((16,1,1024),F32)],
        scratch_shapes=[pltpu.VMEM((1024,T),F32)],
        compiler_params=pltpu.CompilerParams(vmem_limit_bytes=vmem),
    )(length, base, qkvT,qkvT,qkvT)

def bwd_kernel(len_ref, base_ref, qT_ref, kT_ref, vT_ref, oT_ref, doT_ref, lt_ref, dq_ref, dk_ref, dv_ref, dist_ref, g_ref, dg_ref, dkv, dvv):
    for U,t in enumerate(toeplitz(base_ref)): g_ref[U*T:(U+1)*T,:]=t
    kT=kT_ref[0]
    k=kT.T; v=vT_ref[0].T
    kid = 768+lax.broadcasted_iota(jnp.int32,(T,1),0)
    kmask = jnp.where(kid<len_ref[0],0.0,NEG).astype(F32)
    for bi in (3,2,1,0):
        nk=(bi+1)*T
        sl=slice(bi*T,(bi+1)*T)
        qT=qT_ref[0,:,sl]*BF(0.125)
        doT=doT_ref[0,:,sl]
        inner=jnp.sum(doT.astype(F32)*oT_ref[0,:,sl].astype(F32),axis=0,keepdims=True)
        lt=lt_ref[0,:,sl]
        s=jnp.dot(k[:nk],qT,preferred_element_type=F32)+g_ref[(3-bi)*T:,:]
        if bi==3:
            s=jnp.concatenate([s[:768],s[768:]+kmask],axis=0)
        p=jnp.exp(s-lt)
        dp=jnp.dot(v[:nk],doT,preferred_element_type=F32)
        ds=p*(dp-inner)
        pb=p.astype(BF); dsb=ds.astype(BF)
        dq_ref[0,:,sl]=(jnp.dot(kT[:,:nk],dsb,preferred_element_type=F32)*0.125).astype(BF)
        dvp=lax.dot_general(doT,pb,(((1,),(1,)),((),())),preferred_element_type=F32)
        dkp=lax.dot_general(qT,dsb,(((1,),(1,)),((),())),preferred_element_type=F32)
        if bi==3:
            dkv[...]=dkp; dvv[...]=dvp; dg_ref[...]=ds
        else:
            dkv[:,:nk]+=dkp; dvv[:,:nk]+=dvp; dg_ref[(3-bi)*T:,:]+=ds
    dk_ref[0]=dkv[...].astype(BF); dv_ref[0]=dvv[...].astype(BF)
    skew_sums(dg_ref, dist_ref)

def skew_sums(dg_ref, dist_ref):
    row=lax.broadcasted_iota(jnp.int32,(T,T),0); col=lax.broadcasted_iota(jnp.int32,(T,T),1)
    upper = col>=row
    for V in range(4):
        cur=dg_ref[V*T:(V+1)*T,:]
        prev=dg_ref[(V-1)*T:V*T,:] if V else 0.0
        z=jnp.where(upper,cur,prev)
        acc=z[0:8]
        for g in range(1,T//8):
            acc=acc+pltpu.roll(z[8*g:8*g+8],T-8*g,1)
        tot=acc[0:1]
        for r in range(1,8):
            tot=tot+pltpu.roll(acc[r:r+1],T-r,1)
        dist_ref[0,V:V+1,:]=tot

def attn_bwd(length, base, qkvT, oT, doT, lt, vmem=48<<20):
    hs=lambda off: pl.BlockSpec((1,64,1024),lambda h:(h+off,0,0))
    return pl.pallas_call(bwd_kernel, grid=(16,),
        in_specs=[pl.BlockSpec(memory_space=pltpu.SMEM), pl.BlockSpec((1,4,T),lambda h:(h,0,0)), hs(0),hs(16),hs(32),hs(0),hs(0),pl.BlockSpec((1,1,1024),lambda h:(h,0,0))],
        out_specs=[hs(0),hs(0),hs(0), pl.BlockSpec((1,4,T),lambda h:(h,0,0))],
        out_shape=[jax.ShapeDtypeStruct((16,64,1024),BF)]*3+[jax.ShapeDtypeStruct((16,4,T),F32)],
        scratch_shapes=[pltpu.VMEM((1024,T),F32),pltpu.VMEM((1024,T),F32),pltpu.VMEM((64,1024),F32),pltpu.VMEM((64,1024),F32)],
        compiler_params=pltpu.CompilerParams(vmem_limit_bytes=vmem),
    )(length, base, qkvT,qkvT,qkvT,oT,doT,lt)


def per_device(inputs, lengths, bucket_table, ln1_gain, ln1_shift, w_qkv, rel_bias, w_out, ln2_gain, ln2_shift, w_in, w_down, cotangent):
    gather = lambda w: lax.all_gather(w, "fsdp", axis=0, tiled=True)
    small = gather(jnp.concatenate([ln1_gain, ln1_shift, ln2_gain, ln2_shift, rel_bias])[None])
    qkv_full = gather(w_qkv)
    out_full = gather(w_out)
    in_full = gather(w_in)
    down_full = gather(w_down)
    width = inputs.shape[-1]
    n = ln1_gain.shape[0]
    gain_one, shift_one, gain_two, shift_two = (small[:, i * n:(i + 1) * n].reshape(-1).astype(F32) for i in range(4))
    table_heads = small[:, 4 * n:].reshape(HEADS, BUCKETS)
    slots = inputs.shape[1]
    onehot = bucket_onehot(bucket_table, BUCKETS)
    by_distance = jnp.einsum("hb,sb->hs", table_heads, onehot, preferred_element_type=F32)
    base = by_distance.reshape(HEADS, slots // T, T)[:, ::-1]
    residual = inputs.reshape(slots, width).astype(F32)
    normed_one = layer_norm(residual, gain_one, shift_one).astype(BF)
    projT = jnp.einsum("rd,dc->cr", normed_one, qkv_full, preferred_element_type=F32).astype(BF)
    qkvT = projT.reshape(3 * HEADS, HEAD_DIM, slots)
    oT, log_total = attn_fwd(lengths, base, qkvT)
    attT = oT.reshape(width, slots)
    middle = residual + jnp.einsum("kr,kd->rd", attT, out_full, preferred_element_type=F32)
    normed_two = layer_norm(middle, gain_two, shift_two).astype(BF)
    hidden_pre = jnp.dot(normed_two, in_full, preferred_element_type=F32)
    hidden = gelu_exact(hidden_pre).astype(BF)
    ffn_out = jnp.dot(hidden, down_full, preferred_element_type=F32)
    valid = (lax.iota(jnp.int32, slots) < lengths[0]).astype(F32)[:, None]
    outputs = ((middle + ffn_out) * valid).astype(BF).reshape(inputs.shape)
    out_grad = cotangent.reshape(slots, width).astype(F32) * valid
    out_low = out_grad.astype(BF)
    down_grad = jnp.einsum("rf,rd->fd", hidden, out_low, preferred_element_type=F32)
    hidden_grad = jnp.einsum("rd,fd->rf", out_low, down_full, preferred_element_type=F32)
    pre_grad = jax.vjp(gelu_exact, hidden_pre)[1](hidden_grad)[0].astype(BF)
    in_grad = jnp.einsum("rd,rf->df", normed_two, pre_grad, preferred_element_type=F32)
    normed_two_grad = jnp.einsum("rf,df->rd", pre_grad, in_full, preferred_element_type=F32)
    middle_part, gain_two_grad, shift_two_grad = jax.vjp(layer_norm, middle, gain_two, shift_two)[1](normed_two_grad)
    middle_grad = out_grad + middle_part
    branch_grad = middle_grad.astype(BF)
    out_w_grad = jnp.einsum("kr,rd->kd", attT, branch_grad, preferred_element_type=F32)
    doT = jnp.einsum("kd,rd->kr", out_full, branch_grad, preferred_element_type=F32).astype(BF)
    dq, dk, dv, dist = attn_bwd(lengths, base, qkvT, oT, doT.reshape(HEADS, HEAD_DIM, slots), log_total)
    distance_total = dist[:, ::-1].reshape(HEADS, slots)
    table_grad = jnp.dot(distance_total, onehot.astype(F32), precision=lax.Precision.HIGHEST, preferred_element_type=F32)
    pgT = jnp.concatenate([dq, dk, dv], axis=0).reshape(3 * width, slots)
    qkv_grad = jnp.einsum("rd,er->de", normed_one, pgT, preferred_element_type=F32)
    normed_one_grad = jnp.einsum("er,de->rd", pgT, qkv_full, preferred_element_type=F32)
    input_part, gain_one_grad, shift_one_grad = jax.vjp(layer_norm, residual, gain_one, shift_one)[1](normed_one_grad)
    input_grad = (middle_grad + input_part).reshape(inputs.shape)
    def reduced(g):
        part = lax.psum_scatter(g.astype(BF), "fsdp", scatter_dimension=0, tiled=True)
        return lax.psum(part, "rep").astype(F32)
    groups = small.shape[0]
    packed = jnp.concatenate([v.reshape(groups, -1) for v in (gain_one_grad, shift_one_grad, gain_two_grad, shift_two_grad, table_grad)], axis=1)
    tiny = lax.psum(lax.psum_scatter(packed, "fsdp", scatter_dimension=0, tiled=True), "rep")[0]
    return (outputs, input_grad, tiny[:n], tiny[n:2 * n], reduced(qkv_grad), tiny[4 * n:], reduced(out_w_grad), tiny[2 * n:3 * n], tiny[3 * n:4 * n], reduced(in_grad), reduced(down_grad))


def solution(mesh):
    placed = (
        P(("rep", "fsdp"), None, None),
        P(("rep", "fsdp")),
        P(),
        P("fsdp"),
        P("fsdp"),
        P("fsdp", None),
        P("fsdp"),
        P("fsdp", None),
        P("fsdp"),
        P("fsdp"),
        P("fsdp", None),
        P("fsdp", None),
        P(("rep", "fsdp"), None, None),
    )
    return jax.shard_map(
        per_device,
        mesh=mesh,
        in_specs=placed,
        out_specs=(
            P(("rep", "fsdp"), None, None),
            P(("rep", "fsdp"), None, None),
            P("fsdp"),
            P("fsdp"),
            P("fsdp", None),
            P("fsdp"),
            P("fsdp", None),
            P("fsdp"),
            P("fsdp"),
            P("fsdp", None),
            P("fsdp", None),
        ),
        check_vma=False,
    )
```

time: 1670 us -> 680 us (0.41)
  local copies, waits for them, and re-layouts: 963 us -> 53.4 us
  waiting for transfers between devices: 55.5 us -> 250 us
  other arithmetic: 214 us -> 35.3 us
  matrix products: 320 us -> 181 us
  Pallas kernels: 0 us -> 70.5 us
  blocking collectives: 86.6 us -> 63.4 us
    convert_element_type x7 -> x1, local copies, waits for them, and re-layouts: 307 us -> 8.65 us  [per_device(): jnp.einsum('rd,dc->cr', normed_one, qkv_full, preferred_element_type=F32)]
    reshape x10 -> x2, local copies, waits for them, and re-layouts: 284 us -> 0.15 us  [the longest x1 0.08 us: per_device(): table_heads = small[:, 4 * n:].reshape(HEADS, BUCKETS)]
    unnamed x270 -> x91, local copies, waits for them, and re-layouts: 250 us -> 30.5 us
    reduce_scatter x4, waiting for transfers between devices: 0.03 us -> 144 us  [reduced(): lax.psum_scatter(g.astype(BF), 'fsdp', scatter_dimension=0, tiled=True)]
    dot_general x50 -> x14, matrix products: 320 us -> 181 us  [the longest x1 48.1 us: per_device(): hidden_pre = jnp.dot(normed_two, in_full, preferred_element_type=F32)]
    convert_element_type x27 -> x8, other arithmetic: 102 us -> 11.5 us  [the longest x4 8.63 us: reduced(): return lax.psum(part, 'rep').astype(F32)]
    reduce_sum x12 -> x0, other arithmetic: 81.9 us -> none  [the longest x6 69.1 us: diagonal_sums(): sums = jnp.sum(skewed.astype(jnp.float32), axis=1)]
    pallas_call x0 -> x2, Pallas kernels: none -> 70.5 us  [the longest x1 37.2 us: attn_bwd(): pl.pallas_call(bwd_kernel, grid=(16,), in_specs=[pl.BlockSpec(memory_spac...]
  transfers between devices with their start and end apart: 9 -> 9, of which waited for: 1 -> 6; matrix products, arithmetic and copies ran while one was open for 83% -> 29% of each run, Pallas kernels for 0% -> 11%
where the time goes in v1:
time: 680 us; the launch traced here: 670 us
  waiting for transfers between devices  250 us (37%)
  matrix products  181 us (27%)
  Pallas kernels  70.5 us (10%)
  blocking collectives  63.4 us (9%)
  local copies, waits for them, and re-layouts  53.4 us (8%)
  other arithmetic  35.3 us (5%)
  between operations  16.1 us (2%)
    reduce_scatter x4, waiting for transfers between devices, reduced(): lax.psum_scatter(g.astype(BF), 'fsdp', scatter_dimension=0, tiled=True)  144 us
    psum x1, waiting for transfers between devices, reduced(): return lax.psum(part, 'rep').astype(F32)  66.8 us
    unnamed x2, blocking collectives  50.8 us
    dot_general x1, matrix products, per_device(): hidden_pre = jnp.dot(normed_two, in_full, preferred_element_type=F32)  48.1 us
    pallas_call x1, Pallas kernels, attn_bwd(): pl.pallas_call(bwd_kernel, grid=(16,), in_specs=[pl.BlockSpec(memory_spac...  37.2 us
    all_gather x4, waiting for transfers between devices, per_device(): gather = lambda w: lax.all_gather(w, 'fsdp', axis=0, tiled=True)  36.8 us
    pallas_call x1, Pallas kernels, attn_fwd(): pl.pallas_call(fwd_kernel, grid=(16,), in_specs=[pl.BlockSpec(memory_spac...  33.3 us
    unnamed x91, local copies, waits for them, and re-layouts  30.5 us
  transfers between devices with their start and end apart: 9, of which 6 were waited for; matrix products, arithmetic and copies ran while one was open for 29% of the time, Pallas kernels for 11%

profile of v1, /device:TPU:0, one launch (start us, length us, event | category | flops | bytes accessed | tf_op | source)
XLA Modules:
  0.0 669.5 jit_solution(16762407245026960490)
XLA Ops:
  7.2 0.7 all-gather.6.cloned.1.call-update
  8.0 0.7 all-gather.8.cloned.1.call-update
  8.7 0.7 all-gather.10.cloned.1.call-update
  9.4 0.5 all-gather.12.cloned.1.call-update
  10.7 0.7 eq.37
  11.4 1.3 fusion.60
  13.4 0.8 dynamic-update-slice.6
  14.2 0.8 dynamic-update-slice.7
  15.0 0.8 dynamic-update-slice.8
  15.9 0.8 dynamic-update-slice.9
  16.7 0.8 dynamic-update-slice.10
  17.7 26.0 %all-reduce = bf16[4608]{0:T(1024)(128)(2,1)S(1)} all-reduce(bf16[4608]{0:T(1024)(128)(2,1)S(1)} %dynamic-update-slice), channel_id=2, replica_groups=mesh['rep'=4,'fsdp'=8] {'fsdp'}, use_global_device_ids=true, to_apply=%add | all-reduce | flops 4608 | bytes 18432
  44.3 3.0 copy.35
  47.7 0.6 fusion.17
  48.3 4.0 copy.39
  52.3 6.1 all-gather.6.cloned.1.call-done
  58.4 12.0 %convert_bitcast_fusion = bf16[3072,1024]{0,1:T(8,128)(2,1)} fusion(bf16[1024,3072]{1,0:T(8,128)(2,1)} %all-gather.6.cloned.1.call-done, bf16[1,1024,1024]{1,2,0:T(8,128)(2,1)S(1)} %copy.35, f32[1024]{0:T(1024)S(1)} %get-tuple-element.59, f32[1024]{0:T(1024)S(1)} %get-tuple-element.60, f32[1024]{0:T(1024)S(1)} %fusion.51, f32[1024]{0:T(1024)S(1)} %broadcast_multiply_fusion.1), kind=kOutput, calls=%fused_computation.22 | convolution fusion | flops 6451888128 | bytes 14696448 | tf_op jit(solution)/shard_map/rd,dc->cr/dot_general | solution.py:148
  70.4 8.7 %copy.37 = bf16[3072,1024]{1,0:T(8,128)(2,1)} copy(bf16[3072,1024]{0,1:T(8,128)(2,1)} %convert_bitcast_fusion) | data formatting | bytes 12582912 | tf_op jit(solution)/shard_map/convert_element_type | solution.py:148
  79.1 33.3 %shard_map.212 = (bf16[16,64,1024]{2,1,0:T(8,128)(2,1)S(1)}, f32[16,1,1024]{2,1,0:T(1,128)S(1)}) custom-call(s32[1]{0:T(128)} %copy.62.len_ref, f32[16,4,256]{2,1,0:T(4,128)S(1)} %rev.6.base_ref, bf16[48,64,1024]{2,1,0:T(8,128)(2,1)} %bitcast.130, bf16[48,64,1024]{2,1,0:T(8,128)(2,1)} %bitcast.131, bf16[48,64,1024]{2,1,0:T(8,128)(2,1)} %bitcast.132), custom_call_target="tpu_custom_call" | custom-call | tf_op jit(solution)/shard_map/pallas_call | solution.py:67
  112.4 5.4 fusion.61
  117.9 0.5 multiply_reduce_fusion.2
  118.4 1.5 copy-done.5
  119.9 2.0 add_convert_fusion.3.clone.4
  121.9 22.6 %all-gather.10.cloned.1.call-done = bf16[1024,4096]{1,0:T(8,128)(2,1)} async-done(((bf16[128,4096]{1,0:T(8,128)(2,1)}), bf16[1024,4096]{1,0:T(8,128)(2,1)}) %all-gather.10.cloned.1.call-update) | async-done | bytes 8388624 | tf_op jit(solution)/shard_map/all_gather | solution.py:132
  144.5 48.1 %multiply_convert_fusion = (bf16[1024,4096]{1,0:T(8,128)(2,1)}, f32[1024,4096]{1,0:T(8,128)}, f32[1024,4096]{1,0:T(8,128)}) fusion(bf16[1024,4096]{1,0:T(8,128)(2,1)} %all-gather.10.cloned.1.call-done, bf16[1024,1024]{0,1:T(8,128)(2,1)} %add_convert_fusion.3.clone.4), kind=kOutput, calls=%fused_computation.3 | convolution fusion | flops 8862564352 | bytes 52428800 | tf_op jit(solution)/shard_map/dot_general | solution.py:154
  192.6 8.1 %all-gather.12.cloned.1.call-done = bf16[4096,1024]{1,0:T(8,128)(2,1)} async-done(((bf16[512,1024]{1,0:T(8,128)(2,1)}), bf16[4096,1024]{1,0:T(8,128)(2,1)}) %all-gather.12.cloned.1.call-update) | async-done | bytes 8388624 | tf_op jit(solution)/shard_map/all_gather | solution.py:132
  200.7 22.8 %add_convert_fusion = bf16[1024,4096]{1,0:T(8,128)(2,1)} fusion(f32[1024,4096]{1,0:T(8,128)} %get-tuple-element.56, f32[1024,4096]{1,0:T(8,128)} %get-tuple-element.69, bf16[4096,1024]{1,0:T(8,128)(2,1)} %all-gather.12.cloned.1.call-done, bf16[1,1024,1024]{1,2,0:T(8,128)(2,1)S(1)} %copy-done.9, f32[1024]{0:T(1024)S(1)} %fusion.50), kind=kOutput, calls=%fused_computation.2 | convolution fusion | flops 8651800576 | bytes 52432896 | tf_op jit(solution)/shard_map/rd,fd->rf/dot_general | solution.py:162
  223.5 16.1 %fusion.63 = (f32[1024]{0:T(1024)}, f32[1024,1024]{1,0:T(8,128)}) fusion(bf16[1024,4096]{1,0:T(8,128)(2,1)} %add_convert_fusion, bf16[1024,4096]{1,0:T(8,128)(2,1)} %all-gather.10.cloned.1.call-done), kind=kOutput, calls=%fused_computation.111 | convolution fusion | flops 8590982144 | bytes 20975616 | tf_op jit(solution)/shard_map/rf,df->rd/dot_general | solution.py:165
  239.6 5.3 copy.40
  245.0 4.8 multiply_reduce_fusion
  249.8 1.0 copy-done.8
  250.9 1.0 fusion.58
  251.9 0.9 fusion.25
  252.9 1.2 copy-done.7
  254.0 1.3 copy-done.12
  255.4 3.7 convolution_convert_fusion.4
  259.1 5.3 convolution_convert_fusion.3
  264.4 37.2 %shard_map.213 = (bf16[16,64,1024]{2,1,0:T(8,128)(2,1)S(1)}, bf16[16,64,1024]{2,1,0:T(8,128)(2,1)S(1)}, bf16[16,64,1024]{2,1,0:T(8,128)(2,1)}, f32[16,4,256]{2,1,0:T(4,128)S(1)}) custom-call(s32[1]{0:T(128)} %copy.62.len_ref, f32[16,4,256]{2,1,0:T(4,128)S(1)} %rev.6.base_ref, bf16[48,64,1024]{2,1,0:T(8,128)(2,1)} %bitcast.133, ...), custom_call_target="tpu_custom_call" | custom-call | tf_op jit(solution)/shard_map/pallas_call | solution.py:122
  301.6 4.0 pad_maximum_fusion
  305.6 2.6 copy-done.11
  308.3 8.8 %convolution_convert_fusion.2 = bf16[1024,3072]{1,0:T(8,128)(2,1)} fusion(bf16[3072,1024]{1,0:T(8,128)(2,1)S(1)} %bitcast.136, bf16[1,1024,1024]{1,2,0:T(8,128)(2,1)S(1)} %copy-done.3, f32[1024]{0:T(1024)S(1)} %copy-done.35, f32[1024]{0:T(1024)S(1)} %copy-done.23, f32[1024]{0:T(1024)S(1)} %copy-done.25, f32[1024]{0:T(1024)S(1)} %copy-done.15), kind=kOutput, calls=%fused_computation.26 | convolution fusion | flops 6451888128 | bytes 14696448 | tf_op jit(solution)/shard_map/rd,er->de/dot_general | solution.py:175
  317.1 15.0 %convolution_convert_fusion = bf16[4096,1024]{1,0:T(8,128)(2,1)} fusion(bf16[1024,4096]{1,0:T(8,128)(2,1)} %get-tuple-element.55, bf16[1,1024,1024]{1,2,0:T(8,128)(2,1)} %copy.39, f32[1024]{0:T(1024)S(1)} %fusion.50), kind=kOutput, calls=%fused_computation.17 | convolution fusion | flops 8597274624 | bytes 18878464 | tf_op jit(solution)/shard_map/rf,rd->fd/dot_general | solution.py:161
  332.2 0.6 copy-done.31
  332.8 15.4 %convolution_convert_fusion.1 = bf16[1024,4096]{1,0:T(8,128)(2,1)} fusion(bf16[1024,4096]{1,0:T(8,128)(2,1)} %add_convert_fusion, f32[1024,1024]{0,1:T(8,128)} %copy-done.5, f32[1024]{0:T(1024)S(1)} %copy-done.31, f32[1024]{0:T(1024)S(1)} %copy-done.21, f32[1024]{0:T(1024)S(1)} %copy-done.19, f32[1024]{0:T(1024)S(1)} %copy-done.17), kind=kOutput, calls=%fused_computation.18 | convolution fusion | flops 8599371776 | bytes 20987904 | tf_op jit(solution)/shard_map/rd,rf->df/dot_general | solution.py:164
  348.7 12.2 %fusion.62 = (f32[1024]{0:T(1024)S(1)}, f32[1024,1024]{1,0:T(8,128)}) fusion(bf16[3072,1024]{1,0:T(8,128)(2,1)} %bitcast.137, bf16[1024,3072]{1,0:T(8,128)(2,1)} %all-gather.6.cloned.1.call-done), kind=kOutput, calls=%fused_computation.110 | convolution fusion | flops 6443498496 | bytes 16781312 | tf_op jit(solution)/shard_map/er,de->rd/dot_general | solution.py:176
  360.9 5.5 copy.41
  366.7 3.1 fusion.18
  369.8 15.4 %fusion.26 = bf16[1,1024,1024]{1,2,0:T(8,128)(2,1)} fusion(f32[1024,1024]{0,1:T(8,128)} %copy-done.5, f32[1024]{0:T(1024)S(1)} %fusion.50, bf16[1024,4096]{1,0:T(8,128)(2,1)} %get-tuple-element.55, bf16[4096,1024]{1,0:T(8,128)(2,1)} %all-gather.12.cloned.1.call-done), kind=kOutput, calls=%fused_computation.54 | convolution fusion | flops 8593080320 | bytes 23072768 | tf_op jit(solution)/shard_map/dot_general | solution.py:156
  385.3 68.4 %reduce-scatter.11.cloned.1.call-done = bf16[512,1024]{1,0:T(8,128)(2,1)} async-done(((bf16[4096,1024]{1,0:T(8,128)(2,1)}), bf16[512,1024]{1,0:T(8,128)(2,1)}) %reduce-scatter.11.cloned.1.call-update) | async-done | bytes 1048592 | tf_op jit(solution)/shard_map/reduce_scatter | solution.py:180
  453.7 75.2 %reduce-scatter.9.cloned.1.call-done = bf16[128,4096]{1,0:T(8,128)(2,1)} async-done(((bf16[1024,4096]{1,0:T(8,128)(2,1)}), bf16[128,4096]{1,0:T(8,128)(2,1)}) %reduce-scatter.9.cloned.1.call-update) | async-done | bytes 1048592 | tf_op jit(solution)/shard_map/reduce_scatter | solution.py:180
  529.0 3.9 copy.44
  533.0 3.9 fusion.16
  537.2 5.5 add_bitcast_fusion
  542.6 5.4 copy.45
  548.0 24.8 %all-reduce.1 = f32[8,576]{1,0:T(8,128)S(1)} all-reduce(f32[8,576]{1,0:T(8,128)S(1)} %constant_dynamic-update-slice_fusion), channel_id=3, replica_groups=mesh['rep'=4,'fsdp'=8] {'fsdp'}, use_global_device_ids=true, to_apply=%region_12.0.clone | all-reduce | flops 4608 | bytes 36864
  572.8 0.7 constant_dynamic-slice_fusion
  573.5 12.6 %psum.35 = f32[1,576]{1,0:T(1,128)S(1)} all-reduce(f32[1,576]{1,0:T(1,128)S(1)} %constant_dynamic-slice_fusion), channel_id=1, replica_groups=mesh['rep'=4,'fsdp'=8] {'rep'}, use_global_device_ids=true, to_apply=%region_13.0 | all-reduce | flops 576 | bytes 4608 | tf_op jit(solution)/shard_map/psum | solution.py:184
  586.1 0.5 slice_bitcast_fusion.6
  586.6 0.5 slice_bitcast_fusion.4
  587.1 66.8 %all-reduce.5.cloned.1.call-done = (bf16[128,3072]{1,0:T(8,128)(2,1)}, bf16[128,1024]{1,0:T(8,128)(2,1)}, bf16[128,4096]{1,0:T(8,128)(2,1)}, bf16[512,1024]{1,0:T(8,128)(2,1)}) async-done(((bf16[128,3072]{1,0:T(8,128)(2,1)}, bf16[128,1024]{1,0:T(8,128)(2,1)}, bf16[128,4096]{1,0:T(8,128)(2,1)}, bf16[512,1024]{1,0:T(8,128)(2,1)}), (bf16[128,3072]{1,0:T(8,128)(2,1)}, bf16[128,1024]{1,0:T(8,128)(2,1)}, ...) | async-done | bytes 3145744 | tf_op jit(solution)/shard_map/psum | solution.py:181
  653.9 1.9 convert_element_type.153
  655.8 2.4 convert_element_type.151
  658.2 2.8 convert_element_type.155
  661.0 1.6 convert_element_type.157
  (114 shorter events, 2.9 us)
Async XLA Ops:
  7.2 51.2 %all-gather.6.cloned.1.call-start = ((), (), s32[]{:S(2)}) async-start(), calls=%async_computation.4 | async-start | bytes 7077888 | tf_op jit(solution)/shard_map/all_gather | solution.py:132
  7.9 104.5 %all-gather.8.cloned.1.call-start = ((), (), s32[]{:S(2)}) async-start(), calls=%async_computation.5 | async-start | bytes 2359296 | tf_op jit(solution)/shard_map/all_gather | solution.py:132
  8.7 135.9 %all-gather.10.cloned.1.call-start = ((), (), s32[]{:S(2)}) async-start(), calls=%async_computation.6 | async-start | bytes 9437184 | tf_op jit(solution)/shard_map/all_gather | solution.py:132
  9.4 191.3 %all-gather.12.cloned.1.call-start = ((), (), s32[]{:S(2)}) async-start(), calls=%async_computation.7 | async-start | bytes 9437184 | tf_op jit(solution)/shard_map/all_gather | solution.py:132
  10.0 375.3 %reduce-scatter.7.cloned.1.call-start = ((), (), s32[]{:S(2)}) async-start(), calls=%async_computation.9 | async-start | bytes 2359296 | tf_op jit(solution)/shard_map/reduce_scatter | solution.py:180
  47.3 11.1 %copy-start.2 = (bf16[1,1024,1024]{1,2,0:T(8,128)(2,1)}, bf16[1,1024,1024]{1,2,0:T(8,128)(2,1)S(1)}, u32[]{:S(2)}) copy-start(bf16[1,1024,1024]{1,2,0:T(8,128)(2,1)S(1)} %copy.35) | copy-start | bytes 6291460
  47.6 22.8 %copy-start.14 = (f32[1024]{0:T(1024)}, f32[1024]{0:T(1024)S(1)}, u32[]{:S(2)}) copy-start(f32[1024]{0:T(1024)S(1)} %broadcast_multiply_fusion.1) | copy-start | bytes 12292
  48.3 4.0 copy-start.26
  48.3 22.1 %copy-start.24 = (f32[1024]{0:T(1024)}, f32[1024]{0:T(1024)S(1)}, u32[]{:S(2)}) copy-start(f32[1024]{0:T(1024)S(1)} %fusion.51) | copy-start | bytes 12292
  52.3 18.1 %copy-start.22 = (f32[1024]{0:T(1024)}, f32[1024]{0:T(1024)S(1)}, u32[]{:S(2)}) copy-start(f32[1024]{0:T(1024)S(1)} %get-tuple-element.60) | copy-start | bytes 12292
  52.3 18.1 %copy-start.34 = (f32[1024]{0:T(1024)}, f32[1024]{0:T(1024)S(1)}, u32[]{:S(2)}) copy-start(f32[1024]{0:T(1024)S(1)} %get-tuple-element.59) | copy-start | bytes 12292
  52.3 66.1 %copy-start.20 = (f32[1024]{0:T(1024)}, f32[1024]{0:T(1024)S(1)}, u32[]{:S(2)}) copy-start(f32[1024]{0:T(1024)S(1)} %get-tuple-element.57) | copy-start | bytes 12292
  52.3 66.1 %copy-start.30 = (f32[1024]{0:T(1024)}, f32[1024]{0:T(1024)S(1)}, u32[]{:S(2)}) copy-start(f32[1024]{0:T(1024)S(1)} %get-tuple-element.58) | copy-start | bytes 12292
  112.4 5.5 copy-start
  117.9 2.1 copy-start.5
  117.9 2.0 copy-start.16
  118.4 74.2 %copy-start.28 = (f32[1024]{0:T(1024)}, f32[1024]{0:T(1024)S(1)}, u32[]{:S(2)}) copy-start(f32[1024]{0:T(1024)S(1)} %multiply_reduce_fusion.2) | copy-start | bytes 12292
  118.4 1.5 copy-start.18
  121.9 78.8 %copy-start.9 = (bf16[1,1024,1024]{1,2,0:T(8,128)(2,1)S(1)}, bf16[1,1024,1024]{1,2,0:T(8,128)(2,1)}, u32[]{:S(2)}) copy-start(bf16[1,1024,1024]{1,2,0:T(8,128)(2,1)} %copy.39) | copy-start | bytes 6291460
  239.6 5.3 copy-start.17
  239.6 5.3 copy-start.19
  239.6 5.3 copy-start.21
  244.9 4.9 copy-start.29
  244.9 4.9 copy-start.6
  245.0 5.9 copy-start.8
  251.9 2.1 copy-start.7
  251.9 3.4 copy-start.1
  254.0 1.3 copy-start.12
  255.4 3.8 copy-start.36
  259.1 126.2 %reduce-scatter.5.cloned.1.call-start = ((), (), s32[]{:S(2)}) async-start(), calls=%async_computation.8 | async-start | bytes 7077888 | tf_op jit(solution)/shard_map/reduce_scatter | solution.py:180
  301.6 6.7 copy-start.3
  301.6 6.7 copy-start.15
  301.6 6.7 copy-start.23
  301.6 6.7 copy-start.25
  301.6 6.7 copy-start.35
  305.6 2.7 copy-start.11
  317.1 136.7 %reduce-scatter.11.cloned.1.call-start = ((), (), s32[]{:S(2)}) async-start(), calls=%async_computation.11 | async-start | bytes 9437184 | tf_op jit(solution)/shard_map/reduce_scatter | solution.py:180
  332.2 0.7 copy-start.31
  332.2 196.7 %reduce-scatter.9.cloned.1.call-start = ((), (), s32[]{:S(2)}) async-start(), calls=%async_computation.10 | async-start | bytes 9437184 | tf_op jit(solution)/shard_map/reduce_scatter | solution.py:180
  348.2 305.7 %all-reduce.5.cloned.1.call-start = ((), (), s32[]{:S(2)}) async-start(), calls=%async_computation.12 | async-start | bytes 6291456 | tf_op jit(solution)/shard_map/psum | solution.py:181
  360.9 5.5 copy-start.32
  369.8 159.1 %copy-start.27 = (f32[1024]{0:T(1024)S(1)}, f32[1024]{0:T(1024)}, u32[]{:S(2)}) copy-start(f32[1024]{0:T(1024)} %copy-done.26) | copy-start | bytes 12292
  533.0 3.9 copy-start.4
  533.0 4.2 copy-start.10
  542.6 5.4 copy-start.33
  653.9 7.1 %copy-start.13 = (bf16[512,1024]{1,0:T(8,128)(2,1)S(1)}, bf16[512,1024]{1,0:T(8,128)(2,1)}, u32[]{:S(2)}) copy-start(bf16[512,1024]{1,0:T(8,128)(2,1)} %get-tuple-element.52) | copy-start | bytes 3145732
Sparse Core Ops, SparseCore 0:
  9.9 48.4 all-gather.5
  60.3 27.9 all-gather.7
  90.1 54.3 all-gather.9
  146.3 54.3 all-gather.11
  259.2 41.2 reduce-scatter.6
  317.2 61.7 reduce-scatter.4
  382.5 71.2 reduce-scatter.10
  457.6 71.2 reduce-scatter.8
  531.5 122.3 all-reduce.4

commit v2 on v1

v2 whole, which is shorter than its diff:
```python
import functools

import jax
import jax.numpy as jnp
from jax import lax
from jax.experimental import pallas as pl
from jax.experimental.pallas import tpu as pltpu
from jax.sharding import PartitionSpec as P

HEADS = 16
HEAD_DIM = 64
BUCKETS = 32
T = 256
NEG = -1e30
F32 = jnp.float32
BF = jnp.bfloat16
GROUPS = 8
CHUNKS = 4
HEAD_GROUPS = 4
NN = (((1,), (0,)), ((), ()))
NT = (((1,), (1,)), ((), ()))
TN = (((0,), (0,)), ((), ()))
TT = (((0,), (1,)), ((), ()))
ANY = pl.BlockSpec(memory_space=pl.ANY)
SMEM = pl.BlockSpec(memory_space=pltpu.SMEM)


def dot(a, b, form=NN):
    return lax.dot_general(a, b, form, preferred_element_type=F32)


def params(mib=60):
    return pltpu.CompilerParams(vmem_limit_bytes=mib << 20)


def cost(flops, moved, exps=0):
    return pl.CostEstimate(flops=int(flops), bytes_accessed=int(moved), transcendentals=int(exps))


def resident(shape):
    return pl.BlockSpec(shape, lambda i, *_: (0,) * len(shape))


def shape_of(shape, kind):
    return jax.ShapeDtypeStruct(shape, kind)


def last_block(part, width):
    at = part.shape[1] // width - 1
    return pl.BlockSpec((part.shape[0], width), lambda i: (0, at))


def block_of(me, r):
    return pl.multiple_of(jnp.bitwise_xor(me, r) * 128, 128)


PLACES = ((0, 0, 1), (2, 0, 1), (4, 0, 1), (6, 0, 2), (6, 1, 2), (1, 0, 1), (3, 0, 1), (5, 0, 1), (7, 0, 2), (7, 1, 2))


def in_order(parts):
    by = {(r, half): p for (r, half, _), p in zip(PLACES, parts)}
    return [by[r, half] for r in range(8) for half in range(2 if r >= 6 else 1)]


def normalise(v):
    centred = v - jnp.mean(v, axis=-1, keepdims=True)
    rstd = lax.rsqrt(jnp.mean(centred * centred, axis=-1, keepdims=True) + 1e-5)
    return centred * rstd, rstd


def with_deps(kernel, inputs, count):
    def body(*refs):
        return kernel(*refs[:inputs], *refs[inputs + count:])
    return body


def prepare_kernel(me_ref, len_ref, x_ref, cot_ref, bucket_ref, *refs):
    small_ref, n1t_ref, og_ref, vec_ref, base_ref, abs_s = refs
    me = me_ref[0]
    rows = x_ref.shape[0]

    @pl.when(pl.program_id(0) == 0)
    def _():
        small = small_ref[...].astype(F32)
        for r in range(8):
            for k in range(4):
                vec_ref[k:k + 1, pl.ds(block_of(me, r), 128)] = small[r:r + 1, k * 128:(k + 1) * 128]
        table = jnp.concatenate([
            small[h // 2:h // 2 + 1, 512 + h % 2 * BUCKETS:512 + (h % 2 + 1) * BUCKETS] for h in range(HEADS)]).astype(BF)
        slots = bucket_ref.shape[1]
        onehot = (bucket_ref[...] == lax.broadcasted_iota(jnp.int32, (BUCKETS, slots), 0)).astype(BF)
        by = dot(table, onehot)
        for u in range(slots // T):
            base_ref[:, u, :] = by[:, slots - (u + 1) * T:slots - u * T]

    hat, _ = normalise(x_ref[...].astype(F32))
    abs_s[...] = hat * vec_ref[0:1] + vec_ref[1:2]
    for r in range(8):
        n1t_ref[r * 128:(r + 1) * 128, :] = abs_s[:, pl.ds(block_of(me, r), 128)].astype(BF).T
    slot = pl.program_id(0) * rows + lax.broadcasted_iota(jnp.int32, (rows, 1), 0)
    og_ref[...] = jnp.where(slot < len_ref[0], cot_ref[...], jnp.zeros_like(cot_ref))


def prepare(me, lengths, x, cot, buckets, small, deps=()):
    rows, width = x.shape
    tile = pl.BlockSpec((T, width), lambda i: (i, 0))
    return pl.pallas_call(
        with_deps(prepare_kernel, 6, len(deps)), grid=(rows // T,), name="prepare",
        in_specs=[SMEM, SMEM, tile, tile, resident(buckets.shape), resident(small.shape)] + [ANY] * len(deps),
        out_specs=[pl.BlockSpec((width, T), lambda i: (0, i)), tile, resident((4, width)), resident((HEADS, rows // T, T))],
        out_shape=[shape_of((width, rows), BF), shape_of((rows, width), BF), shape_of((4, width), F32),
                   shape_of((HEADS, rows // T, T), F32)],
        scratch_shapes=[pltpu.VMEM((T, width), F32)],
        compiler_params=params(), cost_estimate=cost(1e9, 8e6),
    )(me, lengths, x, cot, buckets, small, *deps)


def pack_kernel(wi_ref, wd_ref, *refs):
    for c, out in enumerate(refs):
        for k in range(2):
            for b in range(8):
                col = (b * CHUNKS + 2 * c + k) * 128
                out[k, :128, b * 128:(b + 1) * 128] = wi_ref[:, col:col + 128]
            out[k, 128:, :] = wd_ref[(2 * c + k) * 128:(2 * c + k + 1) * 128, :]


def pack(w_in, w_down, deps):
    vm = pl.BlockSpec(memory_space=pltpu.VMEM)
    return pl.pallas_call(
        with_deps(pack_kernel, 2, len(deps)), name="pack", in_specs=[vm] * 2 + [ANY] * len(deps), out_specs=[vm] * 2,
        out_shape=[shape_of((2, 256, 1024), BF)] * 2, compiler_params=params(), cost_estimate=cost(1e6, 4e6),
    )(w_in, w_down, *deps)


def lead_kernel(qkv_ref, out_ref, a_ref, b_ref, c_ref, d_ref, e_ref, piece_ref, small_ref):
    cols = qkv_ref.shape[1]
    piece_ref[:, :cols] = qkv_ref[...]
    piece_ref[:, cols:] = out_ref[...]
    at = 0
    for ref in (a_ref, b_ref, c_ref, d_ref, e_ref):
        small_ref[:, at:at + ref.shape[1]] = ref[...]
        at += ref.shape[1]


def lead(w_qkv, w_out, *small):
    vm = pl.BlockSpec(memory_space=pltpu.VMEM)
    rows, cols = w_qkv.shape[0], w_qkv.shape[1] + w_out.shape[1]
    small = [v[None] for v in small]
    return pl.pallas_call(
        lead_kernel, name="lead", in_specs=[vm] * 7, out_specs=[vm] * 2,
        out_shape=[shape_of((rows, cols), BF), shape_of((1, sum(v.shape[1] for v in small)), BF)],
        compiler_params=params(), cost_estimate=cost(1e6, 2e6),
    )(w_qkv, w_out, *small)


def project_kernel(n1t_ref, *refs):
    w = jnp.concatenate([r[...] for r in in_order(refs[:10])], axis=0)
    out = dot(w, n1t_ref[...], TN).astype(BF)
    refs[10][...] = out.reshape(refs[10].shape)


def project(n1t, parts):
    width, rows = n1t.shape
    cols = 3 * width
    tile = 512
    return pl.pallas_call(
        project_kernel, grid=(cols // tile,), name="project",
        in_specs=[resident((width, rows))] + [pl.BlockSpec((p.shape[0], tile), lambda i: (0, i)) for p in parts],
        out_specs=pl.BlockSpec((tile // HEAD_DIM, HEAD_DIM, rows), lambda i: (i, 0, 0)),
        out_shape=shape_of((cols // HEAD_DIM, HEAD_DIM, rows), BF),
        compiler_params=params(), cost_estimate=cost(2 * rows * width * cols, 14e6),
    )(n1t, *parts)


def toeplitz(base_ref):
    row = lax.broadcasted_iota(jnp.int32, (T, T), 0)
    col = lax.broadcasted_iota(jnp.int32, (T, T), 1)
    count = base_ref.shape[1]
    rolled = [
        pltpu.roll(jnp.broadcast_to(base_ref[0, u:u + 1, :], (T, T)), 0, 1, stride=1, stride_axis=0)
        for u in range(count)
    ]
    return [jnp.where(col >= row, rolled[u], rolled[u + 1] if u + 1 < count else NEG) for u in range(count)]


def key_mask(len_ref, start):
    slot = start + lax.broadcasted_iota(jnp.int32, (T, 1), 0)
    return jnp.where(slot < len_ref[0], 0.0, NEG).astype(F32)


def attend_kernel(me_ref, len_ref, base_ref, q_ref, k_ref, v_ref, o_ref, lt_ref, g_ref):
    tiles = base_ref.shape[1]
    for u, t in enumerate(toeplitz(base_ref)):
        g_ref[u * T:(u + 1) * T, :] = t
    k = k_ref[0].T
    v = v_ref[0]
    for b in range(tiles):
        nk = (b + 1) * T
        sl = slice(b * T, nk)
        q = q_ref[0, :, sl] * BF(HEAD_DIM ** -0.5)
        s = dot(k[:nk], q) + g_ref[(tiles - 1 - b) * T:, :]
        if b == tiles - 1:
            s = jnp.concatenate([s[:b * T], s[b * T:] + key_mask(len_ref, b * T)], axis=0)
        m = jnp.max(s, axis=0, keepdims=True)
        p = jnp.exp(s - m)
        total = jnp.sum(p, axis=0, keepdims=True)
        o = dot(v[:, :nk], p.astype(BF))
        o_ref[0, :, sl] = (o * (1.0 / total)).astype(BF)
        lt_ref[0, :, sl] = m + jnp.log(total)


def head_place(h, me_ref):
    return jnp.bitwise_xor(h // 2, me_ref[0]) * 2 + h % 2


def attend(me, lengths, base, qkv):
    heads = HEADS
    rows = qkv.shape[-1]
    tiles = rows // T
    block = (1, HEAD_DIM, rows)
    at = lambda off: pl.BlockSpec(block, lambda h, m: (h + off, 0, 0))
    return pl.pallas_call(
        attend_kernel, name="attend",
        grid_spec=pltpu.PrefetchScalarGridSpec(
            num_scalar_prefetch=1, grid=(heads,),
            in_specs=[SMEM, pl.BlockSpec((1, tiles, T), lambda h, m: (head_place(h, m), 0, 0)), at(0), at(heads), at(2 * heads)],
            out_specs=[pl.BlockSpec(block, lambda h, m: (head_place(h, m), 0, 0)),
                       pl.BlockSpec((1, 1, rows), lambda h, m: (h, 0, 0))],
            scratch_shapes=[pltpu.VMEM((rows, T), F32)]),
        out_shape=[shape_of((heads, HEAD_DIM, rows), BF), shape_of((heads, 1, rows), F32)],
        compiler_params=params(), cost_estimate=cost(30e9, 10e6),
    )(me, lengths, base, qkv, qkv, qkv)


def skew_sums(dg_ref, dist_ref):
    row = lax.broadcasted_iota(jnp.int32, (T, T), 0)
    col = lax.broadcasted_iota(jnp.int32, (T, T), 1)
    for u in range(dist_ref.shape[1]):
        z = jnp.where(col >= row, dg_ref[u * T:(u + 1) * T, :], dg_ref[(u - 1) * T:u * T, :] if u else 0.0)
        acc = z[0:8]
        for g in range(1, T // 8):
            acc = acc + pltpu.roll(z[8 * g:8 * g + 8], T - 8 * g, 1)
        tot = acc[0:1]
        for r in range(1, 8):
            tot = tot + pltpu.roll(acc[r:r + 1], T - r, 1)
        dist_ref[0, u:u + 1, :] = tot


def attend_back_kernel(me_ref, len_ref, base_ref, q_ref, k_ref, v_ref, o_ref, do_ref, lt_ref,
                       dq_ref, dk_ref, dv_ref, dist_ref, g_ref, dg_ref, dk_s, dv_s):
    tiles = base_ref.shape[1]
    scale = HEAD_DIM ** -0.5
    for u, t in enumerate(toeplitz(base_ref)):
        g_ref[u * T:(u + 1) * T, :] = t
    kt = k_ref[0]
    k = kt.T
    v = v_ref[0].T
    for b in range(tiles - 1, -1, -1):
        nk = (b + 1) * T
        sl = slice(b * T, nk)
        low = (tiles - 1 - b) * T
        q = q_ref[0, :, sl] * BF(scale)
        do = do_ref[0, :, sl]
        inner = jnp.sum(do.astype(F32) * o_ref[0, :, sl].astype(F32), axis=0, keepdims=True)
        s = dot(k[:nk], q) + g_ref[low:, :]
        if b == tiles - 1:
            s = jnp.concatenate([s[:b * T], s[b * T:] + key_mask(len_ref, b * T)], axis=0)
        p = jnp.exp(s - lt_ref[0, :, sl])
        ds = p * (dot(v[:nk], do) - inner)
        pb = p.astype(BF)
        dsb = ds.astype(BF)
        dq_ref[0, :, sl] = (dot(kt[:, :nk], dsb) * scale).astype(BF)
        dvp = dot(do, pb, NT)
        dkp = dot(q, dsb, NT)
        if b == tiles - 1:
            dk_s[...] = dkp
            dv_s[...] = dvp
            dg_ref[...] = ds
        else:
            dk_s[:, :nk] += dkp
            dv_s[:, :nk] += dvp
            dg_ref[low:, :] += ds
    dk_ref[0] = dk_s[...].astype(BF)
    dv_ref[0] = dv_s[...].astype(BF)
    skew_sums(dg_ref, dist_ref)


def attend_back(me, lengths, base, qkv, o, do, lt, first, count, deps=()):
    rows = qkv.shape[-1]
    tiles = rows // T
    block = (1, HEAD_DIM, rows)
    at = lambda off: pl.BlockSpec(block, lambda h, m: (h + off + first, 0, 0))
    placed = pl.BlockSpec(block, lambda h, m: (head_place(h + first, m), 0, 0))
    out = pl.BlockSpec(block, lambda h, m: (h, 0, 0))
    return pl.pallas_call(
        with_deps(attend_back_kernel, 9, len(deps)), name="attend_back",
        grid_spec=pltpu.PrefetchScalarGridSpec(
            num_scalar_prefetch=1, grid=(count,),
            in_specs=[SMEM, pl.BlockSpec((1, tiles, T), lambda h, m: (head_place(h + first, m), 0, 0)), at(0), at(HEADS), at(2 * HEADS),
                      placed, placed, pl.BlockSpec((1, 1, rows), lambda h, m: (h + first, 0, 0))] + [ANY] * len(deps),
            out_specs=[out, out, out, pl.BlockSpec((1, tiles, T), lambda h, m: (h, 0, 0))],
            scratch_shapes=[pltpu.VMEM((rows, T), F32), pltpu.VMEM((rows, T), F32),
                            pltpu.VMEM((HEAD_DIM, rows), F32), pltpu.VMEM((HEAD_DIM, rows), F32)]),
        out_shape=[shape_of((count, HEAD_DIM, rows), BF)] * 3 + [shape_of((count, tiles, T), F32)],
        compiler_params=params(), cost_estimate=cost(2.4e9 * count, 1.2e6 * count),
    )(me, lengths, base, qkv, qkv, qkv, o, do, lt, *deps)


def middle_kernel(me_ref, at_ref, x_ref, gain_ref, shift_ref, *refs):
    parts, (mid_ref, n2_ref, n2t_ref, abs_s) = refs[:10], refs[10:]
    me = me_ref[0]
    w = jnp.concatenate([r[...] for r in in_order(parts)], axis=0)
    mid = x_ref[...].astype(F32) + dot(at_ref[...], w, TN)
    mid_ref[...] = mid
    hat, _ = normalise(mid)
    abs_s[...] = hat * gain_ref[...] + shift_ref[...]
    for r in range(8):
        sl = slice(r * 128, (r + 1) * 128)
        part = abs_s[:, pl.ds(block_of(me, r), 128)].astype(BF)
        n2_ref[:, sl] = part
        n2t_ref[sl, :] = part.T


def middle_of(me, at, x, gain, shift, parts, deps=()):
    rows, width = x.shape
    tile = pl.BlockSpec((T, width), lambda i: (i, 0))
    turned = pl.BlockSpec((width, T), lambda i: (0, i))
    return pl.pallas_call(
        with_deps(middle_kernel, 5 + len(parts), len(deps)), grid=(rows // T,), name="middle",
        in_specs=[SMEM, turned, tile, resident((1, width)), resident((1, width))] + [last_block(p, width) for p in parts]
        + [ANY] * len(deps),
        out_specs=[tile, tile, turned],
        out_shape=[shape_of((rows, width), F32), shape_of((rows, width), BF), shape_of((width, rows), BF)],
        scratch_shapes=[pltpu.VMEM((T, width), F32)],
        compiler_params=params(), cost_estimate=cost(2 * rows * width * width, 14e6),
    )(me, at, x, gain, shift, *parts, *deps)


def gelu_parts(x):
    a = jnp.abs(x)
    t = 1.0 / (1.0 + a * (0.3275911 * 0.7071067811865476))
    e = jnp.exp(x * x * -0.5)
    poly = t * (0.127414796 + t * (-0.142248368 + t * (0.7107068705 + t * (-0.7265760135 + t * 0.5307027145))))
    q = poly * e
    phi = jnp.where(x >= 0.0, 1.0 - q, q)
    return x * phi, phi + x * (e * 0.3989422804014327)


def feed_kernel(c, stacked, counts, me_ref, n2_h, n2t_h, og_h, w_h, *refs):
    carried, held, deps, outs = counts
    carry, refs = refs[:carried], refs[carried + held + deps:]
    outs, refs = refs[:outs], refs[outs:]
    n2_v, n2t_v, og_v, w_v, y_v, g_v, send_v, keep_v, sem_in, sem_out = refs
    me = me_ref[0]
    loads = [(n2_h, n2_v)]
    loads += [(w_h.at[jnp.bitwise_xor(me, r), c], w_v.at[r]) for r in range(8)]
    loads += [(og_h, og_v)]
    early = len(loads)
    loads += list(zip(carry, (y_v, g_v))) + [(n2t_h, n2t_v)]
    copies = [pltpu.make_async_copy(a, b, sem_in.at[i]) for i, (a, b) in enumerate(loads)]
    for x in copies:
        x.start()
    for x in copies[:early]:
        x.wait()
    pairs = [(y_v, outs[0]), (g_v, outs[1])]
    if stacked:
        pairs += [((send_v if r % 2 else keep_v).at[r // 2], outs[2].at[jnp.bitwise_xor(me, r), c]) for r in range(8)]
    else:
        pairs += [(send_v, outs[2].at[:, c]), (keep_v, outs[3].at[:, c])]
    stores = [pltpu.make_async_copy(a, b, sem_out.at[i]) for i, (a, b) in enumerate(pairs)]
    n2 = n2_v[...]
    og = og_v[...]
    for t in range(2):
        offs = [block_of(me, 4 * t + j) for j in range(4)]
        wi = jnp.concatenate([w_v[:, :128, pl.ds(o, 128)].reshape(1024, 128) for o in offs], axis=1)
        wd = w_v[4 * t:4 * t + 4, 128:, :].reshape(512, 1024)
        hid, slope = gelu_parts(dot(n2, wi))
        hid = hid.astype(BF)
        pre = (dot(og, wd, NT) * slope).astype(BF)
        if t == 0:
            for x in copies[early:]:
                x.wait()
        if not carried and t == 0:
            y_v[...] = dot(hid, wd)
            g_v[...] = dot(pre, wi, NT)
        else:
            y_v[...] += dot(hid, wd)
            g_v[...] += dot(pre, wi, NT)
        if t == 1:
            stores[0].start()
            stores[1].start()
        dwi = dot(n2t_v[...], pre).astype(BF)
        for r in range(8):
            for j, o in enumerate(offs):
                (send_v if r % 2 else keep_v)[r // 2, :128, pl.ds(o, 128)] = dwi[r * 128:(r + 1) * 128, j * 128:(j + 1) * 128]
        dwd = dot(hid, og, TN).astype(BF)
        for j in range(4):
            r = 4 * t + j
            (send_v if r % 2 else keep_v)[r // 2, 128:, :] = dwd[j * 128:(j + 1) * 128]
    for x in stores[2:]:
        x.start()
    for x in stores:
        x.wait()


def feed(c, stacked, me, n2, n2t, og, w, carry, held, deps=()):
    rows, width = n2.shape
    half = (4, 256, 1024)
    carry = carry or ()
    grads = [(8, 2, 256, 1024)] if stacked else [(4, 2, 256, 1024)] * 2
    counts = (len(carry), len(held), len(deps), 2 + len(grads))
    n_in = 11 + len(carry)
    n_out = 10 if stacked else 4
    return pl.pallas_call(
        functools.partial(feed_kernel, c, stacked, counts), name="feed",
        in_specs=[SMEM] + [ANY] * (4 + sum(counts[:3])), out_specs=[ANY] * counts[3],
        out_shape=[shape_of((rows, width), F32)] * 2 + [shape_of(g, BF) for g in grads],
        input_output_aliases={5 + len(carry) + i: 2 + i for i in range(len(held))},
        scratch_shapes=[pltpu.VMEM((rows, width), BF), pltpu.VMEM((width, rows), BF), pltpu.VMEM((rows, width), BF),
                        pltpu.VMEM((8, 256, 1024), BF), pltpu.VMEM((rows, width), F32), pltpu.VMEM((rows, width), F32),
                        pltpu.VMEM(half, BF), pltpu.VMEM(half, BF),
                        pltpu.SemaphoreType.DMA((n_in,)), pltpu.SemaphoreType.DMA((n_out,))],
        compiler_params=params(), cost_estimate=cost(20e9, 30e6),
    )(me, n2, n2t, og, w, *carry, *held, *deps)


def norm_back(hat, rstd, grad, gain):
    t = grad * gain
    return (t - jnp.mean(t, axis=-1, keepdims=True) - hat * jnp.mean(t * hat, axis=-1, keepdims=True)) * rstd


def middle_back_kernel(me_ref, mid_ref, g_ref, og_ref, at_ref, gain_ref, *refs):
    parts, (mg_ref, do_ref, send_ref, keep_ref, vec_ref, abs_s, acc_s) = refs[:10], refs[10:]
    me = me_ref[0]
    i = pl.program_id(0)
    for r in range(8):
        abs_s[:, pl.ds(block_of(me, r), 128)] = g_ref[:, r * 128:(r + 1) * 128]
    grad = abs_s[...]
    hat, rstd = normalise(mid_ref[...])
    sums = jnp.concatenate([jnp.sum(grad * hat, axis=0, keepdims=True), jnp.sum(grad, axis=0, keepdims=True)], axis=0)
    mg = og_ref[...].astype(F32) + norm_back(hat, rstd, grad, gain_ref[...])
    mg_ref[...] = mg
    branch = mg.astype(BF)
    w = jnp.concatenate([r[...] for r in in_order(parts)], axis=0)
    do_ref[...] = dot(w, branch, NT).astype(BF)
    dw = dot(at_ref[...], branch)

    @pl.when(i == 0)
    def _():
        vec_ref[...] = sums
        acc_s[...] = dw

    @pl.when(i > 0)
    def _():
        vec_ref[...] += sums
        acc_s[...] += dw

    @pl.when(i == pl.num_programs(0) - 1)
    def _():
        for r in range(8):
            (send_ref if r % 2 else keep_ref)[r // 2] = acc_s[r * 128:(r + 1) * 128, :].astype(BF)


def middle_back(me, mid, g, og, at, gain, parts, deps=()):
    rows, width = mid.shape
    tile = pl.BlockSpec((T, width), lambda i: (i, 0))
    turned = pl.BlockSpec((width, T), lambda i: (0, i))
    block = (4, 128, width)
    return pl.pallas_call(
        with_deps(middle_back_kernel, 6 + len(parts), len(deps)), grid=(rows // T,), name="middle_back",
        in_specs=[SMEM, tile, tile, tile, turned, resident((1, width))] + [last_block(p, width) for p in parts] + [ANY] * len(deps),
        out_specs=[tile, turned, resident(block), resident(block), resident((2, width))],
        out_shape=[shape_of((rows, width), F32), shape_of((width, rows), BF), shape_of(block, BF), shape_of(block, BF),
                   shape_of((2, width), F32)],
        scratch_shapes=[pltpu.VMEM((T, width), F32), pltpu.VMEM((width, width), F32)],
        compiler_params=params(), cost_estimate=cost(4 * rows * width * width, 24e6),
    )(me, mid, g, og, at, gain, *parts, *deps)


def staged_kernel(steps, count, deps, where_ref, *refs):
    n_out = sum(len(outs) for _, outs, _ in steps)
    sources, refs = refs[:count], refs[count + deps:]
    dests, refs = refs[:n_out], refs[n_out:]
    held, kept, sem_in, sem_out = refs[:count], refs[count:count + n_out], refs[-2], refs[-1]
    loads = []
    for ins, _, _ in steps:
        for _, index in ins:
            k = len(loads)
            loads.append(pltpu.make_async_copy(sources[k].at[index] if index else sources[k], held[k], sem_in.at[k]))
    for c in loads:
        c.start()
    stores = []
    a = b = 0
    for ins, outs, fn in steps:
        for c in loads[a:a + len(ins)]:
            c.wait()
        fn(where_ref, held[a:a + len(ins)], kept[b:b + len(outs)])
        for k in range(b, b + len(outs)):
            stores.append(pltpu.make_async_copy(kept[k], dests[k], sem_out.at[k]))
            stores[-1].start()
        a += len(ins)
        b += len(outs)
    for c in stores:
        c.wait()


def staged(where, steps, deps=()):
    steps = [([v if isinstance(v, tuple) else (v, ()) for v in ins], outs, fn) for ins, outs, fn in steps]
    arrays = [v for ins, _, _ in steps for v, _ in ins]
    held = [shape_of(v.shape[len(index):], v.dtype) for ins, _, _ in steps for v, index in ins]
    outs = [o for _, outs, _ in steps for o in outs]
    flat = pl.pallas_call(
        functools.partial(staged_kernel, steps, len(arrays), len(deps)), name="staged",
        in_specs=[SMEM] + [ANY] * (len(arrays) + len(deps)), out_specs=[ANY] * len(outs), out_shape=outs,
        scratch_shapes=[pltpu.VMEM(v.shape, v.dtype) for v in held + outs]
        + [pltpu.SemaphoreType.DMA((len(arrays),)), pltpu.SemaphoreType.DMA((len(outs),))],
        compiler_params=params(), cost_estimate=cost(3e9, 10e6),
    )(where, *arrays, *deps)
    result = []
    for _, o, _ in steps:
        result.append(flat[:len(o)])
        flat = flat[len(o):]
    return result


def plus(*refs):
    total = refs[0].astype(F32)
    for r in refs[1:]:
        total = total + r.astype(F32)
    return total


def project_back(n1t, three, extra=()):
    cols = three[0].shape[0]
    before = sum(e[0].shape[2] for e in extra)
    block = shape_of((4, 128, before + 3 * cols), BF)

    def fn(_, ins, outs):
        at = 0
        for k in range(len(extra)):
            width = ins[4 + 2 * k].shape[2]
            outs[0][:, :, at:at + width] = ins[4 + 2 * k][...]
            outs[1][:, :, at:at + width] = ins[5 + 2 * k][...]
            at += width
        n1 = ins[0][...]
        for j in range(3):
            dw = dot(n1, ins[1 + j][...], NT).astype(BF)
            for r in range(8):
                outs[r % 2 == 0][r // 2, :, at + j * cols:at + (j + 1) * cols] = dw[r * 128:(r + 1) * 128]

    return [n1t, *three] + [v for e in extra for v in e], [block, block], fn


def finish_kernel(groups, me_ref, len_ref, x_ref, mid_ref, y_ref, mg_ref, gain_ref, *refs):
    parts, refs = refs[:10], refs[10:]
    grads, (out_ref, ig_ref, vec_ref, abs_s) = refs[:3 * groups], refs[3 * groups:]
    me = me_ref[0]
    i = pl.program_id(0)
    rows, width = x_ref.shape
    w = jnp.concatenate([r[...] for r in in_order(parts)], axis=0)
    total = jnp.zeros((rows, width), F32)
    pg = jnp.concatenate([grads[3 * g + j][...] for j in range(3) for g in range(groups)], axis=0)
    total = dot(pg, w, TT)
    for r in range(8):
        abs_s[:, pl.ds(block_of(me, r), 128)] = total[:, r * 128:(r + 1) * 128]
    grad = abs_s[...]
    hat, rstd = normalise(x_ref[...].astype(F32))
    sums = jnp.concatenate([jnp.sum(grad * hat, axis=0, keepdims=True), jnp.sum(grad, axis=0, keepdims=True)], axis=0)
    ig_ref[...] = mg_ref[...] + norm_back(hat, rstd, grad, gain_ref[...])
    slot = i * rows + lax.broadcasted_iota(jnp.int32, (rows, 1), 0)
    out_ref[...] = jnp.where(slot < len_ref[0], mid_ref[...] + y_ref[...], 0.0).astype(BF)

    @pl.when(i == 0)
    def _():
        vec_ref[...] = sums

    @pl.when(i > 0)
    def _():
        vec_ref[...] += sums


def finish(me, lengths, x, mid, y, mg, gain, parts, grads, deps=()):
    rows, width = x.shape
    tile = pl.BlockSpec((T, width), lambda i: (i, 0))
    return pl.pallas_call(
        with_deps(functools.partial(finish_kernel, len(grads) // 3), 7 + len(parts) + len(grads), len(deps)),
        grid=(rows // T,), name="finish",
        in_specs=[SMEM, SMEM, tile, tile, tile, tile, resident((1, width))] + [resident((p.shape[0], 3 * width)) for p in parts]
        + [pl.BlockSpec((g.shape[0], T), lambda i: (0, i)) for g in grads] + [ANY] * len(deps),
        out_specs=[tile, tile, resident((2, width))],
        out_shape=[shape_of((rows, width), BF), shape_of((rows, width), F32), shape_of((2, width), F32)],
        scratch_shapes=[pltpu.VMEM((T, width), F32)],
        compiler_params=params(), cost_estimate=cost(6 * rows * width * width, 34e6),
    )(me, lengths, x, mid, y, mg, gain, *parts, *grads, *deps)


def flip(v, k):
    return lax.ppermute(v, "fsdp", [(i, i ^ k) for i in range(GROUPS)])


def xor_rows(v, me):
    for k in (1, 2, 4):
        turned = v.reshape((8 // (2 * k), 2, k) + v.shape[1:])[:, ::-1].reshape(v.shape)
        v = jnp.where((me & k) != 0, turned, v)
    return v


def split_full(full):
    m = full.shape[0] // 8
    return [full[r * m + half * (m // of):r * m + (half + 1) * (m // of)] for r, half, of in PLACES]


def add(*vs):
    total = vs[0].astype(F32)
    for v in vs[1:]:
        total = total + v.astype(F32)
    return total.astype(vs[0].dtype)


def scatter_sums(keep, got):
    h, c = keep.shape[1] // 2, keep.shape[2]

    def fn(_, ins, outs):
        k, g = ins
        for out, half, pair in zip(outs, (0, 1, 0, 1), ((1, 3), (2, 3), (0, 2), (0, 1))):
            for n, j in enumerate(pair):
                out[n] = plus(k[j, half * h:(half + 1) * h, :], g[j, half * h:(half + 1) * h, :]).astype(BF)

    return [keep, got], [shape_of((2, h, c), BF)] * 4, fn


def scatter_second(sums, ga, gb):
    def fn(_, ins, outs):
        outs[0][...] = plus(ins[0][...], ins[1][...]).astype(BF)
        outs[1][...] = plus(ins[2][...], ins[3][...]).astype(BF)

    return [(sums[2], (1,)), (ga, (1,)), (sums[3], (1,)), (gb, (1,))], [shape_of(sums[2].shape[1:], BF)] * 2, fn


def scatter_last(sums, ga, gb, fa, fb, split):
    h, c = fa.shape

    def fn(where, ins, outs):
        a = plus(ins[0][...], ins[1][...], ins[2][...]).astype(BF)
        b = plus(ins[3][...], ins[4][...], ins[5][...]).astype(BF)
        if split:
            odd = where[1] == 1
            outs[0][...] = jnp.where(odd, a, b)
            outs[1][...] = jnp.where(odd, b, a)
        else:
            outs[0][:h] = a
            outs[0][h:] = b

    out = [shape_of((h, c), BF)] * 2 if split else [shape_of((2 * h, c), BF)]
    return [(sums[2], (0,)), (ga, (0,)), fa, (sums[3], (0,)), (gb, (0,)), fb], out, fn


def copies_second(keep, got):
    q, c = keep.shape[0] // 2, keep.shape[1]

    def fn(where, ins, outs):
        a = plus(ins[0][:q], ins[1][:q]).astype(BF)
        b = plus(ins[0][q:], ins[1][q:]).astype(BF)
        high = where[2] == 1
        outs[0][...] = jnp.where(high, a, b)
        outs[1][...] = jnp.where(high, b, a)

    return [keep, got], [shape_of((q, c), BF)] * 2, fn


def copies_third(keep, got):
    def fn(_, ins, outs):
        outs[0][...] = plus(ins[0][...], ins[1][...]).astype(BF)

    return [keep, got], [shape_of(keep.shape, BF)], fn


def copies_join(mine, got, bit):
    q, c = mine.shape

    def fn(where, ins, outs):
        second = where[bit] == 1
        a, b = ins[0][...], ins[1][...]
        outs[0][:q] = jnp.where(second, b, a)
        outs[0][q:] = jnp.where(second, a, b)

    return [mine, got], [shape_of((2 * q, c), BF)], fn


def vector_sums(where, vec_one, vec_two, dists, buckets):
    def fn(where, ins, outs):
        by = jnp.concatenate([jnp.concatenate([d[:, u, :] for u in range(d.shape[1] - 1, -1, -1)], axis=1) for d in ins[2:-1]])
        onehot = (ins[-1][...] == lax.broadcasted_iota(jnp.int32, (BUCKETS, by.shape[1]), 0)).astype(F32)
        table = lax.dot_general(by, onehot, NT, precision=lax.Precision.HIGHEST, preferred_element_type=F32)
        outs[2][...] = jnp.concatenate([jnp.concatenate([table[2 * r:2 * r + 1], table[2 * r + 1:2 * r + 2]], axis=1) for r in range(8)])
        for r in range(8):
            out = outs[1 - r % 2]
            row = slice(r // 2, r // 2 + 1)
            for k in range(4):
                out[row, k * 128:(k + 1) * 128] = ins[k // 2][k % 2:k % 2 + 1, pl.ds(block_of(where[0], r), 128)]
            out[row, 512:] = outs[2][pl.ds(jnp.bitwise_xor(where[0], r), 1), :]

    out = shape_of((4, 576), F32)
    return [vec_one, vec_two, *dists, buckets], [out, out, shape_of((8, 64), F32)], fn


def vector_halve(keep, got):
    n = keep.shape[0] // 2

    def fn(_, ins, outs):
        for k in range(n):
            for out, row in zip(outs, (2 * k + 1, 2 * k)):
                out[k:k + 1] = ins[0][row:row + 1] + ins[1][row:row + 1]

    return [keep, got], [shape_of((n, 576), F32)] * 2, fn


def vector_add(*vs):
    def fn(_, ins, outs):
        outs[0][...] = plus(*(r[...] for r in ins))

    return list(vs), [shape_of(vs[0].shape, F32)], fn


def feed_result(one, two):
    def fn(_, ins, outs):
        for c in range(CHUNKS):
            v = ins[c // 2]
            base = c % 2 * 256
            for b in range(8):
                col = (b * CHUNKS + c) * 128
                outs[0][:, col:col + 128] = v[base:base + 128, b * 128:(b + 1) * 128].astype(F32)
            outs[1][c * 128:(c + 1) * 128, :] = v[base + 128:base + 256, :].astype(F32)

    return [one, two], [shape_of((128, 4096), F32), shape_of((512, 1024), F32)], fn


def project_result(v1, v3, x3, v4, x4):
    def fn(where, ins, outs):
        qkv, out = outs
        v1, v3, x3, *v4 = ins
        width = out.shape[1]
        part = qkv.shape[1] // (3 * HEAD_GROUPS)
        out[...] = v1[:, :width].astype(F32)
        odd = where[1] == 1
        a, b = v3[...], x3[...]
        both = jnp.concatenate([jnp.where(odd, b, a), jnp.where(odd, a, b)]).astype(F32)
        last = plus(*(r[...] for r in v4)).astype(BF).astype(F32)
        for j in range(3):
            base = j * HEAD_GROUPS * part
            qkv[:, base:base + part] = v1[:, width + j * part:width + (j + 1) * part].astype(F32)
            for g in range(2):
                at = (3 * g + j) * part
                qkv[:, base + (g + 1) * part:base + (g + 2) * part] = both[:, at:at + part]
            qkv[:, base + 3 * part:base + 4 * part] = last[:, j * part:(j + 1) * part]

    return [v1, v3, x3, v4, *x4], [shape_of((128, 3072), F32), shape_of((128, 1024), F32)], fn


def copy_swap(v, k):
    return lax.ppermute(v, "rep", [(i, i ^ k) for i in range(4)])


def copy_turns(v, count):
    return [lax.ppermute(v, "rep", [(i, (i + k) % count) for i in range(count)]) for k in range(1, count)]


def copies_sum_flat(v, count):
    return add(v, *(lax.ppermute(v, "rep", [(i, (i + k) % count) for i in range(count)]) for k in range(1, count)))


def per_device(n_fsdp, n_rep, inputs, lengths, bucket_table, ln1_gain, ln1_shift, w_qkv, rel_bias, w_out, ln2_gain, ln2_shift,
               w_in, w_down, cotangent):
    near = n_fsdp == GROUPS and n_rep == 4
    _, slots, width = inputs.shape
    hidden = w_in.shape[1]
    me = lax.axis_index("fsdp").astype(jnp.int32) if near else jnp.int32(0)
    me1 = me.reshape(1)
    x = inputs.reshape(slots, width)
    cot = cotangent.reshape(slots, width)
    full = lambda w: lax.all_gather(w, "fsdp", axis=0, tiled=True)

    if near:
        piece, small = lead(w_qkv, w_out, ln1_gain, ln1_shift, ln2_gain, ln2_shift, rel_bias)
        half = piece.shape[0] // 2
        r2, r4 = flip(piece, 2), flip(piece, 4)
        for k in (1, 2, 4):
            small = jnp.concatenate([small, flip(small, k)])
        n1t, og, vecs, base = prepare(me1, lengths, x, cot, bucket_table[None], small, (r2, r4))
        r6a, r6b = flip(r2[:half], 4), flip(r4[half:], 2)
        ffn_w = [full(v.reshape(512, 1024)).reshape(8, 2, 256, 1024) for v in pack(w_in, w_down, (r2, r4, n1t))]
        parts = [piece, r2, r4, r6a, r6b]
        parts = parts + [flip(v, 1) for v in parts]
    else:
        n = ln1_gain.shape[0]
        small = full(jnp.concatenate([ln1_gain, ln1_shift, ln2_gain, ln2_shift, rel_bias])[None])
        small = jnp.concatenate([small[:, i * n:(i + 1) * n].reshape(8, 128) for i in range(4)] + [small[:, 4 * n:].reshape(8, 64)], axis=1)
        n1t, og, vecs, base = prepare(me1, lengths, x, cot, bucket_table[None], small)
        parts = split_full(jnp.concatenate([full(w_qkv), full(w_out)], axis=1))
        wi_c = full(w_in).reshape(8, width // 8, 8, CHUNKS, 128)
        wd_c = full(w_down).reshape(8, CHUNKS, 128, width)
        chunk = [jnp.concatenate([wi_c[:, :, :, c].reshape(8, width // 8, 1024), wd_c[:, c]], axis=1) for c in range(CHUNKS)]
        ffn_w = [jnp.stack(chunk[2 * h:2 * h + 2], axis=1) for h in range(2)]
    n = ln1_gain.shape[0]
    gain_one, shift_one, gain_two, shift_two = (vecs[i:i + 1] for i in range(4))
    qkv = project(n1t, parts)
    o, lt = attend(me1, lengths, base, qkv)
    at = o.reshape(width, slots)
    mid, n2, n2t = middle_of(me1, at, x, gain_two, shift_two, parts)
    y, g, one = feed(0, True, me1, n2, n2t, og, ffn_w[0], (), ())
    y, g, one = feed(1, True, me1, n2, n2t, og, ffn_w[0], (y, g), (one,))
    y, g, *two = feed(0, not near, me1, n2, n2t, og, ffn_w[1], (y, g), ())
    y, g, *two = feed(1, not near, me1, n2, n2t, og, ffn_w[1], (y, g), two)
    mg, do, out_send, out_keep, vec_two = middle_back(me1, mid, g, og, at, gain_two, parts)
    do = do.reshape(HEADS, HEAD_DIM, slots)
    per = HEADS // HEAD_GROUPS
    grads, dists = [], []
    rep = lax.axis_index("rep").astype(jnp.int32)
    where = jnp.stack([me, rep % 2, rep // 2])

    def back(k, deps=()):
        *three, dist = attend_back(me1, lengths, base, qkv, o, do, lt, k * per, per, deps)
        three = [v.reshape(per * HEAD_DIM, slots) for v in three]
        grads.extend(three)
        dists.append(dist)
        return three

    if near:
        h1 = lax.psum_scatter(one.reshape(8 * 512, 1024), "fsdp", scatter_dimension=0, tiled=True)
        send2, keep2 = (v.reshape(4, 512, 1024) for v in two)
        got2 = flip(send2, 1)
        (s2,) = staged(where, [scatter_sums(keep2, got2)], (mg,))
        g2 = flip(s2[0], 2), flip(s2[1], 4)
        t0 = back(0, s2)
        ((send1, keep1),) = staged(where, [project_back(n1t, t0, [(out_send, out_keep)])], (h1,))
        h1 = lax.psum(h1, "rep")
        got1 = flip(send1, 1)
        t1 = back(1, (send1,))
        p1, f2, s1 = staged(where, [project_back(n1t, t1), scatter_second(s2, *g2), scatter_sums(keep1, got1)])
        f2 = flip(f2[0], 4), flip(f2[1], 2)
        g1 = flip(s1[0], 2), flip(s1[1], 4)
        t2 = back(2, s1)
        (send3, keep3), c2, f1 = staged(where, [project_back(n1t, t2, [p1]), scatter_last(s2, *g2, *f2, True), scatter_second(s1, *g1)])
        got3 = flip(send3, 1)
        x2 = copy_swap(c2[0], 1)
        f1 = flip(f1[0], 4), flip(f1[1], 2)
        t3 = back(3, (send3,))
        (send4, keep4), c2, c1, s3 = staged(where, [
            project_back(n1t, t3), copies_second(c2[1], x2), scatter_last(s1, *g1, *f1, True), scatter_sums(keep3, got3)])
        got4 = flip(send4, 1)
        x2 = copy_swap(c2[0], 2)
        x1 = copy_swap(c1[0], 1)
        g3 = flip(s3[0], 2), flip(s3[1], 4)
        tail = (send4,)
    else:
        pieces = [staged(where, [project_back(n1t, back(k))])[0] for k in range(HEAD_GROUPS)]
        tail = ()
    outputs, input_grad, vec_one = finish(me1, lengths, x, mid, y, mg, gain_one, parts, grads, tail)

    if near:
        (out_v, keep_v, _), s4, (v2,), c1, f3 = staged(where, [
            vector_sums(where, vec_one, vec_two, dists, bucket_table[None]),
            scatter_sums(keep4, got4), copies_third(c2[1], x2), copies_second(c1[1], x1), scatter_second(s3, *g3)], (h1,))
        got_v = flip(out_v, 1)
        g4 = flip(s4[0], 2), flip(s4[1], 4)
        x2 = copy_swap(v2, 2)
        x1 = copy_swap(c1[0], 2)
        f3 = flip(f3[0], 4), flip(f3[1], 2)
        (out_v, keep_v), f4, (v2,), (v1,), c3 = staged(where, [
            vector_halve(keep_v, got_v),
            scatter_second(s4, *g4), copies_join(v2, x2, 2), copies_third(c1[1], x1), scatter_last(s3, *g3, *f3, True)])
        f4 = flip(f4[0], 4), flip(f4[1], 2)
        x2 = copy_swap(v2, 1)
        x1 = copy_swap(v1, 2)
        x3 = copy_swap(c3[0], 1)
        got_v = flip(out_v, 2)
        (out_v, keep_v), (v4,), (h2,), (v1,), c3 = staged(where, [
            vector_halve(keep_v, got_v),
            scatter_last(s4, *g4, *f4, False), copies_join(v2, x2, 1), copies_join(v1, x1, 2), copies_second(c3[1], x3)])
        x4 = copy_turns(v4, 4)
        got_v = flip(out_v, 4)
        x1 = copy_swap(v1, 1)
        x3 = copy_swap(c3[0], 2)
        (vec,), (v1,), (v3,), (in_grad, down_grad) = staged(where, [
            vector_add(keep_v, got_v), copies_join(v1, x1, 1), copies_third(c3[1], x3), feed_result(h1, h2)])
        got_v = copy_turns(vec, 4)
        x3 = copy_swap(v3, 2)
        (v3,), (tiny,) = staged(where, [copies_join(v3, x3, 2), vector_add(vec, *got_v)])
        x3 = copy_swap(v3, 1)
        ((qkv_grad, out_g),) = staged(where, [project_result(v1, v3, x3, v4, x4)])
        tiny = tiny[0]
    else:
        onehot = (bucket_table[:, None] == lax.iota(jnp.int32, BUCKETS)[None, :]).astype(F32)
        distance_total = jnp.concatenate(dists)[:, ::-1].reshape(HEADS, slots)
        table_grad = jnp.dot(distance_total, onehot, precision=lax.Precision.HIGHEST, preferred_element_type=F32)
        vec = jnp.concatenate([v.reshape(n_fsdp, -1) for v in (vec_one[0], vec_one[1], vec_two[0], vec_two[1], table_grad)], axis=1)
        reduced = lambda v: lax.psum(lax.psum_scatter(v, "fsdp", scatter_dimension=0, tiled=True), "rep")
        whole = lambda s, k: jnp.stack([k, s], axis=1).reshape((8,) + s.shape[1:])
        tiny = reduced(vec)[0]
        stack = jnp.concatenate([one, two[0]], axis=1)
        in_grad = reduced(stack[:, :, :128].reshape(8, CHUNKS, 128, 8, 128).transpose(0, 2, 3, 1, 4).reshape(width, hidden))
        down_grad = reduced(stack[:, :, 128:].reshape(hidden, width))
        out_g = reduced(whole(out_send, out_keep).reshape(width, width))
        qkv_grad = reduced(jnp.stack([whole(s, k).reshape(width, 3, -1) for s, k in pieces], axis=2).reshape(width, 3 * width))
    return (outputs.reshape(inputs.shape), input_grad.reshape(inputs.shape), tiny[:n], tiny[n:2 * n], qkv_grad.astype(F32),
            tiny[4 * n:], out_g.astype(F32), tiny[2 * n:3 * n], tiny[3 * n:4 * n], in_grad.astype(F32), down_grad.astype(F32))


def solution(mesh):
    rows = P(("rep", "fsdp"), None, None)
    vec = P("fsdp")
    mat = P("fsdp", None)
    return jax.shard_map(
        functools.partial(per_device, mesh.shape["fsdp"], mesh.shape["rep"]),
        mesh=mesh,
        in_specs=(rows, P(("rep", "fsdp")), P(), vec, vec, mat, vec, mat, vec, vec, mat, mat, rows),
        out_specs=(rows, rows, vec, vec, mat, vec, mat, vec, vec, mat, mat),
        check_vma=False,
    )
```

time: 680 us -> 513 us (0.75)
  Pallas kernels: 70.5 us -> 287 us
  matrix products: 181 us -> 0 us
  waiting for transfers between devices: 250 us -> 131 us
  blocking collectives: 63.4 us -> 0 us
  starting transfers between devices: 0.36 us -> 54.4 us
  local copies, waits for them, and re-layouts: 53.4 us -> 16.5 us
  other arithmetic: 35.3 us -> 3.25 us
    pallas_call x2 -> x27, Pallas kernels: 70.5 us -> 287 us  [the longest x4 87.4 us: feed(): pl.pallas_call(functools.partial(feed_kernel, c, stacked, counts), name='...]
    dot_general x14 -> x0, matrix products: 181 us -> none  [the longest x1 48.1 us: per_device(): hidden_pre = jnp.dot(normed_two, in_full, preferred_element_type=F32)]
    reduce_scatter x4 -> x1, waiting for transfers between devices: 144 us -> 0.02 us  [per_device(): lax.psum_scatter(one.reshape(8 * 512, 1024), 'fsdp', scatter_dimension=0,...]
    ppermute x0 -> x53, waiting for transfers between devices: none -> 123 us  [the longest x35 78.7 us: flip(): return lax.ppermute(v, 'fsdp', [(i, i ^ k) for i in range(GROUPS)])]
    psum x1, waiting for transfers between devices: 66.8 us -> 7.63 us  [per_device(): h1 = lax.psum(h1, 'rep')]
    ppermute x0 -> x53, starting transfers between devices: none -> 54.2 us  [the longest x35 28.8 us: flip(): return lax.ppermute(v, 'fsdp', [(i, i ^ k) for i in range(GROUPS)])]
    unnamed x2 -> x0, blocking collectives: 50.8 us -> none
    all_gather x4 -> x2, waiting for transfers between devices: 36.8 us -> 0.04 us  [per_device(): full = lambda w: lax.all_gather(w, 'fsdp', axis=0, tiled=True)]
  transfers between devices with their start and end apart: 9 -> 57, of which waited for: 6 -> 25; matrix products, arithmetic and copies ran while one was open for 29% -> 1% of each run, Pallas kernels for 11% -> 46%
where the time goes in v2:
time: 513 us; the launch traced here: 508 us
  Pallas kernels  287 us (56%)
  waiting for transfers between devices  131 us (26%)
  starting transfers between devices  54.4 us (11%)
  local copies, waits for them, and re-layouts  16.5 us (3%)
  between operations  15.3 us (3%)
    pallas_call x4, Pallas kernels, feed(): pl.pallas_call(functools.partial(feed_kernel, c, stacked, counts), name='...  87.4 us
    ppermute x35, waiting for transfers between devices, flip(): return lax.ppermute(v, 'fsdp', [(i, i ^ k) for i in range(GROUPS)])  78.7 us
    pallas_call x11, Pallas kernels, staged(): pl.pallas_call(functools.partial(staged_kernel, steps, len(arrays), len(d...  56.1 us
    pallas_call x4, Pallas kernels, attend_back(): pl.pallas_call(with_deps(attend_back_kernel, 9, len(deps)), name='attend_...  44.1 us
    ppermute x12, waiting for transfers between devices, copy_swap(): return lax.ppermute(v, 'rep', [(i, i ^ k) for i in range(4)])  35.6 us
    pallas_call x1, Pallas kernels, attend(): pl.pallas_call(attend_kernel, name='attend', grid_spec=pltpu.PrefetchScal...  34.7 us
    ppermute x35, starting transfers between devices, flip(): return lax.ppermute(v, 'fsdp', [(i, i ^ k) for i in range(GROUPS)])  28.8 us
    ppermute x12, starting transfers between devices, copy_swap(): return lax.ppermute(v, 'rep', [(i, i ^ k) for i in range(4)])  17.7 us
  transfers between devices with their start and end apart: 57, of which 25 were waited for; matrix products, arithmetic and copies ran while one was open for 1% of the time, Pallas kernels for 46%

profile of v2, /device:TPU:0, one launch (start us, length us, event | category | flops | bytes accessed | tf_op | source)
XLA Modules:
  0.0 507.6 jit_solution(838462182983283389)
XLA Ops:
  7.2 2.3 lead.1
  9.6 3.0 collective-permute-start.4
  12.5 1.5 collective-permute-start.3
  16.7 20.7 %collective-permute-done.1 = bf16[2,576]{1,0:T(2,128)(2,1)S(1)} collective-permute-done((bf16[2,576]{1,0:T(2,128)(2,1)S(1)}, bf16[2,576]{1,0:T(2,128)(2,1)S(1)}, u32[]{:S(2)}, u32[]{:S(2)}) %collective-permute-start.1) | collective-permute-done | bytes 2336 | tf_op jit(solution)/shard_map/ppermute | solution.py:598
  39.1 2.7 collective-permute-done.2
  44.4 6.0 %prepare.1 = (bf16[1024,1024]{1,0:T(8,128)(2,1)}, bf16[1024,1024]{1,0:T(8,128)(2,1)}, f32[4,1024]{1,0:T(4,128)}, f32[16,4,256]{2,1,0:T(4,128)}) custom-call(s32[1]{0:T(128)} %bitcast.refs_0_.me_ref, s32[1]{0:T(128)S(6)} %copy.31.refs_1_.len_ref, bf16[1024,1024]{1,0:T(8,128)(2,1)} %bitcast.44, bf16[1024,1024]{1,0:T(8,128)(2,1)} %bitcast.63, ...), custom_call_target="tpu_custom_call" | custom-call | flops 1000000000 | bytes 8000000 | tf_op jit(solution)/shard_map/prepare/pallas_call | solution.py:107
  50.4 3.2 pack.1
  54.5 1.6 collective-permute-start.6
  57.2 16.6 %collective-permute-done.6.refs_4_.refs_9_.refs_10_.refs_11_ = bf16[64,4096]{1,0:T(8,128)(2,1)S(1)} collective-permute-done((bf16[64,4096]{1,0:T(8,128)(2,1)S(1)}, bf16[64,4096]{1,0:T(8,128)(2,1)S(1)}, u32[]{:S(2)}, u32[]{:S(2)}) %collective-permute-start.6) | collective-permute-done | bytes 524320 | tf_op jit(solution)/shard_map/ppermute | solution.py:598
  73.8 2.2 collective-permute-done.5.refs_3_.refs_8_.refs_9_.refs_10_
  79.5 12.0 %project.1.q_ref.k_ref.v_ref.refs_3_.refs_4_.refs_5_ = bf16[48,64,1024]{2,1,0:T(8,128)(2,1)} custom-call(bf16[1024,1024]{1,0:T(8,128)(2,1)} %get-tuple-element.130.n1t_ref.refs_4_.refs_0_, bf16[128,4096]{1,0:T(8,128)(2,1)} %get-tuple-element.128.refs_0_.refs_5_.refs_6_.refs_7_, bf16[128,4096]{1,0:T(8,128)(2,1)} %copy-done.2, bf16[128,4096]{1,0:T(8,128)(2,1)} %copy-done, ...), custom_call_target="tpu_custom_call" | custom-call | flops 6442450944 | bytes 14000000 | tf_op jit(solution)/shard_map/project/pallas_call | solution.py:166
  91.5 34.7 %attend.1 = (bf16[16,64,1024]{2,1,0:T(8,128)(2,1)}, f32[16,1,1024]{2,1,0:T(1,128)}) custom-call(s32[1]{0:T(128)} %bitcast.refs_0_.me_ref, s32[1]{0:T(128)S(6)} %copy.31.refs_1_.len_ref, f32[16,4,256]{2,1,0:T(4,128)} %get-tuple-element.129.base_ref.refs_2_, bf16[48,64,1024]{2,1,0:T(8,128)(2,1)} %project.1.q_ref.k_ref.v_ref.refs_3_.refs_4_.refs_5_, ...), custom_call_target="tpu_custom_call" | custom-call | flops 30000001024 | bytes 10000000 | tf_op jit(solution)/shard_map/attend/pallas_call | solution.py:222
  126.2 9.5 %middle.1 = (f32[1024,1024]{1,0:T(8,128)}, bf16[1024,1024]{1,0:T(8,128)(2,1)}, bf16[1024,1024]{1,0:T(8,128)(2,1)}) custom-call(s32[1]{0:T(128)} %bitcast.refs_0_.me_ref, bf16[1024,1024]{1,0:T(8,128)(2,1)} %bitcast.48, bf16[1024,1024]{1,0:T(8,128)(2,1)} %bitcast.45, f32[1,1024]{1,0:T(1,128)} %get-tuple-element.245.refs_3_.refs_5_, ...), custom_call_target="tpu_custom_call" | custom-call | flops 2147483648 | bytes 14000000 | tf_op jit(solution)/shard_map/middle/pallas_call | solution.py:328
  135.7 21.4 %feed.4 = (f32[1024,1024]{1,0:T(8,128)}, f32[1024,1024]{1,0:T(8,128)}, bf16[8,2,256,1024]{3,2,1,0:T(8,128)(2,1)}) custom-call(s32[1]{0:T(128)} %bitcast.refs_0_.me_ref, bf16[1024,1024]{1,0:T(8,128)(2,1)} %get-tuple-element.134.n2_h, bf16[1024,1024]{1,0:T(8,128)(2,1)} %get-tuple-element.135.n2t_h, bf16[1024,1024]{1,0:T(8,128)(2,1)} %get-tuple-element.136.og_h.refs_3_, ...), custom_call_target="tpu_custom_call" | custom-call | flops 20000000000 | bytes 30000000 | tf_op jit(solution)/shard_map/feed/pallas_call | solution.py:414
  157.2 21.6 %feed.5 = (f32[1024,1024]{1,0:T(8,128)}, f32[1024,1024]{1,0:T(8,128)}, bf16[8,2,256,1024]{3,2,1,0:T(8,128)(2,1)}) custom-call(s32[1]{0:T(128)} %bitcast.refs_0_.me_ref, bf16[1024,1024]{1,0:T(8,128)(2,1)} %get-tuple-element.134.n2_h, bf16[1024,1024]{1,0:T(8,128)(2,1)} %get-tuple-element.135.n2t_h, ...), custom_call_target="tpu_custom_call", output_to_operand_aliasing={{2}: (7, {})} | custom-call | flops 20000000000 | bytes 30000000 | tf_op jit(solution)/shard_map/feed/pallas_call | solution.py:414
  178.8 22.3 %feed.6 = (f32[1024,1024]{1,0:T(8,128)}, f32[1024,1024]{1,0:T(8,128)}, bf16[4,2,256,1024]{3,2,1,0:T(8,128)(2,1)}, bf16[4,2,256,1024]{3,2,1,0:T(8,128)(2,1)}) custom-call(s32[1]{0:T(128)} %bitcast.refs_0_.me_ref, bf16[1024,1024]{1,0:T(8,128)(2,1)} %get-tuple-element.134.n2_h, bf16[1024,1024]{1,0:T(8,128)(2,1)} %get-tuple-element.135.n2t_h, ...), custom_call_target="tpu_custom_call" | custom-call | flops 20000000000 | bytes 30000000 | tf_op jit(solution)/shard_map/feed/pallas_call | solution.py:414
  201.1 22.1 %feed.7 = (f32[1024,1024]{1,0:T(8,128)}, f32[1024,1024]{1,0:T(8,128)}, bf16[4,2,256,1024]{3,2,1,0:T(8,128)(2,1)}, bf16[4,2,256,1024]{3,2,1,0:T(8,128)(2,1)}) custom-call(s32[1]{0:T(128)} %bitcast.refs_0_.me_ref, bf16[1024,1024]{1,0:T(8,128)(2,1)} %get-tuple-element.134.n2_h, ...), custom_call_target="tpu_custom_call", output_to_operand_aliasing={{2}: (7, {}), {3}: (8, {})} | custom-call | flops 20000000000 | bytes 30000000 | tf_op jit(solution)/shard_map/feed/pallas_call | solution.py:414
  224.4 14.7 %middle_back.1 = (f32[1024,1024]{1,0:T(8,128)}, bf16[1024,1024]{1,0:T(8,128)(2,1)}, bf16[4,128,1024]{2,1,0:T(8,128)(2,1)}, bf16[4,128,1024]{2,1,0:T(8,128)(2,1)}, f32[2,1024]{1,0:T(2,128)}) custom-call(s32[1]{0:T(128)} %bitcast.refs_0_.me_ref, f32[1024,1024]{1,0:T(8,128)} %get-tuple-element.133.refs_1_.refs_3_, f32[1024,1024]{1,0:T(8,128)} %get-tuple-element.149.refs_2_, ...), custom_call_target="tpu_custom_call" | custom-call | flops 4294967296 | bytes 24000000 | tf_op jit(solution)/shard_map/middle_back/pallas_call | solution.py:469
  239.1 6.6 %staged.11 = (bf16[2,256,1024]{2,1,0:T(8,128)(2,1)}, bf16[2,256,1024]{2,1,0:T(8,128)(2,1)}, bf16[2,256,1024]{2,1,0:T(8,128)(2,1)}, bf16[2,256,1024]{2,1,0:T(8,128)(2,1)}) custom-call(s32[3]{0:T(128)} %pad_add_fusion.where_ref, bf16[4,512,1024]{2,1,0:T(8,128)(2,1)} %bitcast.50, bf16[4,512,1024]{2,1,0:T(8,128)(2,1)} %collective-permute-done.12.refs_1_, ...), custom_call_target="tpu_custom_call" | custom-call | flops 3000000000 | bytes 10000000 | tf_op jit(solution)/shard_map/staged/pallas_call | solution.py:512
  245.7 10.9 %attend_back.4 = (bf16[4,64,1024]{2,1,0:T(8,128)(2,1)}, bf16[4,64,1024]{2,1,0:T(8,128)(2,1)}, bf16[4,64,1024]{2,1,0:T(8,128)(2,1)}, f32[4,4,256]{2,1,0:T(4,128)}) custom-call(s32[1]{0:T(128)} %bitcast.refs_0_.me_ref, s32[1]{0:T(128)S(6)} %copy.31.refs_1_.len_ref, f32[16,4,256]{2,1,0:T(4,128)} %get-tuple-element.129.base_ref.refs_2_, ...), custom_call_target="tpu_custom_call" | custom-call | flops 9600000000 | bytes 4800000 | tf_op jit(solution)/shard_map/attend_back/pallas_call | solution.py:295
  256.6 7.1 %staged.12 = (bf16[4,128,1792]{2,1,0:T(8,128)(2,1)}, bf16[4,128,1792]{2,1,0:T(8,128)(2,1)}) custom-call(s32[3]{0:T(128)} %pad_add_fusion.where_ref, bf16[1024,1024]{1,0:T(8,128)(2,1)} %get-tuple-element.130.n1t_ref.refs_4_.refs_0_, bf16[256,1024]{1,0:T(8,128)(2,1)} %bitcast.66, bf16[256,1024]{1,0:T(8,128)(2,1)} %bitcast.68, bf16[256,1024]{1,0:T(8,128)(2,1)} %bitcast.70, ...), custom_call_target="tpu_custom_call" | custom-call | flops 3000000000 | bytes 10000000 | tf_op jit(solution)/shard_map/staged/pallas_call | solution.py:512
  264.0 11.2 %attend_back.5 = (bf16[4,64,1024]{2,1,0:T(8,128)(2,1)}, bf16[4,64,1024]{2,1,0:T(8,128)(2,1)}, bf16[4,64,1024]{2,1,0:T(8,128)(2,1)}, f32[4,4,256]{2,1,0:T(4,128)}) custom-call(s32[1]{0:T(128)} %bitcast.refs_0_.me_ref, s32[1]{0:T(128)S(6)} %copy.31.refs_1_.len_ref, f32[16,4,256]{2,1,0:T(4,128)} %get-tuple-element.129.base_ref.refs_2_, ...), custom_call_target="tpu_custom_call" | custom-call | flops 9600000000 | bytes 4800000 | tf_op jit(solution)/shard_map/attend_back/pallas_call | solution.py:295
  275.2 14.5 %collective-permute-done.13.refs_5_.refs_7_ = bf16[2,256,1024]{2,1,0:T(8,128)(2,1)S(1)} collective-permute-done((bf16[2,256,1024]{2,1,0:T(8,128)(2,1)}, bf16[2,256,1024]{2,1,0:T(8,128)(2,1)S(1)}, u32[]{:S(2)}, u32[]{:S(2)}) %collective-permute-start.13) | collective-permute-done | bytes 1048608 | tf_op jit(solution)/shard_map/ppermute | solution.py:598
  291.5 6.7 %staged.13 = (bf16[4,128,768]{2,1,0:T(8,128)(2,1)}, bf16[4,128,768]{2,1,0:T(8,128)(2,1)}, bf16[256,1024]{1,0:T(8,128)(2,1)}, bf16[256,1024]{1,0:T(8,128)(2,1)}, ...) custom-call(s32[3]{0:T(128)} %pad_add_fusion.where_ref, ...), custom_call_target="tpu_custom_call" | custom-call | flops 3000000000 | bytes 10000000 | tf_op jit(solution)/shard_map/staged/pallas_call | solution.py:512
  298.3 1.5 collective-permute-start.18
  300.0 1.7 collective-permute-start.16
  302.4 10.9 %attend_back.6 = (bf16[4,64,1024]{2,1,0:T(8,128)(2,1)}, bf16[4,64,1024]{2,1,0:T(8,128)(2,1)}, bf16[4,64,1024]{2,1,0:T(8,128)(2,1)}, f32[4,4,256]{2,1,0:T(4,128)}) custom-call(s32[1]{0:T(128)} %bitcast.refs_0_.me_ref, s32[1]{0:T(128)S(6)} %copy.31.refs_1_.len_ref, f32[16,4,256]{2,1,0:T(4,128)} %get-tuple-element.129.base_ref.refs_2_, ...), custom_call_target="tpu_custom_call" | custom-call | flops 9600000000 | bytes 4800000 | tf_op jit(solution)/shard_map/attend_back/pallas_call | solution.py:295
  313.4 9.3 %collective-permute-done.16.refs_8_ = bf16[256,1024]{1,0:T(8,128)(2,1)S(1)} collective-permute-done((bf16[256,1024]{1,0:T(8,128)(2,1)}, bf16[256,1024]{1,0:T(8,128)(2,1)S(1)}, u32[]{:S(2)}, u32[]{:S(2)}) %collective-permute-start.16) | collective-permute-done | bytes 524320 | tf_op jit(solution)/shard_map/ppermute | solution.py:598
  323.7 7.3 %staged.14 = (bf16[4,128,1536]{2,1,0:T(8,128)(2,1)}, bf16[4,128,1536]{2,1,0:T(8,128)(2,1)}, bf16[256,1024]{1,0:T(8,128)(2,1)}, bf16[256,1024]{1,0:T(8,128)(2,1)}...) custom-call(s32[3]{0:T(128)} %pad_add_fusion.where_ref, ...), custom_call_target="tpu_custom_call" | custom-call | flops 3000000000 | bytes 10000000 | tf_op jit(solution)/shard_map/staged/pallas_call | solution.py:512
  332.4 1.7 collective-permute-start.20
  334.1 11.1 %attend_back.7 = (bf16[4,64,1024]{2,1,0:T(8,128)(2,1)}, bf16[4,64,1024]{2,1,0:T(8,128)(2,1)}, bf16[4,64,1024]{2,1,0:T(8,128)(2,1)}, f32[4,4,256]{2,1,0:T(4,128)}) custom-call(s32[1]{0:T(128)} %bitcast.refs_0_.me_ref, s32[1]{0:T(128)S(6)} %copy.31.refs_1_.len_ref, f32[16,4,256]{2,1,0:T(4,128)} %get-tuple-element.129.base_ref.refs_2_, ...), custom_call_target="tpu_custom_call" | custom-call | flops 9600000000 | bytes 4800000 | tf_op jit(solution)/shard_map/attend_back/pallas_call | solution.py:295
  345.3 16.6 %collective-permute-done.20.refs_5_ = bf16[256,1024]{1,0:T(8,128)(2,1)S(1)} collective-permute-done((bf16[256,1024]{1,0:T(8,128)(2,1)}, bf16[256,1024]{1,0:T(8,128)(2,1)S(1)}, u32[]{:S(2)}, u32[]{:S(2)}) %collective-permute-start.20) | collective-permute-done | bytes 524320 | tf_op jit(solution)/shard_map/ppermute | solution.py:761
  363.2 6.7 %staged.15 = (bf16[4,128,768]{2,1,0:T(8,128)(2,1)}, bf16[4,128,768]{2,1,0:T(8,128)(2,1)}, bf16[128,1024]{1,0:T(8,128)(2,1)}, bf16[128,1024]{1,0:T(8,128)(2,1)}, ...) custom-call(s32[3]{0:T(128)} %pad_add_fusion.where_ref, ...), custom_call_target="tpu_custom_call" | custom-call | flops 3000000000 | bytes 10000000 | tf_op jit(solution)/shard_map/staged/pallas_call | solution.py:512
  370.0 6.1 %collective-permute-start.25 = (bf16[128,1024]{1,0:T(8,128)(2,1)}, bf16[128,1024]{1,0:T(8,128)(2,1)S(1)}, u32[]{:S(2)}, u32[]{:S(2)}) collective-permute-start(bf16[128,1024]{1,0:T(8,128)(2,1)} %get-tuple-element.201), channel_id=1, source_target_pairs={{0,16},{8,24},{16,0},{24,8},{1,17},{9,25},{17,1},{25,9},{2,18},{10... | collective-permute-start | bytes 786440 | tf_op jit(solution)/shard_map/ppermute | solution.py:761
  377.4 1.4 collective-permute-start.28
  378.8 16.9 %finish.1 = (bf16[1024,1024]{1,0:T(8,128)(2,1)}, f32[1024,1024]{1,0:T(8,128)}, f32[2,1024]{1,0:T(2,128)}) custom-call(s32[1]{0:T(128)} %bitcast.refs_0_.me_ref, s32[1]{0:T(128)S(6)} %copy.31.refs_1_.len_ref, bf16[1024,1024]{1,0:T(8,128)(2,1)} %bitcast.46, f32[1024,1024]{1,0:T(8,128)} %get-tuple-element.133.refs_1_.refs_3_, ...), custom_call_target="tpu_custom_call" | custom-call | flops 6442450944 | bytes 34000000 | tf_op jit(solution)/shard_map/finish/pallas_call | solution.py:585
  395.7 7.6 %all-reduce.2.cloned.1.call-done.refs_17_.refs_6_ = bf16[512,1024]{1,0:T(8,128)(2,1)} async-done(((bf16[512,1024]{1,0:T(8,128)(2,1)}), bf16[512,1024]{1,0:T(8,128)(2,1)}) %all-reduce.2.cloned.1.call-update) | async-done | bytes 1048592 | tf_op jit(solution)/shard_map/psum | solution.py:836
  404.7 3.7 staged.16
  409.1 2.3 collective-permute-start.32
  411.4 1.5 collective-permute-start.30
  412.9 1.5 collective-permute-start.31
  414.9 7.1 %collective-permute-done.33.refs_9_ = bf16[32,1792]{1,0:T(8,128)(2,1)S(1)} collective-permute-done((bf16[32,1792]{1,0:T(8,128)(2,1)}, bf16[32,1792]{1,0:T(8,128)(2,1)S(1)}, u32[]{:S(2)}, u32[]{:S(2)}) %collective-permute-start.33) | collective-permute-done | bytes 114720 | tf_op jit(solution)/shard_map/ppermute | solution.py:761
  422.0 1.5 collective-permute-start.35
  424.3 4.5 collective-permute-done.35.refs_15_
  429.6 3.4 staged.17
  433.1 2.0 collective-permute-start.41
  435.7 1.7 collective-permute-start.36
  437.4 1.4 collective-permute-start.37
  439.5 1.7 collective-permute-start.38
  442.3 2.1 collective-permute-done.38.refs_7_
  444.4 6.3 %collective-permute-done.40.refs_11_ = bf16[32,1792]{1,0:T(8,128)(2,1)S(1)} collective-permute-done((bf16[32,1792]{1,0:T(8,128)(2,1)}, bf16[32,1792]{1,0:T(8,128)(2,1)S(1)}, u32[]{:S(2)}, u32[]{:S(2)}) %collective-permute-start.40) | collective-permute-done | bytes 114720 | tf_op jit(solution)/shard_map/ppermute | solution.py:761
  450.6 2.1 collective-permute-done.41.refs_13_
  453.6 3.5 staged.18
  457.8 1.7 collective-permute-start.44
  459.5 1.8 collective-permute-start.42
  461.3 2.0 collective-permute-done.42.refs_1_
  465.7 5.1 staged.19
  472.1 2.3 collective-permute-start.48
  475.8 2.5 collective-permute-start.52
  479.4 1.4 collective-permute-done.47.refs_4_
  482.6 2.4 staged.20
  487.7 7.0 %collective-permute-done.51.refs_5_ = bf16[128,768]{1,0:T(8,128)(2,1)S(1)} collective-permute-done((bf16[128,768]{1,0:T(8,128)(2,1)S(1)}, bf16[128,768]{1,0:T(8,128)(2,1)S(1)}, u32[]{:S(2)}, u32[]{:S(2)}) %collective-permute-start.51) | collective-permute-done | bytes 196640 | tf_op jit(solution)/shard_map/ppermute | solution.py:765
  494.6 1.9 collective-permute-done.49.refs_2_
  497.2 3.6 staged.21
  (196 shorter events, 40.5 us)
Async XLA Ops:
  7.2 128.6 %all-gather.5.cloned.1.call-start = ((), (), s32[]{:S(2)}) async-start(), calls=%async_computation.2 | async-start | bytes 9437184 | tf_op jit(solution)/shard_map/all_gather | solution.py:781
  9.6 33.5 %collective-permute-start.4 = (bf16[128,4096]{1,0:T(8,128)(2,1)}, bf16[128,4096]{1,0:T(8,128)(2,1)S(1)}, u32[]{:S(2)}, u32[]{:S(2)}) collective-permute-start(bf16[128,4096]{1,0:T(8,128)(2,1)} %get-tuple-element.128.refs_0_.refs_5_.refs_6_.refs_7_), channel_id=1, source_target_pairs={{0,4},{1,5},{2,6},{3,7},{4,0},{5,1},{6,2},{7,3},{8,12},{9,13},{10,... | collective-permute-start | bytes 3145736 | tf_op jit(solution)/shard_map/ppermute | solution.py:598
  12.5 30.6 %collective-permute-start.3 = (bf16[128,4096]{1,0:T(8,128)(2,1)}, bf16[128,4096]{1,0:T(8,128)(2,1)S(1)}, u32[]{:S(2)}, u32[]{:S(2)}) collective-permute-start(bf16[128,4096]{1,0:T(8,128)(2,1)} %get-tuple-element.128.refs_0_.refs_5_.refs_6_.refs_7_), channel_id=1, source_target_pairs={{0,2},{1,3},{2,0},{3,1},{4,6},{5,7},{6,4},{7,5},{8,10},{9,11},{10,... | collective-permute-start | bytes 3145736 | tf_op jit(solution)/shard_map/ppermute | solution.py:598
  14.0 1.4 collective-permute-start
  16.1 21.3 %collective-permute-start.1 = (bf16[2,576]{1,0:T(2,128)(2,1)S(1)}, bf16[2,576]{1,0:T(2,128)(2,1)S(1)}, u32[]{:S(2)}, u32[]{:S(2)}) collective-permute-start(bf16[2,576]{1,0:T(2,128)(2,1)S(1)} %pad_maximum_fusion.2), channel_id=1, source_target_pairs={{0,2},{1,3},{2,0},{3,1},{4,6},{5,7},{6,4},{7,5},{8,10},{9,11},{10,... | collective-permute-start | bytes 6920 | tf_op jit(solution)/shard_map/ppermute | solution.py:598
  38.1 3.7 collective-permute-start.2
  50.4 25.6 %copy-start.18 = (f32[4,1024]{1,0:T(4,128)S(1)}, f32[4,1024]{1,0:T(4,128)}, u32[]{:S(2)}) copy-start(f32[4,1024]{1,0:T(4,128)} %get-tuple-element.132) | copy-start | bytes 49156
  53.6 125.2 %all-gather.3.cloned.1.call-start = ((), (), s32[]{:S(2)}) async-start(), calls=%async_computation.1 | async-start | bytes 9437184 | tf_op jit(solution)/shard_map/all_gather | solution.py:781
  54.4 202.3 %reduce-scatter.2.cloned.1.call-start = ((), (), s32[]{:S(2)}) async-start(), calls=%async_computation.3 | async-start | bytes 9437184 | tf_op jit(solution)/shard_map/reduce_scatter | solution.py:829
  54.4 22.3 %collective-permute-start.7 = (bf16[128,4096]{1,0:T(8,128)(2,1)S(1)}, bf16[128,4096]{1,0:T(8,128)(2,1)S(1)}, u32[]{:S(2)}, u32[]{:S(2)}) collective-permute-start(bf16[128,4096]{1,0:T(8,128)(2,1)S(1)} %copy-done.4), channel_id=1, source_target_pairs={{0,1},{1,0},{2,3},{3,2},{4,5},{5,4},{6,7},{7,6},{8,9},{9,8},{10,11... | collective-permute-start | bytes 3145736 | tf_op jit(solution)/shard_map/ppermute | solution.py:598
  54.5 19.2 %collective-permute-start.6 = (bf16[64,4096]{1,0:T(8,128)(2,1)S(1)}, bf16[64,4096]{1,0:T(8,128)(2,1)S(1)}, u32[]{:S(2)}, u32[]{:S(2)}) collective-permute-start(bf16[64,4096]{1,0:T(8,128)(2,1)S(1)} %slice.61), channel_id=1, source_target_pairs={{0,2},{1,3},{2,0},{3,1},{4,6},{5,7},{6,4},{7,5},{8,10},{9,11},{10,... | collective-permute-start | bytes 1572872 | tf_op jit(solution)/shard_map/ppermute | solution.py:598
  56.1 19.9 %collective-permute-start.5 = (bf16[64,4096]{1,0:T(8,128)(2,1)S(1)}, bf16[64,4096]{1,0:T(8,128)(2,1)S(1)}, u32[]{:S(2)}, u32[]{:S(2)}) collective-permute-start(bf16[64,4096]{1,0:T(8,128)(2,1)S(1)} %slice.60), channel_id=1, source_target_pairs={{0,4},{1,5},{2,6},{3,7},{4,0},{5,1},{6,2},{7,3},{8,12},{9,13},{10,... | collective-permute-start | bytes 1572872 | tf_op jit(solution)/shard_map/ppermute | solution.py:598
  56.7 20.0 %collective-permute-start.9 = (bf16[128,4096]{1,0:T(8,128)(2,1)S(1)}, bf16[128,4096]{1,0:T(8,128)(2,1)S(1)}, u32[]{:S(2)}, u32[]{:S(2)}) collective-permute-start(bf16[128,4096]{1,0:T(8,128)(2,1)S(1)} %copy-done.1), channel_id=1, source_target_pairs={{0,1},{1,0},{2,3},{3,2},{4,5},{5,4},{6,7},{7,6},{8,9},{9,8},{10,11... | collective-permute-start | bytes 3145736 | tf_op jit(solution)/shard_map/ppermute | solution.py:598
  56.7 22.7 %collective-permute-start.8 = (bf16[128,4096]{1,0:T(8,128)(2,1)S(1)}, bf16[128,4096]{1,0:T(8,128)(2,1)}, u32[]{:S(2)}, u32[]{:S(2)}) collective-permute-start(bf16[128,4096]{1,0:T(8,128)(2,1)S(1)} %copy-done.3), channel_id=1, source_target_pairs={{0,1},{1,0},{2,3},{3,2},{4,5},{5,4},{6,7},{7,6},{8,9},{9,8},{10,11... | collective-permute-start | bytes 3145736 | tf_op jit(solution)/shard_map/ppermute | solution.py:598
  73.8 2.9 collective-permute-start.11
  76.0 1.9 collective-permute-start.10
  223.3 15.8 %collective-permute-start.12 = (bf16[4,512,1024]{2,1,0:T(8,128)(2,1)}, bf16[4,512,1024]{2,1,0:T(8,128)(2,1)}, u32[]{:S(2)}, u32[]{:S(2)}) collective-permute-start(bf16[4,512,1024]{2,1,0:T(8,128)(2,1)} %bitcast.90), channel_id=1, source_target_pairs={{0,1},{1,0},{2,3},{3,2},{4,5},{5,4},{6,7},{7,6},{8,9},{9,8},{10,11... | collective-permute-start | bytes 12582920 | tf_op jit(solution)/shard_map/ppermute | solution.py:598
  263.7 139.7 %all-reduce.2.cloned.1.call-start = ((), (), s32[]{:S(2)}) async-start(), calls=%async_computation.4 | async-start | bytes 2097152 | tf_op jit(solution)/shard_map/psum | solution.py:836
  263.8 25.9 %collective-permute-start.15 = (bf16[4,128,1792]{2,1,0:T(8,128)(2,1)}, bf16[4,128,1792]{2,1,0:T(8,128)(2,1)S(1)}, u32[]{:S(2)}, u32[]{:S(2)}) collective-permute-start(bf16[4,128,1792]{2,1,0:T(8,128)(2,1)} %get-tuple-element.165.refs_9_), channel_id=1, source_target_pairs={{0,1},{1,0},{2,3},{3,2},{4,5},{5,4},{6,7},{7,6},{8,9},{9,8},{10,11... | collective-permute-start | bytes 5505032 | tf_op jit(solution)/shard_map/ppermute | solution.py:598
  263.8 25.8 %collective-permute-start.13 = (bf16[2,256,1024]{2,1,0:T(8,128)(2,1)}, bf16[2,256,1024]{2,1,0:T(8,128)(2,1)S(1)}, u32[]{:S(2)}, u32[]{:S(2)}) collective-permute-start(bf16[2,256,1024]{2,1,0:T(8,128)(2,1)} %get-tuple-element.155.refs_9_), channel_id=1, source_target_pairs={{0,2},{1,3},{2,0},{3,1},{4,6},{5,7},{6,4},{7,5},{8,10},{9,11},{10,... | collective-permute-start | bytes 3145736 | tf_op jit(solution)/shard_map/ppermute | solution.py:598
  263.9 25.7 %collective-permute-start.14 = (bf16[2,256,1024]{2,1,0:T(8,128)(2,1)}, bf16[2,256,1024]{2,1,0:T(8,128)(2,1)S(1)}, u32[]{:S(2)}, u32[]{:S(2)}) collective-permute-start(bf16[2,256,1024]{2,1,0:T(8,128)(2,1)} %get-tuple-element.156.refs_10_), channel_id=1, source_target_pairs={{0,4},{1,5},{2,6},{3,7},{4,0},{5,1},{6,2},{7,3},{8,12},{9,13},{10,... | collective-permute-start | bytes 3145736 | tf_op jit(solution)/shard_map/ppermute | solution.py:598
  298.3 15.0 %collective-permute-start.18 = (bf16[2,64,1792]{2,1,0:T(8,128)(2,1)}, bf16[2,64,1792]{2,1,0:T(8,128)(2,1)S(1)}, u32[]{:S(2)}, u32[]{:S(2)}) collective-permute-start(bf16[2,64,1792]{2,1,0:T(8,128)(2,1)} %get-tuple-element.170.refs_9_), channel_id=1, source_target_pairs={{0,2},{1,3},{2,0},{3,1},{4,6},{5,7},{6,4},{7,5},{8,10},{9,11},{10,... | collective-permute-start | bytes 1376264 | tf_op jit(solution)/shard_map/ppermute | solution.py:598
  299.7 13.7 %collective-permute-start.19 = (bf16[2,64,1792]{2,1,0:T(8,128)(2,1)}, bf16[2,64,1792]{2,1,0:T(8,128)(2,1)S(1)}, u32[]{:S(2)}, u32[]{:S(2)}) collective-permute-start(bf16[2,64,1792]{2,1,0:T(8,128)(2,1)} %get-tuple-element.171.refs_10_), channel_id=1, source_target_pairs={{0,4},{1,5},{2,6},{3,7},{4,0},{5,1},{6,2},{7,3},{8,12},{9,13},{10,... | collective-permute-start | bytes 1376264 | tf_op jit(solution)/shard_map/ppermute | solution.py:598
  300.0 22.6 %collective-permute-start.16 = (bf16[256,1024]{1,0:T(8,128)(2,1)}, bf16[256,1024]{1,0:T(8,128)(2,1)S(1)}, u32[]{:S(2)}, u32[]{:S(2)}) collective-permute-start(bf16[256,1024]{1,0:T(8,128)(2,1)} %get-tuple-element.179), channel_id=1, source_target_pairs={{0,4},{1,5},{2,6},{3,7},{4,0},{5,1},{6,2},{7,3},{8,12},{9,13},{10,... | collective-permute-start | bytes 1572872 | tf_op jit(solution)/shard_map/ppermute | solution.py:598
  301.8 20.9 %collective-permute-start.17 = (bf16[256,1024]{1,0:T(8,128)(2,1)}, bf16[256,1024]{1,0:T(8,128)(2,1)S(1)}, u32[]{:S(2)}, u32[]{:S(2)}) collective-permute-start(bf16[256,1024]{1,0:T(8,128)(2,1)} %get-tuple-element.180), channel_id=1, source_target_pairs={{0,2},{1,3},{2,0},{3,1},{4,6},{5,7},{6,4},{7,5},{8,10},{9,11},{10,... | collective-permute-start | bytes 1572872 | tf_op jit(solution)/shard_map/ppermute | solution.py:598
  331.0 30.9 %collective-permute-start.23 = (bf16[4,128,1536]{2,1,0:T(8,128)(2,1)}, bf16[4,128,1536]{2,1,0:T(8,128)(2,1)S(1)}, u32[]{:S(2)}, u32[]{:S(2)}) collective-permute-start(bf16[4,128,1536]{2,1,0:T(8,128)(2,1)} %get-tuple-element.181.refs_9_), channel_id=1, source_target_pairs={{0,1},{1,0},{2,3},{3,2},{4,5},{5,4},{6,7},{7,6},{8,9},{9,8},{10,11... | collective-permute-start | bytes 4718600 | tf_op jit(solution)/shard_map/ppermute | solution.py:598
  331.1 14.1 %collective-permute-start.21 = (bf16[64,1792]{1,0:T(8,128)(2,1)}, bf16[64,1792]{1,0:T(8,128)(2,1)S(1)}, u32[]{:S(2)}, u32[]{:S(2)}) collective-permute-start(bf16[64,1792]{1,0:T(8,128)(2,1)} %get-tuple-element.187), channel_id=1, source_target_pairs={{0,4},{1,5},{2,6},{3,7},{4,0},{5,1},{6,2},{7,3},{8,12},{9,13},{10,... | collective-permute-start | bytes 688136 | tf_op jit(solution)/shard_map/ppermute | solution.py:598
  331.8 13.5 %collective-permute-start.22 = (bf16[64,1792]{1,0:T(8,128)(2,1)}, bf16[64,1792]{1,0:T(8,128)(2,1)S(1)}, u32[]{:S(2)}, u32[]{:S(2)}) collective-permute-start(bf16[64,1792]{1,0:T(8,128)(2,1)} %get-tuple-element.188), channel_id=1, source_target_pairs={{0,2},{1,3},{2,0},{3,1},{4,6},{5,7},{6,4},{7,5},{8,10},{9,11},{10,... | collective-permute-start | bytes 688136 | tf_op jit(solution)/shard_map/ppermute | solution.py:598
  332.4 29.5 %collective-permute-start.20 = (bf16[256,1024]{1,0:T(8,128)(2,1)}, bf16[256,1024]{1,0:T(8,128)(2,1)S(1)}, u32[]{:S(2)}, u32[]{:S(2)}) collective-permute-start(bf16[256,1024]{1,0:T(8,128)(2,1)} %get-tuple-element.186), channel_id=1, source_target_pairs={{0,8},{8,0},{16,24},{24,16},{1,9},{9,1},{17,25},{25,17},{2,10},{10... | collective-permute-start | bytes 1572872 | tf_op jit(solution)/shard_map/ppermute | solution.py:761
  345.2 16.6 %copy-start.28 = (bf16[64,1792]{1,0:T(8,128)(2,1)}, bf16[64,1792]{1,0:T(8,128)(2,1)S(1)}, u32[]{:S(2)}) copy-start(bf16[64,1792]{1,0:T(8,128)(2,1)S(1)} %collective-permute-done.21.refs_8_) | copy-start | bytes 688132
  345.3 16.6 %copy-start.29 = (bf16[64,1792]{1,0:T(8,128)(2,1)}, bf16[64,1792]{1,0:T(8,128)(2,1)S(1)}, u32[]{:S(2)}) copy-start(bf16[64,1792]{1,0:T(8,128)(2,1)S(1)} %collective-permute-done.22.refs_11_) | copy-start | bytes 688132
  369.9 33.6 %collective-permute-start.24 = (bf16[4,128,768]{2,1,0:T(8,128)(2,1)}, bf16[4,128,768]{2,1,0:T(8,128)(2,1)S(1)}, u32[]{:S(2)}, u32[]{:S(2)}) collective-permute-start(bf16[4,128,768]{2,1,0:T(8,128)(2,1)} %get-tuple-element.190.refs_29_), channel_id=1, source_target_pairs={{0,1},{1,0},{2,3},{3,2},{4,5},{5,4},{6,7},{7,6},{8,9},{9,8},{10,11... | collective-permute-start | bytes 2359304 | tf_op jit(solution)/shard_map/ppermute | solution.py:598
  369.9 33.5 %collective-permute-start.26 = (bf16[64,1792]{1,0:T(8,128)(2,1)}, bf16[64,1792]{1,0:T(8,128)(2,1)S(1)}, u32[]{:S(2)}, u32[]{:S(2)}) collective-permute-start(bf16[64,1792]{1,0:T(8,128)(2,1)} %get-tuple-element.203), channel_id=1, source_target_pairs={{0,8},{8,0},{16,24},{24,16},{1,9},{9,1},{17,25},{25,17},{2,10},{10... | collective-permute-start | bytes 688136 | tf_op jit(solution)/shard_map/ppermute | solution.py:761
  370.0 33.4 %collective-permute-start.25 = (bf16[128,1024]{1,0:T(8,128)(2,1)}, bf16[128,1024]{1,0:T(8,128)(2,1)S(1)}, u32[]{:S(2)}, u32[]{:S(2)}) collective-permute-start(bf16[128,1024]{1,0:T(8,128)(2,1)} %get-tuple-element.201), channel_id=1, source_target_pairs={{0,16},{8,24},{16,0},{24,8},{1,17},{9,25},{17,1},{25,9},{2,18},{10... | collective-permute-start | bytes 786440 | tf_op jit(solution)/shard_map/ppermute | solution.py:761
  376.1 27.3 %collective-permute-start.27 = (bf16[2,64,1536]{2,1,0:T(8,128)(2,1)}, bf16[2,64,1536]{2,1,0:T(8,128)(2,1)S(1)}, u32[]{:S(2)}, u32[]{:S(2)}) collective-permute-start(bf16[2,64,1536]{2,1,0:T(8,128)(2,1)} %get-tuple-element.205), channel_id=1, source_target_pairs={{0,2},{1,3},{2,0},{3,1},{4,6},{5,7},{6,4},{7,5},{8,10},{9,11},{10,... | collective-permute-start | bytes 1179656 | tf_op jit(solution)/shard_map/ppermute | solution.py:598
  377.4 26.0 %collective-permute-start.28 = (bf16[2,64,1536]{2,1,0:T(8,128)(2,1)}, bf16[2,64,1536]{2,1,0:T(8,128)(2,1)S(1)}, u32[]{:S(2)}, u32[]{:S(2)}) collective-permute-start(bf16[2,64,1536]{2,1,0:T(8,128)(2,1)} %get-tuple-element.207), channel_id=1, source_target_pairs={{0,4},{1,5},{2,6},{3,7},{4,0},{5,1},{6,2},{7,3},{8,12},{9,13},{10,... | collective-permute-start | bytes 1179656 | tf_op jit(solution)/shard_map/ppermute | solution.py:598
  408.4 13.6 %collective-permute-start.33 = (bf16[32,1792]{1,0:T(8,128)(2,1)}, bf16[32,1792]{1,0:T(8,128)(2,1)S(1)}, u32[]{:S(2)}, u32[]{:S(2)}) collective-permute-start(bf16[32,1792]{1,0:T(8,128)(2,1)} %get-tuple-element.216), channel_id=1, source_target_pairs={{0,16},{8,24},{16,0},{24,8},{1,17},{9,25},{17,1},{25,9},{2,18},{10... | collective-permute-start | bytes 344072 | tf_op jit(solution)/shard_map/ppermute | solution.py:761
  409.1 19.7 %collective-permute-start.32 = (bf16[128,1024]{1,0:T(8,128)(2,1)}, bf16[128,1024]{1,0:T(8,128)(2,1)S(1)}, u32[]{:S(2)}, u32[]{:S(2)}) collective-permute-start(bf16[128,1024]{1,0:T(8,128)(2,1)} %get-tuple-element.214.refs_6_), channel_id=1, source_target_pairs={{0,16},{8,24},{16,0},{24,8},{1,17},{9,25},{17,1},{25,9},{2,18},{10... | collective-permute-start | bytes 786440 | tf_op jit(solution)/shard_map/ppermute | solution.py:761
  411.4 2.9 collective-permute-start.29
  411.4 12.1 %collective-permute-start.30 = (bf16[2,64,768]{2,1,0:T(8,128)(2,1)}, bf16[2,64,768]{2,1,0:T(8,128)(2,1)S(1)}, u32[]{:S(2)}, u32[]{:S(2)}) collective-permute-start(bf16[2,64,768]{2,1,0:T(8,128)(2,1)} %get-tuple-element.211), channel_id=1, source_target_pairs={{0,2},{1,3},{2,0},{3,1},{4,6},{5,7},{6,4},{7,5},{8,10},{9,11},{10,... | collective-permute-start | bytes 589832 | tf_op jit(solution)/shard_map/ppermute | solution.py:598
  412.9 10.6 %collective-permute-start.31 = (bf16[2,64,768]{2,1,0:T(8,128)(2,1)}, bf16[2,64,768]{2,1,0:T(8,128)(2,1)S(1)}, u32[]{:S(2)}, u32[]{:S(2)}) collective-permute-start(bf16[2,64,768]{2,1,0:T(8,128)(2,1)} %get-tuple-element.213), channel_id=1, source_target_pairs={{0,4},{1,5},{2,6},{3,7},{4,0},{5,1},{6,2},{7,3},{8,12},{9,13},{10,... | collective-permute-start | bytes 589832 | tf_op jit(solution)/shard_map/ppermute | solution.py:598
  414.4 14.5 %copy-start.47 = (f32[4,576]{1,0:T(4,128)}, f32[4,576]{1,0:T(4,128)S(1)}, u32[]{:S(2)}) copy-start(f32[4,576]{1,0:T(4,128)S(1)} %collective-permute-done.29.refs_1_) | copy-start | bytes 27652
  414.4 10.0 %collective-permute-start.34 = (bf16[64,1536]{1,0:T(8,128)(2,1)}, bf16[64,1536]{1,0:T(8,128)(2,1)S(1)}, u32[]{:S(2)}, u32[]{:S(2)}) collective-permute-start(bf16[64,1536]{1,0:T(8,128)(2,1)} %get-tuple-element.217), channel_id=1, source_target_pairs={{0,4},{1,5},{2,6},{3,7},{4,0},{5,1},{6,2},{7,3},{8,12},{9,13},{10,... | collective-permute-start | bytes 589832 | tf_op jit(solution)/shard_map/ppermute | solution.py:598
  422.0 6.8 %collective-permute-start.35 = (bf16[64,1536]{1,0:T(8,128)(2,1)}, bf16[64,1536]{1,0:T(8,128)(2,1)S(1)}, u32[]{:S(2)}, u32[]{:S(2)}) collective-permute-start(bf16[64,1536]{1,0:T(8,128)(2,1)} %get-tuple-element.218), channel_id=1, source_target_pairs={{0,2},{1,3},{2,0},{3,1},{4,6},{5,7},{6,4},{7,5},{8,10},{9,11},{10,... | collective-permute-start | bytes 589832 | tf_op jit(solution)/shard_map/ppermute | solution.py:598
  433.0 19.7 %collective-permute-start.39 = (bf16[256,1024]{1,0:T(8,128)(2,1)}, bf16[256,1024]{1,0:T(8,128)(2,1)S(1)}, u32[]{:S(2)}, u32[]{:S(2)}) collective-permute-start(bf16[256,1024]{1,0:T(8,128)(2,1)} %get-tuple-element.223.refs_8_), channel_id=1, source_target_pairs={{0,8},{8,0},{16,24},{24,16},{1,9},{9,1},{17,25},{25,17},{2,10},{10... | collective-permute-start | bytes 1572872 | tf_op jit(solution)/shard_map/ppermute | solution.py:761
  433.1 19.6 %collective-permute-start.41 = (bf16[64,1536]{1,0:T(8,128)(2,1)}, bf16[64,1536]{1,0:T(8,128)(2,1)S(1)}, u32[]{:S(2)}, u32[]{:S(2)}) collective-permute-start(bf16[64,1536]{1,0:T(8,128)(2,1)} %get-tuple-element.226), channel_id=1, source_target_pairs={{0,8},{8,0},{16,24},{24,16},{1,9},{9,1},{17,25},{25,17},{2,10},{10... | collective-permute-start | bytes 589832 | tf_op jit(solution)/shard_map/ppermute | solution.py:761
  435.1 15.5 %collective-permute-start.40 = (bf16[32,1792]{1,0:T(8,128)(2,1)}, bf16[32,1792]{1,0:T(8,128)(2,1)S(1)}, u32[]{:S(2)}, u32[]{:S(2)}) collective-permute-start(bf16[32,1792]{1,0:T(8,128)(2,1)} %get-tuple-element.224.refs_10_), channel_id=1, source_target_pairs={{0,16},{8,24},{16,0},{24,8},{1,17},{9,25},{17,1},{25,9},{2,18},{10... | collective-permute-start | bytes 344072 | tf_op jit(solution)/shard_map/ppermute | solution.py:761
  435.7 3.8 collective-permute-start.36
  437.4 4.8 collective-permute-start.37
  439.5 13.2 %copy-start.48 = (f32[2,576]{1,0:T(2,128)}, f32[2,576]{1,0:T(2,128)S(1)}, u32[]{:S(2)}) copy-start(f32[2,576]{1,0:T(2,128)S(1)} %collective-permute-done.36.refs_1_) | copy-start | bytes 13828
  439.5 4.8 collective-permute-start.38
  442.3 10.5 %copy-start.43 = (bf16[64,768]{1,0:T(8,128)(2,1)}, bf16[64,768]{1,0:T(8,128)(2,1)S(1)}, u32[]{:S(2)}) copy-start(bf16[64,768]{1,0:T(8,128)(2,1)S(1)} %collective-permute-done.37.refs_4_) | copy-start | bytes 294916
  457.1 7.9 %collective-permute-start.43 = (bf16[64,1792]{1,0:T(8,128)(2,1)}, bf16[64,1792]{1,0:T(8,128)(2,1)S(1)}, u32[]{:S(2)}, u32[]{:S(2)}) collective-permute-start(bf16[64,1792]{1,0:T(8,128)(2,1)} %get-tuple-element.229.refs_2_), channel_id=1, source_target_pairs={{0,8},{8,0},{16,24},{24,16},{1,9},{9,1},{17,25},{25,17},{2,10},{10... | collective-permute-start | bytes 688136 | tf_op jit(solution)/shard_map/ppermute | solution.py:761
  457.8 5.9 %collective-permute-start.44 = (bf16[32,1536]{1,0:T(8,128)(2,1)}, bf16[32,1536]{1,0:T(8,128)(2,1)S(1)}, u32[]{:S(2)}, u32[]{:S(2)}) collective-permute-start(bf16[32,1536]{1,0:T(8,128)(2,1)} %get-tuple-element.231), channel_id=1, source_target_pairs={{0,16},{8,24},{16,0},{24,8},{1,17},{9,25},{17,1},{25,9},{2,18},{10... | collective-permute-start | bytes 294920 | tf_op jit(solution)/shard_map/ppermute | solution.py:761
  459.5 3.8 collective-permute-start.42
  465.7 10.1 %copy-start.31 = (bf16[128,768]{1,0:T(8,128)(2,1)S(1)}, bf16[128,768]{1,0:T(8,128)(2,1)}, u32[]{:S(2)}) copy-start(bf16[128,768]{1,0:T(8,128)(2,1)} %get-tuple-element.238.refs_3_) | copy-start | bytes 589828
  470.7 10.6 %collective-permute-start.45 = (bf16[32,1536]{1,0:T(8,128)(2,1)}, bf16[32,1536]{1,0:T(8,128)(2,1)S(1)}, u32[]{:S(2)}, u32[]{:S(2)}) collective-permute-start(bf16[32,1536]{1,0:T(8,128)(2,1)} %get-tuple-element.233.refs_0_), channel_id=1, source_target_pairs={{0,16},{8,24},{16,0},{24,8},{1,17},{9,25},{17,1},{25,9},{2,18},{10... | collective-permute-start | bytes 294920 | tf_op jit(solution)/shard_map/ppermute | solution.py:761
  472.1 6.1 %collective-permute-start.48 = (f32[1,576]{1,0:T(1,128)}, f32[1,576]{1,0:T(1,128)S(1)}, u32[]{:S(2)}, u32[]{:S(2)}) collective-permute-start(f32[1,576]{1,0:T(1,128)} %get-tuple-element.234.refs_2_), channel_id=1, source_target_pairs={{0,24},{8,0},{16,8},{24,16},{1,25},{9,1},{17,9},{25,17},{2,26},{10... | collective-permute-start | bytes 6920 | tf_op jit(solution)/shard_map/ppermute | solution.py:765
  474.4 6.4 %collective-permute-start.47 = (f32[1,576]{1,0:T(1,128)}, f32[1,576]{1,0:T(1,128)S(1)}, u32[]{:S(2)}, u32[]{:S(2)}) collective-permute-start(f32[1,576]{1,0:T(1,128)} %get-tuple-element.234.refs_2_), channel_id=1, source_target_pairs={{0,16},{8,24},{16,0},{24,8},{1,17},{9,25},{17,1},{25,9},{2,18},{10... | collective-permute-start | bytes 6920 | tf_op jit(solution)/shard_map/ppermute | solution.py:765
  474.4 6.9 %collective-permute-start.46 = (f32[1,576]{1,0:T(1,128)}, f32[1,576]{1,0:T(1,128)S(1)}, u32[]{:S(2)}, u32[]{:S(2)}) collective-permute-start(f32[1,576]{1,0:T(1,128)} %get-tuple-element.234.refs_2_), channel_id=1, source_target_pairs={{0,8},{8,16},{16,24},{24,0},{1,9},{9,17},{17,25},{25,1},{2,10},{10... | collective-permute-start | bytes 6920 | tf_op jit(solution)/shard_map/ppermute | solution.py:765
  475.8 11.9 %collective-permute-start.52 = (bf16[128,768]{1,0:T(8,128)(2,1)S(1)}, bf16[128,768]{1,0:T(8,128)(2,1)S(1)}, u32[]{:S(2)}, u32[]{:S(2)}) collective-permute-start(bf16[128,768]{1,0:T(8,128)(2,1)S(1)} %copy-done.31), channel_id=1, source_target_pairs={{0,24},{8,0},{16,8},{24,16},{1,25},{9,1},{17,9},{25,17},{2,26},{10... | collective-permute-start | bytes 589832 | tf_op jit(solution)/shard_map/ppermute | solution.py:765
  478.2 16.4 %collective-permute-start.51 = (bf16[128,768]{1,0:T(8,128)(2,1)S(1)}, bf16[128,768]{1,0:T(8,128)(2,1)S(1)}, u32[]{:S(2)}, u32[]{:S(2)}) collective-permute-start(bf16[128,768]{1,0:T(8,128)(2,1)S(1)} %copy-done.31), channel_id=1, source_target_pairs={{0,16},{8,24},{16,0},{24,8},{1,17},{9,25},{17,1},{25,9},{2,18},{10... | collective-permute-start | bytes 589832 | tf_op jit(solution)/shard_map/ppermute | solution.py:765
  480.8 13.8 %collective-permute-start.50 = (bf16[128,768]{1,0:T(8,128)(2,1)S(1)}, bf16[128,768]{1,0:T(8,128)(2,1)S(1)}, u32[]{:S(2)}, u32[]{:S(2)}) collective-permute-start(bf16[128,768]{1,0:T(8,128)(2,1)S(1)} %copy-done.31), channel_id=1, source_target_pairs={{0,8},{8,16},{16,24},{24,0},{1,9},{9,17},{17,25},{25,1},{2,10},{10... | collective-permute-start | bytes 589832 | tf_op jit(solution)/shard_map/ppermute | solution.py:765
  486.1 10.4 %collective-permute-start.49 = (bf16[64,1536]{1,0:T(8,128)(2,1)}, bf16[64,1536]{1,0:T(8,128)(2,1)S(1)}, u32[]{:S(2)}, u32[]{:S(2)}) collective-permute-start(bf16[64,1536]{1,0:T(8,128)(2,1)} %get-tuple-element.237.refs_1_), channel_id=1, source_target_pairs={{0,8},{8,0},{16,24},{24,16},{1,9},{9,1},{17,25},{25,17},{2,10},{10... | collective-permute-start | bytes 589832 | tf_op jit(solution)/shard_map/ppermute | solution.py:761
  (46 other events, 116.6 us)
Sparse Core Ops, SparseCore 0:
  53.7 59.2 all-gather.4
  114.9 54.3 all-gather.2
  178.9 71.0 reduce-scatter.1
  331.2 72.0 all-reduce.1

commit v3 on v2

v3 whole, which is shorter than its diff:
```python
import functools

import jax
import jax.numpy as jnp
from jax import lax
from jax.experimental import pallas as pl
from jax.experimental.pallas import tpu as pltpu
from jax.sharding import PartitionSpec as P

HEADS = 16
HEAD_DIM = 64
BUCKETS = 32
T = 256
NEG = -1e30
F32 = jnp.float32
BF = jnp.bfloat16
GROUPS = 8
CHUNKS = 4
HEAD_GROUPS = 4
NN = (((1,), (0,)), ((), ()))
NT = (((1,), (1,)), ((), ()))
TN = (((0,), (0,)), ((), ()))
TT = (((0,), (1,)), ((), ()))
ANY = pl.BlockSpec(memory_space=pl.ANY)
SMEM = pl.BlockSpec(memory_space=pltpu.SMEM)


def dot(a, b, form=NN):
    return lax.dot_general(a, b, form, preferred_element_type=F32)


def params(mib=60):
    return pltpu.CompilerParams(vmem_limit_bytes=mib << 20)


def cost(flops, moved, exps=0):
    return pl.CostEstimate(flops=int(flops), bytes_accessed=int(moved), transcendentals=int(exps))


def resident(shape):
    return pl.BlockSpec(shape, lambda i, *_: (0,) * len(shape))


def shape_of(shape, kind):
    return jax.ShapeDtypeStruct(shape, kind)


def last_block(part, width):
    at = part.shape[1] // width - 1
    return pl.BlockSpec((part.shape[0], width), lambda i: (0, at))


def block_of(me, r):
    return pl.multiple_of(jnp.bitwise_xor(me, r) * 128, 128)


PLACES = (0, 2, 4, 6, 1, 3, 5, 7)


def in_order(parts):
    return [parts[PLACES.index(r)] for r in range(8)]


def normalise(v):
    centred = v - jnp.mean(v, axis=-1, keepdims=True)
    rstd = lax.rsqrt(jnp.mean(centred * centred, axis=-1, keepdims=True) + 1e-5)
    return centred * rstd, rstd


def with_deps(kernel, inputs, count):
    def body(*refs):
        return kernel(*refs[:inputs], *refs[inputs + count:])
    return body


def prepare_kernel(me_ref, len_ref, x_ref, cot_ref, bucket_ref, *refs):
    small_ref, n1t_ref, og_ref, vec_ref, base_ref, abs_s = refs
    me = me_ref[0]
    rows = x_ref.shape[0]

    @pl.when(pl.program_id(0) == 0)
    def _():
        small = small_ref[...].astype(F32)
        for r in range(8):
            for k in range(4):
                vec_ref[k:k + 1, pl.ds(block_of(me, r), 128)] = small[r:r + 1, k * 128:(k + 1) * 128]
        table = jnp.concatenate([
            small[h // 2:h // 2 + 1, 512 + h % 2 * BUCKETS:512 + (h % 2 + 1) * BUCKETS] for h in range(HEADS)]).astype(BF)
        slots = bucket_ref.shape[1]
        onehot = (bucket_ref[...] == lax.broadcasted_iota(jnp.int32, (BUCKETS, slots), 0)).astype(BF)
        by = dot(table, onehot)
        for u in range(slots // T):
            base_ref[:, u, :] = by[:, slots - (u + 1) * T:slots - u * T]

    hat, _ = normalise(x_ref[...].astype(F32))
    abs_s[...] = hat * vec_ref[0:1] + vec_ref[1:2]
    for r in range(8):
        n1t_ref[r * 128:(r + 1) * 128, :] = abs_s[:, pl.ds(block_of(me, r), 128)].astype(BF).T
    slot = pl.program_id(0) * rows + lax.broadcasted_iota(jnp.int32, (rows, 1), 0)
    og_ref[...] = jnp.where(slot < len_ref[0], cot_ref[...], jnp.zeros_like(cot_ref))


def prepare(me, lengths, x, cot, buckets, small, deps=()):
    rows, width = x.shape
    tile = pl.BlockSpec((T, width), lambda i: (i, 0))
    return pl.pallas_call(
        with_deps(prepare_kernel, 6, len(deps)), grid=(rows // T,), name="prepare",
        in_specs=[SMEM, SMEM, tile, tile, resident(buckets.shape), resident(small.shape)] + [ANY] * len(deps),
        out_specs=[pl.BlockSpec((width, T), lambda i: (0, i)), tile, resident((4, width)), resident((HEADS, rows // T, T))],
        out_shape=[shape_of((width, rows), BF), shape_of((rows, width), BF), shape_of((4, width), F32),
                   shape_of((HEADS, rows // T, T), F32)],
        scratch_shapes=[pltpu.VMEM((T, width), F32)],
        compiler_params=params(), cost_estimate=cost(1e9, 8e6),
    )(me, lengths, x, cot, buckets, small, *deps)


def pack_kernel(wi_ref, wd_ref, *refs):
    for c, out in enumerate(refs):
        for k in range(2):
            for b in range(8):
                col = (b * CHUNKS + 2 * c + k) * 128
                out[k, :128, b * 128:(b + 1) * 128] = wi_ref[:, col:col + 128]
            out[k, 128:, :] = wd_ref[(2 * c + k) * 128:(2 * c + k + 1) * 128, :]


def pack(w_in, w_down, deps):
    vm = pl.BlockSpec(memory_space=pltpu.VMEM)
    return pl.pallas_call(
        with_deps(pack_kernel, 2, len(deps)), name="pack", in_specs=[vm] * 2 + [ANY] * len(deps), out_specs=[vm] * 2,
        out_shape=[shape_of((2, 256, 1024), BF)] * 2, compiler_params=params(), cost_estimate=cost(1e6, 4e6),
    )(w_in, w_down, *deps)


def lead_kernel(qkv_ref, out_ref, a_ref, b_ref, c_ref, d_ref, e_ref, piece_ref, small_ref):
    cols = qkv_ref.shape[1]
    piece_ref[:, :cols] = qkv_ref[...]
    piece_ref[:, cols:] = out_ref[...]
    at = 0
    for ref in (a_ref, b_ref, c_ref, d_ref, e_ref):
        small_ref[:, at:at + ref.shape[1]] = ref[...]
        at += ref.shape[1]


def lead(w_qkv, w_out, *small):
    vm = pl.BlockSpec(memory_space=pltpu.VMEM)
    rows, cols = w_qkv.shape[0], w_qkv.shape[1] + w_out.shape[1]
    small = [v[None] for v in small]
    return pl.pallas_call(
        lead_kernel, name="lead", in_specs=[vm] * 7, out_specs=[vm] * 2,
        out_shape=[shape_of((rows, cols), BF), shape_of((1, sum(v.shape[1] for v in small)), BF)],
        compiler_params=params(), cost_estimate=cost(1e6, 2e6),
    )(w_qkv, w_out, *small)


def halves_kernel(a_ref, b_ref, a_out, b_out):
    half = a_out.shape[0]
    a_out[...] = a_ref[:half]
    b_out[...] = b_ref[half:]


def halves(a, b):
    vm = pl.BlockSpec(memory_space=pltpu.VMEM)
    out = shape_of((a.shape[0] // 2, a.shape[1]), a.dtype)
    return pl.pallas_call(
        halves_kernel, name="halves", in_specs=[vm] * 2, out_specs=[vm] * 2, out_shape=[out] * 2,
        compiler_params=params(), cost_estimate=cost(1e6, 3e6),
    )(a, b)


def join_kernel(a_ref, b_ref, out_ref):
    half = a_ref.shape[0]
    out_ref[:half] = a_ref[...]
    out_ref[half:] = b_ref[...]


def join(a, b, deps):
    vm = pl.BlockSpec(memory_space=pltpu.VMEM)
    return pl.pallas_call(
        with_deps(join_kernel, 2, len(deps)), name="join", in_specs=[vm] * 2 + [ANY] * len(deps), out_specs=vm,
        out_shape=shape_of((2 * a.shape[0], a.shape[1]), a.dtype), compiler_params=params(), cost_estimate=cost(1e6, 2e6),
    )(a, b, *deps)


def project_kernel(n1t_ref, *refs):
    w = jnp.concatenate([r[...] for r in in_order(refs[:8])], axis=0)
    out = dot(w, n1t_ref[...], TN).astype(BF)
    refs[8][...] = out.reshape(refs[8].shape)


def project(n1t, parts):
    width, rows = n1t.shape
    cols = 3 * width
    tile = 512
    return pl.pallas_call(
        project_kernel, grid=(cols // tile,), name="project",
        in_specs=[resident((width, rows))] + [pl.BlockSpec((p.shape[0], tile), lambda i: (0, i)) for p in parts],
        out_specs=pl.BlockSpec((tile // HEAD_DIM, HEAD_DIM, rows), lambda i: (i, 0, 0)),
        out_shape=shape_of((cols // HEAD_DIM, HEAD_DIM, rows), BF),
        compiler_params=params(), cost_estimate=cost(2 * rows * width * cols, 14e6),
    )(n1t, *parts)


def toeplitz(base_ref):
    row = lax.broadcasted_iota(jnp.int32, (T, T), 0)
    col = lax.broadcasted_iota(jnp.int32, (T, T), 1)
    count = base_ref.shape[1]
    rolled = [
        pltpu.roll(jnp.broadcast_to(base_ref[0, u:u + 1, :], (T, T)), 0, 1, stride=1, stride_axis=0)
        for u in range(count)
    ]
    return [jnp.where(col >= row, rolled[u], rolled[u + 1] if u + 1 < count else NEG) for u in range(count)]


def key_mask(len_ref, start):
    slot = start + lax.broadcasted_iota(jnp.int32, (T, 1), 0)
    return jnp.where(slot < len_ref[0], 0.0, NEG).astype(F32)


def attend_kernel(me_ref, len_ref, base_ref, q_ref, k_ref, v_ref, o_ref, lt_ref, g_ref):
    heads, tiles = base_ref.shape[:2]
    keys = [k_ref[h].T for h in range(heads)]
    for h in range(heads):
        for u, t in enumerate(toeplitz(base_ref.at[h:h + 1])):
            g_ref[h, u * T:(u + 1) * T, :] = t

    def scores(h, b):
        nk = (b + 1) * T
        q = q_ref[h, :, b * T:nk] * BF(HEAD_DIM ** -0.5)
        s = dot(keys[h][:nk], q) + g_ref[h, (tiles - 1 - b) * T:, :]
        if b == tiles - 1:
            s = jnp.concatenate([s[:b * T], s[b * T:] + key_mask(len_ref, b * T)], axis=0)
        return s, jnp.max(s, axis=0, keepdims=True)

    order = [(h, b) for b in range(tiles) for h in range(heads)]
    ahead = scores(*order[0])
    for n, (h, b) in enumerate(order):
        s, m = ahead
        if n + 1 < len(order):
            ahead = scores(*order[n + 1])
        sl = slice(b * T, (b + 1) * T)
        p = jnp.exp(s - m)
        total = jnp.sum(p, axis=0, keepdims=True)
        o = dot(v_ref[h, :, :(b + 1) * T], p.astype(BF))
        o_ref[h, :, sl] = (o * (1.0 / total)).astype(BF)
        lt_ref[h, :, sl] = m + jnp.log(total)


def head_place(h, me_ref):
    return jnp.bitwise_xor(h // 2, me_ref[0]) * 2 + h % 2


def attend(me, lengths, base, qkv):
    rows = qkv.shape[-1]
    tiles = rows // T
    pairs = HEADS // 2
    block = (2, HEAD_DIM, rows)
    at = lambda off: pl.BlockSpec(block, lambda h, m: (h + off, 0, 0))
    return pl.pallas_call(
        attend_kernel, name="attend",
        grid_spec=pltpu.PrefetchScalarGridSpec(
            num_scalar_prefetch=1, grid=(pairs,),
            in_specs=[SMEM, pl.BlockSpec((2, tiles, T), lambda h, m: (jnp.bitwise_xor(h, m[0]), 0, 0)), at(0), at(pairs), at(2 * pairs)],
            out_specs=[pl.BlockSpec(block, lambda h, m: (jnp.bitwise_xor(h, m[0]), 0, 0)),
                       pl.BlockSpec((2, 1, rows), lambda h, m: (h, 0, 0))],
            scratch_shapes=[pltpu.VMEM((2, rows, T), F32)]),
        out_shape=[shape_of((HEADS, HEAD_DIM, rows), BF), shape_of((HEADS, 1, rows), F32)],
        compiler_params=params(), cost_estimate=cost(30e9, 10e6),
    )(me, lengths, base, qkv, qkv, qkv)


def skew_sums(dg_ref, dist_ref):
    row = lax.broadcasted_iota(jnp.int32, (T, T), 0)
    col = lax.broadcasted_iota(jnp.int32, (T, T), 1)
    for u in range(dist_ref.shape[1]):
        z = jnp.where(col >= row, dg_ref[u * T:(u + 1) * T, :], dg_ref[(u - 1) * T:u * T, :] if u else 0.0)
        acc = z[0:8]
        for g in range(1, T // 8):
            acc = acc + pltpu.roll(z[8 * g:8 * g + 8], T - 8 * g, 1)
        tot = acc[0:1]
        for r in range(1, 8):
            tot = tot + pltpu.roll(acc[r:r + 1], T - r, 1)
        dist_ref[0, u:u + 1, :] = tot


def attend_back_kernel(me_ref, len_ref, base_ref, q_ref, k_ref, v_ref, o_ref, do_ref, lt_ref,
                       dq_ref, dk_ref, dv_ref, dist_ref, g_ref, dg_ref, dk_s, dv_s):
    tiles = base_ref.shape[1]
    scale = HEAD_DIM ** -0.5
    for u, t in enumerate(toeplitz(base_ref)):
        g_ref[u * T:(u + 1) * T, :] = t
    kt = k_ref[0]
    k = kt.T
    v = v_ref[0].T

    def scores(b):
        nk = (b + 1) * T
        sl = slice(b * T, nk)
        q = q_ref[0, :, sl] * BF(scale)
        do = do_ref[0, :, sl]
        inner = jnp.sum(do.astype(F32) * o_ref[0, :, sl].astype(F32), axis=0, keepdims=True)
        s = dot(k[:nk], q) + g_ref[(tiles - 1 - b) * T:, :]
        if b == tiles - 1:
            s = jnp.concatenate([s[:b * T], s[b * T:] + key_mask(len_ref, b * T)], axis=0)
        p = jnp.exp(s - lt_ref[0, :, sl])
        ds = p * (dot(v[:nk], do) - inner)
        return q, do, p.astype(BF), ds

    ahead = scores(tiles - 1)
    for b in range(tiles - 1, -1, -1):
        q, do, pb, ds = ahead
        if b:
            ahead = scores(b - 1)
        nk = (b + 1) * T
        low = (tiles - 1 - b) * T
        dsb = ds.astype(BF)
        dq_ref[0, :, b * T:nk] = (dot(kt[:, :nk], dsb) * scale).astype(BF)
        dvp = dot(do, pb, NT)
        dkp = dot(q, dsb, NT)
        if b == tiles - 1:
            dk_s[...] = dkp
            dv_s[...] = dvp
            dg_ref[...] = ds
        else:
            dk_s[:, :nk] += dkp
            dv_s[:, :nk] += dvp
            dg_ref[low:, :] += ds
    dk_ref[0] = dk_s[...].astype(BF)
    dv_ref[0] = dv_s[...].astype(BF)
    skew_sums(dg_ref, dist_ref)


def attend_back(me, lengths, base, qkv, o, do, lt, first, count, deps=()):
    rows = qkv.shape[-1]
    tiles = rows // T
    block = (1, HEAD_DIM, rows)
    at = lambda off: pl.BlockSpec(block, lambda h, m: (h + off + first, 0, 0))
    placed = pl.BlockSpec(block, lambda h, m: (head_place(h + first, m), 0, 0))
    out = pl.BlockSpec(block, lambda h, m: (h, 0, 0))
    return pl.pallas_call(
        with_deps(attend_back_kernel, 9, len(deps)), name="attend_back",
        grid_spec=pltpu.PrefetchScalarGridSpec(
            num_scalar_prefetch=1, grid=(count,),
            in_specs=[SMEM, pl.BlockSpec((1, tiles, T), lambda h, m: (head_place(h + first, m), 0, 0)), at(0), at(HEADS), at(2 * HEADS),
                      placed, placed, pl.BlockSpec((1, 1, rows), lambda h, m: (h + first, 0, 0))] + [ANY] * len(deps),
            out_specs=[out, out, out, pl.BlockSpec((1, tiles, T), lambda h, m: (h, 0, 0))],
            scratch_shapes=[pltpu.VMEM((rows, T), F32), pltpu.VMEM((rows, T), F32),
                            pltpu.VMEM((HEAD_DIM, rows), F32), pltpu.VMEM((HEAD_DIM, rows), F32)]),
        out_shape=[shape_of((count, HEAD_DIM, rows), BF)] * 3 + [shape_of((count, tiles, T), F32)],
        compiler_params=params(), cost_estimate=cost(2.4e9 * count, 1.2e6 * count),
    )(me, lengths, base, qkv, qkv, qkv, o, do, lt, *deps)


def middle_kernel(me_ref, at_ref, x_ref, gain_ref, shift_ref, *refs):
    parts, (mid_ref, n2_ref, n2t_ref, abs_s) = refs[:8], refs[8:]
    me = me_ref[0]
    w = jnp.concatenate([r[...] for r in in_order(parts)], axis=0)
    mid = x_ref[...].astype(F32) + dot(at_ref[...], w, TN)
    mid_ref[...] = mid
    hat, _ = normalise(mid)
    abs_s[...] = hat * gain_ref[...] + shift_ref[...]
    for r in range(8):
        sl = slice(r * 128, (r + 1) * 128)
        part = abs_s[:, pl.ds(block_of(me, r), 128)].astype(BF)
        n2_ref[:, sl] = part
        n2t_ref[sl, :] = part.T


def middle_of(me, at, x, gain, shift, parts, deps=()):
    rows, width = x.shape
    tile = pl.BlockSpec((T, width), lambda i: (i, 0))
    turned = pl.BlockSpec((width, T), lambda i: (0, i))
    return pl.pallas_call(
        with_deps(middle_kernel, 5 + len(parts), len(deps)), grid=(rows // T,), name="middle",
        in_specs=[SMEM, turned, tile, resident((1, width)), resident((1, width))] + [last_block(p, width) for p in parts]
        + [ANY] * len(deps),
        out_specs=[tile, tile, turned],
        out_shape=[shape_of((rows, width), F32), shape_of((rows, width), BF), shape_of((width, rows), BF)],
        scratch_shapes=[pltpu.VMEM((T, width), F32)],
        compiler_params=params(), cost_estimate=cost(2 * rows * width * width, 14e6),
    )(me, at, x, gain, shift, *parts, *deps)


def gelu_parts(x):
    a = jnp.abs(x)
    t = 1.0 / (1.0 + a * (0.3275911 * 0.7071067811865476))
    e = jnp.exp(x * x * -0.5)
    poly = t * (0.127414796 + t * (-0.142248368 + t * (0.7107068705 + t * (-0.7265760135 + t * 0.5307027145))))
    q = poly * e
    phi = jnp.where(x >= 0.0, 1.0 - q, q)
    return x * phi, phi + x * (e * 0.3989422804014327)


def feed_kernel(chunks, stacked, counts, me_ref, n2_h, n2t_h, og_h, w_h, *refs):
    carried, deps, n_out = counts
    carry, refs = refs[:carried], refs[carried + deps:]
    outs, refs = refs[:n_out], refs[n_out:]
    n2_v, n2t_v, og_v, w_v, g_v, hid_v, send_v, keep_v, sem_in, sem_out = refs
    me = me_ref[0]
    shard = [jnp.bitwise_xor(me, r) for r in range(8)]
    loads = [(n2_h, n2_v)]
    for part in (slice(0, 128), slice(128, 256)):
        loads += [(w_h.at[shard[r], chunks[0], part, :], w_v.at[r, 0, part, :]) for r in range(8)]
        if part.start == 0:
            loads.append((og_h, og_v))
    early = (9, 18)
    for k, c in enumerate(chunks[1:]):
        loads += [(w_h.at[shard[r], c], w_v.at[r, k + 1]) for r in range(8)]
    loads += list(zip(carry, (g_v,))) + [(n2t_h, n2t_v)]
    copies = [pltpu.make_async_copy(a, b, sem_in.at[i]) for i, (a, b) in enumerate(loads)]
    for x in copies:
        x.start()
    for x in copies[:early[0]]:
        x.wait()
    stores = []

    def store(a, b):
        stores.append(pltpu.make_async_copy(a, b, sem_out.at[len(stores)]))
        stores[-1].start()

    n2 = n2_v[...]
    steps = 2 * len(chunks)

    def products(t):
        k, u = t // 2, t % 2
        offs = [block_of(me, 4 * u + j) for j in range(4)]
        wi = jnp.concatenate([w_v[:, k, :128, pl.ds(o, 128)].reshape(1024, 128) for o in offs], axis=1)
        units = dot(n2, wi)
        if t == 0:
            for x in copies[early[0]:early[1]]:
                x.wait()
        wd = w_v[4 * u:4 * u + 4, k, 128:, :].reshape(512, 1024)
        return offs, wi, units, dot(og_v[...], wd, NT)

    ahead = products(0)
    og = og_v[...]
    for t in range(steps):
        k, u = t // 2, t % 2
        offs, wi, units, back = ahead
        if t + 1 < steps:
            ahead = products(t + 1)
        hid, slope = gelu_parts(units)
        hid = hid.astype(BF)
        pre = (back * slope).astype(BF)
        hid_v[:, t * 512:(t + 1) * 512] = hid
        store(hid_v.at[:, t * 512:(t + 1) * 512], outs[1].at[:, t * 512:(t + 1) * 512])
        if t == 0:
            for x in copies[early[1]:]:
                x.wait()
        if not carried and t == 0:
            g_v[...] = dot(pre, wi, NT)
        else:
            g_v[...] += dot(pre, wi, NT)
        if t == steps - 1:
            store(g_v, outs[0])
        dwi = dot(n2t_v[...], pre).astype(BF)
        for r in range(8):
            for j, o in enumerate(offs):
                (send_v if r % 2 else keep_v)[k, r // 2, :128, pl.ds(o, 128)] = dwi[r * 128:(r + 1) * 128, j * 128:(j + 1) * 128]
        if u == 1 and not stacked:
            for half, out in ((send_v, outs[2]), (keep_v, outs[3])):
                for b in range(4):
                    store(half.at[k, :, :128, b * 256:(b + 1) * 256], out.at[:, 8 * k + b])
        dwd = dot(hid, og, TN).astype(BF)
        for j in range(4):
            r = 4 * u + j
            (send_v if r % 2 else keep_v)[k, r // 2, 128:, :] = dwd[j * 128:(j + 1) * 128]
        if u == 1:
            if stacked:
                for r in range(8):
                    store((send_v if r % 2 else keep_v).at[k, r // 2], outs[2].at[shard[r], k])
            else:
                for half, out in ((send_v, outs[2]), (keep_v, outs[3])):
                    for b in range(4):
                        store(half.at[k, :, 128:, b * 256:(b + 1) * 256], out.at[:, 8 * k + 4 + b])
    for x in stores:
        x.wait()


def feed(chunks, stacked, me, n2, n2t, og, w, carry=(), deps=()):
    rows, width = n2.shape
    n = len(chunks)
    half = (n, 4, 256, 1024)
    grads = [(8, n, 256, 1024)] if stacked else [(4, 8 * n, 128, 256)] * 2
    counts = (len(carry), len(deps), 2 + len(grads))
    return pl.pallas_call(
        functools.partial(feed_kernel, chunks, stacked, counts), name="feed",
        in_specs=[SMEM] + [ANY] * (4 + len(carry) + len(deps)), out_specs=[ANY] * counts[2],
        out_shape=[shape_of((rows, width), F32), shape_of((rows, 1024 * n), BF)] + [shape_of(g, BF) for g in grads],
        scratch_shapes=[pltpu.VMEM((rows, width), BF), pltpu.VMEM((width, rows), BF), pltpu.VMEM((rows, width), BF),
                        pltpu.VMEM((8, n, 256, 1024), BF), pltpu.VMEM((rows, width), F32), pltpu.VMEM((rows, 1024 * n), BF),
                        pltpu.VMEM(half, BF), pltpu.VMEM(half, BF),
                        pltpu.SemaphoreType.DMA((20 + 8 * n,)), pltpu.SemaphoreType.DMA((20 * n + 1,))],
        compiler_params=params(), cost_estimate=cost(18e9 * n, 25e6),
    )(me, n2, n2t, og, w, *carry, *deps)


def output_kernel(me_ref, len_ref, mid_ref, *refs):
    hids, (w0_h, w1_h), (out_ref, w_v, sem) = refs[:-5], refs[-5:-3], refs[-3:]
    me = me_ref[0]
    i = pl.program_id(0)
    rows = mid_ref.shape[0]

    @pl.when(i == 0)
    def _():
        copies = []
        for k, h in enumerate((w0_h, w1_h)):
            for c in range(2):
                for r in range(8):
                    n = len(copies)
                    copies.append(pltpu.make_async_copy(
                        h.at[jnp.bitwise_xor(me, r), c, 128:, :], w_v.at[(2 * k + c) * 8 + r], sem.at[n]))
        for x in copies:
            x.start()
        for x in copies:
            x.wait()

    hid = jnp.concatenate([h[...] for h in hids], axis=1)
    total = mid_ref[...] + dot(hid, w_v[...].reshape(-1, w_v.shape[2]))
    slot = i * rows + lax.broadcasted_iota(jnp.int32, (rows, 1), 0)
    out_ref[...] = jnp.where(slot < len_ref[0], total, 0.0).astype(BF)


def output(me, lengths, mid, hids, w, deps=()):
    rows, width = mid.shape
    tile = pl.BlockSpec((T, width), lambda i: (i, 0))
    return pl.pallas_call(
        with_deps(output_kernel, 5 + len(hids), len(deps)), grid=(rows // T,), name="output",
        in_specs=[SMEM, SMEM, tile] + [pl.BlockSpec((T, h.shape[1]), lambda i: (i, 0)) for h in hids] + [ANY] * (2 + len(deps)),
        out_specs=tile, out_shape=shape_of((rows, width), BF),
        scratch_shapes=[pltpu.VMEM((32, 128, width), BF), pltpu.SemaphoreType.DMA((32,))],
        compiler_params=params(), cost_estimate=cost(9e9, 20e6),
    )(me, lengths, mid, *hids, *w, *deps)


def norm_back(hat, rstd, grad, gain):
    t = grad * gain
    return (t - jnp.mean(t, axis=-1, keepdims=True) - hat * jnp.mean(t * hat, axis=-1, keepdims=True)) * rstd


def middle_back_kernel(me_ref, mid_ref, g_ref, og_ref, at_ref, gain_ref, *refs):
    parts, (mg_ref, do_ref, send_ref, keep_ref, vec_ref, abs_s, acc_s) = refs[:8], refs[8:]
    me = me_ref[0]
    i = pl.program_id(0)
    for r in range(8):
        abs_s[:, pl.ds(block_of(me, r), 128)] = g_ref[:, r * 128:(r + 1) * 128]
    grad = abs_s[...]
    hat, rstd = normalise(mid_ref[...])
    sums = jnp.concatenate([jnp.sum(grad * hat, axis=0, keepdims=True), jnp.sum(grad, axis=0, keepdims=True)], axis=0)
    mg = og_ref[...].astype(F32) + norm_back(hat, rstd, grad, gain_ref[...])
    mg_ref[...] = mg
    branch = mg.astype(BF)
    w = jnp.concatenate([r[...] for r in in_order(parts)], axis=0)
    do_ref[...] = dot(w, branch, NT).astype(BF)
    dw = dot(at_ref[...], branch)

    @pl.when(i == 0)
    def _():
        vec_ref[...] = sums
        acc_s[...] = dw

    @pl.when(i > 0)
    def _():
        vec_ref[...] += sums
        acc_s[...] += dw

    @pl.when(i == pl.num_programs(0) - 1)
    def _():
        for r in range(8):
            for b in range(4):
                (send_ref if r % 2 else keep_ref)[r // 2, b] = acc_s[r * 128:(r + 1) * 128, b * 256:(b + 1) * 256].astype(BF)


def middle_back(me, mid, g, og, at, gain, parts, deps=()):
    rows, width = mid.shape
    tile = pl.BlockSpec((T, width), lambda i: (i, 0))
    turned = pl.BlockSpec((width, T), lambda i: (0, i))
    block = (4, 4, 128, 256)
    return pl.pallas_call(
        with_deps(middle_back_kernel, 6 + len(parts), len(deps)), grid=(rows // T,), name="middle_back",
        in_specs=[SMEM, tile, tile, tile, turned, resident((1, width))] + [last_block(p, width) for p in parts] + [ANY] * len(deps),
        out_specs=[tile, turned, resident(block), resident(block), resident((2, width))],
        out_shape=[shape_of((rows, width), F32), shape_of((width, rows), BF), shape_of(block, BF), shape_of(block, BF),
                   shape_of((2, width), F32)],
        scratch_shapes=[pltpu.VMEM((T, width), F32), pltpu.VMEM((width, width), F32)],
        compiler_params=params(), cost_estimate=cost(4 * rows * width * width, 24e6),
    )(me, mid, g, og, at, gain, *parts, *deps)


class Part:
    def __init__(self, array, start=0, count=None):
        self.array, self.start = array, start
        self.shape = ((array.shape[0] - start) if count is None else count,) + tuple(array.shape[1:])
        self.dtype = array.dtype

    def part(self, start, count):
        return Part(self.array, self.start + start, count)


def staged_kernel(steps, places, n_in, n_dep, n_out, where_ref, *refs):
    sources, refs = refs[:n_in], refs[n_in + n_dep:]
    dests, refs = refs[:n_out], refs[n_out:]
    n_kept = len(places)
    held, kept, sem_in, sem_out = refs[:n_in], refs[n_in:n_in + n_kept], refs[-2], refs[-1]
    loads = []
    for ins, _, _ in steps:
        for p in ins:
            k = len(loads)
            loads.append(pltpu.make_async_copy(sources[k].at[p.start:p.start + p.shape[0]], held[k], sem_in.at[k]))
    for c in loads:
        c.start()
    stores = []
    a = b = 0
    for ins, outs, fn in steps:
        for c in loads[a:a + len(ins)]:
            c.wait()
        fn(where_ref, held[a:a + len(ins)], kept[b:b + len(outs)])
        for k in range(b, b + len(outs)):
            n, start = places[k]
            stores.append(pltpu.make_async_copy(kept[k], dests[n].at[start:start + kept[k].shape[0]], sem_out.at[k]))
            stores[-1].start()
        a += len(ins)
        b += len(outs)
    for c in stores:
        c.wait()


def staged(where, steps, deps=()):
    steps = [([v if isinstance(v, Part) else Part(v) for v in ins], outs, fn) for ins, outs, fn in steps]
    parts = [v for ins, _, _ in steps for v in ins]
    flat = [o for _, outs, _ in steps for o in outs]
    arrays, places, by_way = [], [], {}
    for way, shape, kind in flat:
        if way is None:
            places.append((len(arrays), 0))
            arrays.append(shape_of(shape, kind))
            continue
        key = (way,) + tuple(shape[1:]) + (kind,)
        if key not in by_way:
            by_way[key] = len(arrays)
            arrays.append(shape_of((0,) + tuple(shape[1:]), kind))
        n = by_way[key]
        places.append((n, arrays[n].shape[0]))
        arrays[n] = shape_of((arrays[n].shape[0] + shape[0],) + tuple(shape[1:]), kind)
    out = pl.pallas_call(
        functools.partial(staged_kernel, steps, places, len(parts), len(deps), len(arrays)), name="staged",
        in_specs=[SMEM] + [ANY] * (len(parts) + len(deps)), out_specs=[ANY] * len(arrays), out_shape=arrays,
        scratch_shapes=[pltpu.VMEM(v.shape, v.dtype) for v in parts] + [pltpu.VMEM(o[1], o[2]) for o in flat]
        + [pltpu.SemaphoreType.DMA((len(parts),)), pltpu.SemaphoreType.DMA((len(flat),))],
        compiler_params=params(), cost_estimate=cost(3e9, 10e6),
    )(where, *(p.array for p in parts), *deps)
    sent = list(out)
    for key, n in by_way.items():
        sent[n] = send(out[n], key[0])
    flat = [[Part(v, start, o[1][0]) for v in sent[n]] if o[0] == "turns" else Part(sent[n], start, o[1][0])
            for (n, start), o in zip(places, flat)]
    result = []
    for _, o, _ in steps:
        result.append(flat[:len(o)])
        flat = flat[len(o):]
    return result, tuple(out)


def send(v, way):
    if way in ("core", "x", "y", "both"):
        return flip(v, {"core": 1, "x": 2, "y": 4, "both": 6}[way])
    if way == "turns":
        return copy_turns(v, 4)
    k = {"pair": 1, "far": 2}[way]
    return lax.ppermute(v, "rep", [(i, i ^ k) for i in range(4)])


def plus(*refs):
    total = refs[0].astype(F32)
    for r in refs[1:]:
        total = total + r.astype(F32)
    return total


def project_back(n1t, three, way):
    block = (12, 128, 256)

    def fn(_, ins, outs):
        n1 = ins[0][...]
        for j in range(3):
            dw = dot(n1, ins[1 + j][...], NT).astype(BF)
            for r in range(8):
                outs[r % 2 == 0][r // 2 * 3 + j] = dw[r * 128:(r + 1) * 128]

    return [n1t, *three], [(way, block, BF), (None, block, BF)], fn


def put(out, v):
    nb, rows = v.shape[0], out.shape[1]
    for k in range(out.shape[0] // nb):
        out[k * nb:(k + 1) * nb] = v[:, k * rows:(k + 1) * rows]


def whole(v):
    nb = v.shape[0] * v.shape[1] // 128
    return jnp.concatenate([v[k * nb:(k + 1) * nb] for k in range(128 // v.shape[1])], axis=1)


class Piece:
    def __init__(self, nb, keep, got, straight, copies):
        self.nb, self.keep, self.got = nb, keep, got
        self.plan = ["straight", "straight_sum"] if straight else ["sums", "second", "shard"]
        self.plan += {"halves": ["quarter", "quarter_back", "half_back"], "pairs": ["far"], "turns": []}[copies]
        self.copies = copies

    def step(self):
        return getattr(self, self.plan.pop(0))()

    def take(self, result):
        self.got = result

    def sums(self):
        nb = self.nb

        def fn(_, ins, outs):
            k, g = ins
            for out, half, pair in zip(outs, (0, 1, 0, 1), ((1, 3), (2, 3), (0, 2), (0, 1))):
                rows = slice(half * 64, half * 64 + 64)
                for n, j in enumerate(pair):
                    at = slice(j * nb, (j + 1) * nb)
                    out[n * nb:(n + 1) * nb] = plus(k[at, rows, :], g[at, rows, :]).astype(BF)

        out = (2 * nb, 64, 256)
        return [self.keep, self.got], [("x", out, BF), ("y", out, BF), (None, out, BF), (None, out, BF)], fn

    def second(self):
        nb = self.nb
        gx, gy, a, b = self.got
        self.rest = (a.part(0, nb), gx.part(0, nb), b.part(0, nb), gy.part(0, nb))

        def fn(_, ins, outs):
            outs[0][...] = plus(ins[0][...], ins[1][...]).astype(BF)
            outs[1][...] = plus(ins[2][...], ins[3][...]).astype(BF)

        out = (nb, 64, 256)
        ins = [v.part(nb, nb) for v in (a, gx, b, gy)]
        return ins, [("y", out, BF), ("x", out, BF)], fn

    def shard(self):
        a, gx, b, gy = self.rest

        def fn(where, ins, outs):
            a = plus(ins[0][...], ins[1][...], ins[2][...]).astype(BF)
            b = plus(ins[3][...], ins[4][...], ins[5][...]).astype(BF)
            self.first_copies(where, outs, a, b)

        return [a, gx, self.got[0], b, gy, self.got[1]], self.first_outs(), fn

    def straight(self):
        nb = self.nb

        def fn(_, ins, outs):
            for out, j in zip(outs, (1, 2, 3, 0)):
                at = slice(j * nb, (j + 1) * nb)
                put(out, plus(ins[0][at], ins[1][at]).astype(BF))

        out = (2 * nb, 64, 256)
        return [self.keep, self.got], [(way, out, BF) for way in ("x", "y", "both", None)], fn

    def straight_sum(self):
        nb = self.nb

        def fn(where, ins, outs):
            v = plus(*(r[...] for r in ins)).astype(BF)
            self.first_copies(where, outs, v[:nb], v[nb:])

        return list(self.got), self.first_outs(), fn

    def first_outs(self):
        nb = self.nb
        out = ((nb if self.copies == "halves" else 2 * nb), 64, 256)
        return [("turns" if self.copies == "turns" else "pair", out, BF), (None, out, BF)]

    def first_copies(self, where, outs, a, b):
        nb = self.nb
        if self.copies == "halves":
            odd = where[1] == 1
            outs[0][...] = jnp.where(odd, a, b)
            outs[1][...] = jnp.where(odd, b, a)
        else:
            for out in outs:
                out[:nb] = a
                out[nb:] = b

    def far(self):
        def fn(_, ins, outs):
            v = whole(plus(ins[0][...], ins[1][...]).astype(BF))
            for out in outs:
                put(out, v)

        out = (4 * self.nb, 32, 256)
        return list(self.got), [("far", out, BF), (None, out, BF)], fn

    def quarter(self):
        def fn(where, ins, outs):
            a = plus(ins[0][:, :32], ins[1][:, :32]).astype(BF)
            b = plus(ins[0][:, 32:], ins[1][:, 32:]).astype(BF)
            high = where[2] == 1
            outs[0][...] = jnp.where(high, a, b)
            outs[1][...] = jnp.where(high, b, a)

        out = (self.nb, 32, 256)
        return list(self.got), [("far", out, BF), (None, out, BF)], fn

    def quarter_back(self):
        def fn(_, ins, outs):
            v = plus(ins[0][...], ins[1][...]).astype(BF)
            outs[0][...] = v
            outs[1][...] = v

        out = (self.nb, 32, 256)
        return list(self.got), [("far", out, BF), (None, out, BF)], fn

    def half_back(self):
        def fn(where, ins, outs):
            high = where[2] == 1
            got, mine = ins[0][...], ins[1][...]
            for out in outs:
                out[:, :32] = jnp.where(high, got, mine)
                out[:, 32:] = jnp.where(high, mine, got)

        out = (self.nb, 64, 256)
        return list(self.got), [("pair", out, BF), (None, out, BF)], fn

    def final(self):
        nb, copies = self.nb, self.copies
        ins = (list(self.got[0]) + [self.got[1]]) if copies == "turns" else list(self.got)

        def value(where, ins, b):
            if copies != "halves":
                rows = ins[0].shape[1]
                return jnp.concatenate([plus(*(r[k * nb + b] for r in ins)) for k in range(128 // rows)]).astype(BF).astype(F32)
            odd = where[1] == 1
            got, mine = ins[0][b].astype(F32), ins[1][b].astype(F32)
            return jnp.concatenate([jnp.where(odd, got, mine), jnp.where(odd, mine, got)])

        return ins, value


def finish_kernel(groups, me_ref, x_ref, mg_ref, gain_ref, *refs):
    parts, refs = refs[:8], refs[8:]
    grads, (ig_ref, vec_ref, abs_s) = refs[:3 * groups], refs[3 * groups:]
    me = me_ref[0]
    i = pl.program_id(0)
    rows, width = x_ref.shape
    w = jnp.concatenate([r[...] for r in in_order(parts)], axis=0)
    pg = jnp.concatenate([grads[3 * g + j][...] for j in range(3) for g in range(groups)], axis=0)
    total = dot(pg, w, TT)
    for r in range(8):
        abs_s[:, pl.ds(block_of(me, r), 128)] = total[:, r * 128:(r + 1) * 128]
    grad = abs_s[...]
    hat, rstd = normalise(x_ref[...].astype(F32))
    sums = jnp.concatenate([jnp.sum(grad * hat, axis=0, keepdims=True), jnp.sum(grad, axis=0, keepdims=True)], axis=0)
    ig_ref[...] = mg_ref[...] + norm_back(hat, rstd, grad, gain_ref[...])

    @pl.when(i == 0)
    def _():
        vec_ref[...] = sums

    @pl.when(i > 0)
    def _():
        vec_ref[...] += sums


def finish(me, x, mg, gain, parts, grads, deps=()):
    rows, width = x.shape
    tile = pl.BlockSpec((T, width), lambda i: (i, 0))
    return pl.pallas_call(
        with_deps(functools.partial(finish_kernel, len(grads) // 3), 4 + len(parts) + len(grads), len(deps)),
        grid=(rows // T,), name="finish",
        in_specs=[SMEM, tile, tile, resident((1, width))] + [resident((p.shape[0], 3 * width)) for p in parts]
        + [pl.BlockSpec((g.shape[0], T), lambda i: (0, i)) for g in grads] + [ANY] * len(deps),
        out_specs=[tile, resident((2, width))],
        out_shape=[shape_of((rows, width), F32), shape_of((2, width), F32)],
        scratch_shapes=[pltpu.VMEM((T, width), F32)],
        compiler_params=params(), cost_estimate=cost(6 * rows * width * width, 34e6),
    )(me, x, mg, gain, *parts, *grads, *deps)


def flip(v, k):
    return lax.ppermute(v, "fsdp", [(i, i ^ k) for i in range(GROUPS)])


def xor_rows(v, me):
    for k in (1, 2, 4):
        turned = v.reshape((8 // (2 * k), 2, k) + v.shape[1:])[:, ::-1].reshape(v.shape)
        v = jnp.where((me & k) != 0, turned, v)
    return v


def split_full(full):
    m = full.shape[0] // 8
    return [full[r * m:(r + 1) * m] for r in PLACES]


def vector_sums(vec_one, vec_two, dists, buckets):
    def fn(where, ins, outs):
        by = jnp.concatenate([jnp.concatenate([d[:, u, :] for u in range(d.shape[1] - 1, -1, -1)], axis=1) for d in ins[2:-1]])
        onehot = (ins[-1][...] == lax.broadcasted_iota(jnp.int32, (BUCKETS, by.shape[1]), 0)).astype(F32)
        table = lax.dot_general(by, onehot, NT, precision=lax.Precision.HIGHEST, preferred_element_type=F32)
        table_s, row_s = outs[2:]
        table_s[...] = jnp.concatenate([jnp.concatenate([table[2 * r:2 * r + 1], table[2 * r + 1:2 * r + 2]], axis=1) for r in range(8)])
        row_s[...] = jnp.zeros_like(row_s)
        for out in outs[:2]:
            out[...] = jnp.zeros_like(out)
        for r in range(8):
            at = pl.ds(block_of(where[0], r), 128)
            for k in range(4):
                row_s[k // 2:k // 2 + 1, k % 2 * 128:(k % 2 + 1) * 128] = ins[k // 2][k % 2:k % 2 + 1, at]
            row_s[2:3, :64] = table_s[pl.ds(jnp.bitwise_xor(where[0], r), 1), :]
            outs[1 - r % 2][r // 2, :16, :] = row_s[...].astype(BF)

    out = (4, 128, 256)
    return [vec_one, vec_two, *dists, buckets], [
        ("core", out, BF), (None, out, BF), (None, (8, 64), F32), (None, (16, 256), F32)], fn


def vector_result(piece):
    mine, value = piece.final()

    def fn(where, ins, outs):
        v = value(where, ins, 0)
        for k in range(4):
            outs[k][...] = v[k // 2:k // 2 + 1, k % 2 * 128:(k % 2 + 1) * 128]
        outs[4][...] = v[2:3, :64]

    return mine, [(None, (1, 128), F32)] * 4 + [(None, (1, 64), F32)], fn


def feed_result(one, pieces):
    finals = [p.final() for p in pieces]

    def fn(where, ins, outs):
        for c in range(2):
            base = c * 256
            for b in range(8):
                col = (b * CHUNKS + c) * 128
                outs[0][:, col:col + 128] = ins[0][base:base + 128, b * 128:(b + 1) * 128].astype(F32)
            outs[1][c * 128:(c + 1) * 128, :] = ins[0][base + 128:base + 256, :].astype(F32)
        at = 1
        for c, (mine, value) in zip((2, 3), finals):
            refs = ins[at:at + len(mine)]
            at += len(mine)
            for b in range(4):
                v = value(where, refs, b)
                for k in range(2):
                    col = ((2 * b + k) * CHUNKS + c) * 128
                    outs[0][:, col:col + 128] = v[:, k * 128:(k + 1) * 128]
                outs[1][c * 128:(c + 1) * 128, b * 256:(b + 1) * 256] = value(where, refs, 4 + b)

    return [one] + [v for mine, _ in finals for v in mine], [(None, (128, 4096), F32), (None, (512, 1024), F32)], fn


def project_result(out_piece, pieces):
    finals = [p.final() for p in [out_piece] + pieces]

    def fn(where, ins, outs):
        at = 0
        for g, (mine, value) in enumerate(finals):
            refs = ins[at:at + len(mine)]
            at += len(mine)
            for b in range(3 if g else 4):
                col = (b * HEAD_GROUPS + g - 1) * 256 if g else b * 256
                outs[0 if g else 1][:, col:col + 256] = value(where, refs, b)

    return [v for mine, _ in finals for v in mine], [(None, (128, 3072), F32), (None, (128, 1024), F32)], fn


def copy_turns(v, count):
    return [lax.ppermute(v, "rep", [(i, (i + k) % count) for i in range(count)]) for k in range(1, count)]


def per_device(n_fsdp, n_rep, inputs, lengths, bucket_table, ln1_gain, ln1_shift, w_qkv, rel_bias, w_out, ln2_gain, ln2_shift,
               w_in, w_down, cotangent):
    near = n_fsdp == GROUPS and n_rep == 4
    _, slots, width = inputs.shape
    hidden = w_in.shape[1]
    me = lax.axis_index("fsdp").astype(jnp.int32) if near else jnp.int32(0)
    me1 = me.reshape(1)
    x = inputs.reshape(slots, width)
    cot = cotangent.reshape(slots, width)
    full = lambda w: lax.all_gather(w, "fsdp", axis=0, tiled=True)

    if near:
        piece, own = lead(w_qkv, w_out, ln1_gain, ln1_shift, ln2_gain, ln2_shift, rel_bias)
        small = jnp.concatenate([own] + [flip(own, k) for k in (2, 4, 6)])
        small = jnp.stack([small, flip(small, 1)], axis=1).reshape(8, -1)
        r2, r4 = flip(piece, 2), flip(piece, 4)
        h2, h4 = halves(r2, r4)
        r6a, r6b = flip(h2, 4), flip(h4, 2)
        n1t, og, vecs, base = prepare(me1, lengths, x, cot, bucket_table[None], small, (h2, h4))
        ffn_w = [full(v.reshape(512, 1024)).reshape(8, 2, 256, 1024) for v in pack(w_in, w_down, (h2, h4))]
        parts = [piece, r2, r4, join(r6a, r6b, (n1t,))]
        parts = parts + [flip(v, 1) for v in parts]
    else:
        n = ln1_gain.shape[0]
        small = full(jnp.concatenate([ln1_gain, ln1_shift, ln2_gain, ln2_shift, rel_bias])[None])
        small = jnp.concatenate([small[:, i * n:(i + 1) * n].reshape(8, 128) for i in range(4)] + [small[:, 4 * n:].reshape(8, 64)], axis=1)
        n1t, og, vecs, base = prepare(me1, lengths, x, cot, bucket_table[None], small)
        parts = split_full(jnp.concatenate([full(w_qkv), full(w_out)], axis=1))
        wi_c = full(w_in).reshape(8, width // 8, 8, CHUNKS, 128)
        wd_c = full(w_down).reshape(8, CHUNKS, 128, width)
        chunk = [jnp.concatenate([wi_c[:, :, :, c].reshape(8, width // 8, 1024), wd_c[:, c]], axis=1) for c in range(CHUNKS)]
        ffn_w = [jnp.stack(chunk[2 * h:2 * h + 2], axis=1) for h in range(2)]
    n = ln1_gain.shape[0]
    gain_one, shift_one, gain_two, shift_two = (vecs[i:i + 1] for i in range(4))
    qkv = project(n1t, parts)
    o, lt = attend(me1, lengths, base, qkv)
    at = o.reshape(width, slots)
    mid, n2, n2t = middle_of(me1, at, x, gain_two, shift_two, parts)
    grads, dists = [], []
    rep = lax.axis_index("rep").astype(jnp.int32)
    where = jnp.stack([me, rep % 2, rep // 2])
    per = HEADS // HEAD_GROUPS
    last = ffn_w[1]

    def back(k, deps=()):
        *three, dist = attend_back(me1, lengths, base, qkv, o, do, lt, k * per, per, deps)
        three = [v.reshape(per * HEAD_DIM, slots) for v in three]
        grads.extend(three)
        dists.append(dist)
        return three

    def slot(pieces, before=(), after=(), deps=()):
        result, made = staged(where, list(before) + [p.step() for p in pieces] + list(after), deps)
        for p, r in zip(pieces, result[len(before):]):
            p.take(r)
        return result[:len(before)] + result[len(before) + len(pieces):], made

    g, hid1, one = feed((0, 1), True, me1, n2, n2t, og, ffn_w[0])
    if near:
        one = lax.psum_scatter(one.reshape(8 * 512, 1024), "fsdp", scatter_dimension=0, tiled=True)
        blocks = lambda v: v.reshape((-1,) + v.shape[2:])
        start = lambda nb, away, keep, *plan: Piece(nb, Part(blocks(keep)), Part(flip(blocks(away), 1)), *plan)
        g, hid2, away, keep = feed((0,), False, me1, n2, n2t, og, last, (g,))
        f2 = start(8, away, keep, False, "halves")
        g, hid3, away, keep = feed((1,), False, me1, n2, n2t, og, last, (g,))
        f3 = start(8, away, keep, False, "halves")
        _, made = slot([f2], deps=(g,))
        mg, do, away, keep, vec_two = middle_back(me1, mid, g, og, at, gain_two, parts, made)
        do = do.reshape(HEADS, HEAD_DIM, slots)
        wo = start(4, away, keep, False, "pairs")
        _, made = slot([f3], deps=(mg,))
        three = back(0, made)
        ((got, keep),), made = slot([f2, f3], [project_back(n1t, three, "core")], deps=(one,))
        one = lax.psum(one, "rep")
        q0 = Piece(3, keep, got, False, "pairs")
        three = back(1, made)
        ((got, keep),), made = slot([f2, f3, wo, q0], [project_back(n1t, three, "core")])
        q1 = Piece(3, keep, got, False, "pairs")
        three = back(2, made)
        ((got, keep),), made = slot([f2, f3, wo, q0, q1], [project_back(n1t, three, "core")])
        q2 = Piece(3, keep, got, True, "pairs")
        three = back(3, made)
        ((got, keep),), made = slot([f2, f3, wo, q0, q1, q2], [project_back(n1t, three, "core")])
        q3 = Piece(3, keep, got, True, "pairs")
        input_grad, vec_one = finish(me1, x, mg, gain_one, parts, grads, made)
        ((got, keep, *_),), made = slot([], [vector_sums(vec_one, vec_two, dists, bucket_table[None])])
        vec = Piece(1, keep, got, True, "pairs")
        came = lambda *pieces: tuple(p.got[0].array for p in pieces)
        _, made = slot([q3, q2, f2, f3, wo, q0, q1, vec], deps=(one,))
        outputs = output(me1, lengths, mid, [hid1, hid2, hid3], ffn_w, made)
        ((in_grad, down_grad),), made = slot([q3, vec, q2, q1], [], [feed_result(one, [f2, f3])], deps=(outputs,) + came(wo, q0))
        _, made = slot([q3, vec], deps=came(q2, q1))
        ((qkv_grad, out_g), tiny), _ = slot([], [project_result(wo, [q0, q1, q2, q3]), vector_result(vec)])
        in_grad, down_grad, qkv_grad, out_g = (v.array for v in (in_grad, down_grad, qkv_grad, out_g))
        tiny = [v.array[0] for v in tiny]
    else:
        g, hid2, two = feed((0, 1), True, me1, n2, n2t, og, last, (g,))
        mg, do, away, keep, vec_two = middle_back(me1, mid, g, og, at, gain_two, parts)
        do = do.reshape(HEADS, HEAD_DIM, slots)
        pieces = [staged(where, [project_back(n1t, back(k), None)])[0][0] for k in range(HEAD_GROUPS)]
        input_grad, vec_one = finish(me1, x, mg, gain_one, parts, grads)
        outputs = output(me1, lengths, mid, [hid1, hid2], ffn_w)
        onehot = (bucket_table[:, None] == lax.iota(jnp.int32, BUCKETS)[None, :]).astype(F32)
        distance_total = jnp.concatenate(dists)[:, ::-1].reshape(HEADS, slots)
        table_grad = jnp.dot(distance_total, onehot, precision=lax.Precision.HIGHEST, preferred_element_type=F32)
        vec = jnp.concatenate([v.reshape(n_fsdp, -1) for v in (vec_one[0], vec_one[1], vec_two[0], vec_two[1], table_grad)], axis=1)
        reduced = lambda v: lax.psum(lax.psum_scatter(v, "fsdp", scatter_dimension=0, tiled=True), "rep")
        tiny = reduced(vec)[0]
        tiny = [tiny[k * n:(k + 1) * n] for k in range(4)] + [tiny[4 * n:]]
        stack = jnp.concatenate([one, two], axis=1)
        in_grad = reduced(stack[:, :, :128].reshape(8, CHUNKS, 128, 8, 128).transpose(0, 2, 3, 1, 4).reshape(width, hidden))
        down_grad = reduced(stack[:, :, 128:].reshape(hidden, width))
        whole = lambda away, keep: jnp.stack([keep, away], axis=1).reshape((8,) + keep.shape[1:]).swapaxes(1, 2)
        out_g = reduced(whole(away, keep).reshape(width, width))
        columns = [whole(*(v.array.reshape(4, 3, 128, 256) for v in p)) for p in pieces]
        qkv_grad = reduced(jnp.stack(columns, axis=3).reshape(width, 3 * width))
    return (outputs.reshape(inputs.shape), input_grad.reshape(inputs.shape), tiny[0], tiny[1], qkv_grad.astype(F32),
            tiny[4], out_g.astype(F32), tiny[2], tiny[3], in_grad.astype(F32), down_grad.astype(F32))


def solution(mesh):
    rows = P(("rep", "fsdp"), None, None)
    vec = P("fsdp")
    mat = P("fsdp", None)
    return jax.shard_map(
        functools.partial(per_device, mesh.shape["fsdp"], mesh.shape["rep"]),
        mesh=mesh,
        in_specs=(rows, P(("rep", "fsdp")), P(), vec, vec, mat, vec, mat, vec, vec, mat, mat, rows),
        out_specs=(rows, rows, vec, vec, mat, vec, mat, vec, vec, mat, mat),
        check_vma=False,
    )
```

time: 513 us -> 460 us (0.90)
  waiting for transfers between devices: 131 us -> 109 us
  Pallas kernels: 287 us -> 273 us
  starting transfers between devices: 54.4 us -> 43.9 us
  local copies, waits for them, and re-layouts: 16.5 us -> 11.2 us
    ppermute x35 -> x36, waiting for transfers between devices: 78.7 us -> 53.2 us  [flip(): return lax.ppermute(v, 'fsdp', [(i, i ^ k) for i in range(GROUPS)])]
    pallas_call x1, Pallas kernels: 34.7 us -> 20.8 us  [attend(): pl.pallas_call(attend_kernel, name='attend', grid_spec=pltpu.PrefetchScal...]
    ppermute x18 -> x9, starting transfers between devices: 25.4 us -> 13.2 us  [send(): return lax.ppermute(v, 'rep', [(i, i ^ k) for i in range(4)])]
    ppermute x18 -> x9, waiting for transfers between devices: 44 us -> 53.7 us  [send(): return lax.ppermute(v, 'rep', [(i, i ^ k) for i in range(4)])]
    psum x1, waiting for transfers between devices: 7.63 us -> 0.01 us  [per_device(): one = lax.psum(one, 'rep')]
    pallas_call x15 -> x17, Pallas kernels: 144 us -> 150 us  [the longest x3 74.7 us: feed(): pl.pallas_call(functools.partial(feed_kernel, chunks, stacked, counts), n...]
    unnamed x106 -> x80, local copies, waits for them, and re-layouts: 13.4 us -> 9.96 us
    ppermute x35 -> x36, starting transfers between devices: 28.8 us -> 30.6 us  [flip(): return lax.ppermute(v, 'fsdp', [(i, i ^ k) for i in range(GROUPS)])]
  transfers between devices with their start and end apart: 57 -> 49, of which waited for: 25 -> 18; matrix products, arithmetic and copies ran while one was open for 1% -> 0% of each run, Pallas kernels for 46% -> 55%
where the time goes in v3:
time: 460 us; the launch traced here: 453 us
  Pallas kernels  273 us (59%)
  waiting for transfers between devices  109 us (24%)
  starting transfers between devices  43.9 us (10%)
  between operations  15.3 us (3%)
  local copies, waits for them, and re-layouts  11.2 us (2%)
    pallas_call x3, Pallas kernels, feed(): pl.pallas_call(functools.partial(feed_kernel, chunks, stacked, counts), n...  74.7 us
    pallas_call x11, Pallas kernels, staged(): pl.pallas_call(functools.partial(staged_kernel, steps, places, len(parts)...  54 us
    ppermute x9, waiting for transfers between devices, send(): return lax.ppermute(v, 'rep', [(i, i ^ k) for i in range(4)])  53.7 us
    ppermute x36, waiting for transfers between devices, flip(): return lax.ppermute(v, 'fsdp', [(i, i ^ k) for i in range(GROUPS)])  53.2 us
    pallas_call x4, Pallas kernels, attend_back(): pl.pallas_call(with_deps(attend_back_kernel, 9, len(deps)), name='attend_...  39.7 us
    ppermute x36, starting transfers between devices, flip(): return lax.ppermute(v, 'fsdp', [(i, i ^ k) for i in range(GROUPS)])  30.6 us
    pallas_call x1, Pallas kernels, attend(): pl.pallas_call(attend_kernel, name='attend', grid_spec=pltpu.PrefetchScal...  20.8 us
    pallas_call x1, Pallas kernels, output(): pl.pallas_call(with_deps(output_kernel, 5 + len(hids), len(deps)), grid=(...  15.9 us
  transfers between devices with their start and end apart: 49, of which 18 were waited for; matrix products, arithmetic and copies ran while one was open for 0% of the time, Pallas kernels for 55%

profile of v3, /device:TPU:0, one launch (start us, length us, event | category | flops | bytes accessed | tf_op | source)
XLA Modules:
  0.0 453.3 jit_solution(15221986330350313672)
XLA Ops:
  7.2 2.3 lead.1
  9.5 3.0 collective-permute-start.5
  12.5 1.5 collective-permute-start.4
  14.0 21.9 %collective-permute-done.5.b_ref.refs_2_.refs_7_.refs_8_.refs_6_ = bf16[128,4096]{1,0:T(8,128)(2,1)S(1)} collective-permute-done((bf16[128,4096]{1,0:T(8,128)(2,1)}, bf16[128,4096]{1,0:T(8,128)(2,1)S(1)}, u32[]{:S(2)}, u32[]{:S(2)}) %collective-permute-start.5) | collective-permute-done | bytes 1048608 | tf_op jit(solution)/shard_map/ppermute | solution.py:885
  35.9 1.5 collective-permute-done.4.a_ref.refs_1_.refs_6_.refs_7_.refs_5_
  38.3 2.5 halves.1
  40.9 3.2 pack.1
  44.9 1.3 collective-permute-start.6
  46.2 1.5 collective-permute-start.7
  49.7 1.5 collective-permute-start
  51.9 12.9 %collective-permute-done.2 = bf16[1,576]{1,0:T(2,128)(2,1)S(1)} collective-permute-done((bf16[1,576]{1,0:T(2,128)(2,1)S(1)}, bf16[1,576]{1,0:T(2,128)(2,1)S(1)}, u32[]{:S(2)}, u32[]{:S(2)}) %collective-permute-start.2) | collective-permute-done | bytes 1184 | tf_op jit(solution)/shard_map/ppermute | solution.py:885
  65.4 2.0 collective-permute-done.3
  68.5 6.0 %prepare.1 = (bf16[1024,1024]{1,0:T(8,128)(2,1)}, bf16[1024,1024]{1,0:T(8,128)(2,1)}, f32[4,1024]{1,0:T(4,128)}, f32[16,4,256]{2,1,0:T(4,128)}) custom-call(s32[1]{0:T(128)} %bitcast.refs_0_.me_ref, s32[1]{0:T(128)S(6)} %copy.26.refs_1_.len_ref, bf16[1024,1024]{1,0:T(8,128)(2,1)} %bitcast.46, bf16[1024,1024]{1,0:T(8,128)(2,1)} %bitcast.64, ...), custom_call_target="tpu_custom_call" | custom-call | flops 1000000000 | bytes 8000000 | tf_op jit(solution)/shard_map/prepare/pallas_call | solution.py:106
  74.5 2.3 join.1.refs_3_.refs_8_.refs_9_.refs_7_
  77.5 3.7 collective-permute-done.11.refs_7_.refs_12_.refs_13_.refs_11_
  81.2 11.7 %project.1.q_ref.k_ref.v_ref.refs_3_.refs_4_.refs_5_ = bf16[48,64,1024]{2,1,0:T(8,128)(2,1)} custom-call(bf16[1024,1024]{1,0:T(8,128)(2,1)} %get-tuple-element.142.refs_2_.n1t_ref.refs_0_, bf16[128,4096]{1,0:T(8,128)(2,1)} %get-tuple-element.138.refs_0_.refs_5_.refs_6_.refs_4_, bf16[128,4096]{1,0:T(8,128)(2,1)} %copy-done.2, bf16[128,4096]{1,0:T(8,128)(2,1)} %copy-done, ...), custom_call_target="tpu_custom_call" | custom-call | flops 6442450944 | bytes 14000000 | tf_op jit(solution)/shard_map/project/pallas_call | solution.py:194
  92.9 20.8 %attend.1 = (bf16[16,64,1024]{2,1,0:T(8,128)(2,1)}, f32[16,1,1024]{2,1,0:T(1,128)}) custom-call(s32[1]{0:T(128)} %bitcast.refs_0_.me_ref, s32[1]{0:T(128)S(6)} %copy.26.refs_1_.len_ref, f32[16,4,256]{2,1,0:T(4,128)} %get-tuple-element.141.base_ref.refs_2_, bf16[48,64,1024]{2,1,0:T(8,128)(2,1)} %project.1.q_ref.k_ref.v_ref.refs_3_.refs_4_.refs_5_, ...), custom_call_target="tpu_custom_call" | custom-call | flops 30000001024 | bytes 10000000 | tf_op jit(solution)/shard_map/attend/pallas_call | solution.py:258
  113.7 9.6 %middle.1 = (f32[1024,1024]{1,0:T(8,128)}, bf16[1024,1024]{1,0:T(8,128)(2,1)}, bf16[1024,1024]{1,0:T(8,128)(2,1)}) custom-call(s32[1]{0:T(128)} %bitcast.refs_0_.me_ref, bf16[1024,1024]{1,0:T(8,128)(2,1)} %bitcast.55, bf16[1024,1024]{1,0:T(8,128)(2,1)} %bitcast.47, f32[1,1024]{1,0:T(1,128)} %get-tuple-element.265.refs_3_.refs_5_, ...), custom_call_target="tpu_custom_call" | custom-call | flops 2147483648 | bytes 14000000 | tf_op jit(solution)/shard_map/middle/pallas_call | solution.py:372
  123.4 34.0 %feed.3 = (f32[1024,1024]{1,0:T(8,128)}, bf16[1024,2048]{1,0:T(8,128)(2,1)}, bf16[8,2,256,1024]{3,2,1,0:T(8,128)(2,1)}) custom-call(s32[1]{0:T(128)} %bitcast.refs_0_.me_ref, bf16[1024,1024]{1,0:T(8,128)(2,1)} %get-tuple-element.146.n2_h, bf16[1024,1024]{1,0:T(8,128)(2,1)} %get-tuple-element.147.n2t_h, bf16[1024,1024]{1,0:T(8,128)(2,1)} %get-tuple-element.148.og_h.refs_3_, ...), custom_call_target="tpu_custom_call" | custom-call | flops 35999997952 | bytes 25000000 | tf_op jit(solution)/shard_map/feed/pallas_call | solution.py:485
  157.4 1.7 all-gather.5.cloned.1.call-done
  159.1 20.6 %feed.4 = (f32[1024,1024]{1,0:T(8,128)}, bf16[1024,1024]{1,0:T(8,128)(2,1)}, bf16[4,8,128,256]{3,2,1,0:T(8,128)(2,1)}, bf16[4,8,128,256]{3,2,1,0:T(8,128)(2,1)}) custom-call(s32[1]{0:T(128)} %bitcast.refs_0_.me_ref, bf16[1024,1024]{1,0:T(8,128)(2,1)} %get-tuple-element.146.n2_h, bf16[1024,1024]{1,0:T(8,128)(2,1)} %get-tuple-element.147.n2t_h, ...), custom_call_target="tpu_custom_call" | custom-call | flops 17999998976 | bytes 25000000 | tf_op jit(solution)/shard_map/feed/pallas_call | solution.py:485
  180.0 20.2 %feed.5 = (f32[1024,1024]{1,0:T(8,128)}, bf16[1024,1024]{1,0:T(8,128)(2,1)}, bf16[4,8,128,256]{3,2,1,0:T(8,128)(2,1)}, bf16[4,8,128,256]{3,2,1,0:T(8,128)(2,1)}) custom-call(s32[1]{0:T(128)} %bitcast.refs_0_.me_ref, bf16[1024,1024]{1,0:T(8,128)(2,1)} %get-tuple-element.146.n2_h, bf16[1024,1024]{1,0:T(8,128)(2,1)} %get-tuple-element.147.n2t_h, ...), custom_call_target="tpu_custom_call" | custom-call | flops 17999998976 | bytes 25000000 | tf_op jit(solution)/shard_map/feed/pallas_call | solution.py:485
  201.1 4.6 %staged.11 = (bf16[16,64,256]{2,1,0:T(8,128)(2,1)}, bf16[16,64,256]{2,1,0:T(8,128)(2,1)}, bf16[16,64,256]{2,1,0:T(8,128)(2,1)}, bf16[16,64,256]{2,1,0:T(8,128)(2,1)}) custom-call(s32[3]{0:T(128)} %pad_add_fusion.where_ref, bf16[32,128,256]{2,1,0:T(8,128)(2,1)} %bitcast.103, bf16[32,128,256]{2,1,0:T(8,128)(2,1)} %collective-permute-done.12.refs_1_, ...), custom_call_target="tpu_custom_call" | custom-call | flops 3000000000 | bytes 10000000 | tf_op jit(solution)/shard_map/staged/pallas_call | solution.py:644
  205.8 1.6 collective-permute-start.14
  208.1 14.9 %middle_back.1 = (f32[1024,1024]{1,0:T(8,128)}, bf16[1024,1024]{1,0:T(8,128)(2,1)}, bf16[4,4,128,256]{3,2,1,0:T(8,128)(2,1)}, bf16[4,4,128,256]{3,2,1,0:T(8,128)(2,1)}, f32[2,1024]{1,0:T(2,128)}) custom-call(s32[1]{0:T(128)} %bitcast.refs_0_.me_ref, f32[1024,1024]{1,0:T(8,128)} %get-tuple-element.145.refs_1_.refs_2_, ...), custom_call_target="tpu_custom_call" | custom-call | flops 4294967296 | bytes 24000000 | tf_op jit(solution)/shard_map/middle_back/pallas_call | solution.py:578
  223.1 1.3 copy-done.22
  224.4 4.4 staged.12
  230.3 9.8 %attend_back.4 = (bf16[4,64,1024]{2,1,0:T(8,128)(2,1)}, bf16[4,64,1024]{2,1,0:T(8,128)(2,1)}, bf16[4,64,1024]{2,1,0:T(8,128)(2,1)}, f32[4,4,256]{2,1,0:T(4,128)}) custom-call(s32[1]{0:T(128)} %bitcast.refs_0_.me_ref, s32[1]{0:T(128)S(6)} %copy.26.refs_1_.len_ref, f32[16,4,256]{2,1,0:T(4,128)} %get-tuple-element.141.base_ref.refs_2_, ...), custom_call_target="tpu_custom_call" | custom-call | flops 9600000000 | bytes 4800000 | tf_op jit(solution)/shard_map/attend_back/pallas_call | solution.py:339
  240.2 6.9 %collective-permute-done.16.refs_9_.refs_11_ = bf16[16,64,256]{2,1,0:T(8,128)(2,1)S(1)} collective-permute-done((bf16[16,64,256]{2,1,0:T(8,128)(2,1)}, bf16[16,64,256]{2,1,0:T(8,128)(2,1)S(1)}, u32[]{:S(2)}, u32[]{:S(2)}) %collective-permute-start.16) | collective-permute-done | bytes 524320 | tf_op jit(solution)/shard_map/ppermute | solution.py:885
  248.1 6.1 %staged.13 = (bf16[12,128,256]{2,1,0:T(8,128)(2,1)}, bf16[12,128,256]{2,1,0:T(8,128)(2,1)}, bf16[16,64,256]{2,1,0:T(8,128)(2,1)}, bf16[16,64,256]{2,1,0:T(8,128)(2,1)}) custom-call(s32[3]{0:T(128)} %pad_add_fusion.where_ref, bf16[1024,1024]{1,0:T(8,128)(2,1)} %get-tuple-element.142.refs_2_.n1t_ref.refs_0_, bf16[256,1024]{1,0:T(8,128)(2,1)} %bitcast.74, ...), custom_call_target="tpu_custom_call" | custom-call | flops 3000000000 | bytes 10000000 | tf_op jit(solution)/shard_map/staged/pallas_call | solution.py:644
  254.3 1.5 collective-permute-start.18
  256.4 10.1 %attend_back.5 = (bf16[4,64,1024]{2,1,0:T(8,128)(2,1)}, bf16[4,64,1024]{2,1,0:T(8,128)(2,1)}, bf16[4,64,1024]{2,1,0:T(8,128)(2,1)}, f32[4,4,256]{2,1,0:T(4,128)}) custom-call(s32[1]{0:T(128)} %bitcast.refs_0_.me_ref, s32[1]{0:T(128)S(6)} %copy.26.refs_1_.len_ref, f32[16,4,256]{2,1,0:T(4,128)} %get-tuple-element.141.base_ref.refs_2_, ...), custom_call_target="tpu_custom_call" | custom-call | flops 9600000000 | bytes 4800000 | tf_op jit(solution)/shard_map/attend_back/pallas_call | solution.py:339
  266.5 1.5 collective-permute-done.18.refs_6_.refs_12_
  270.2 6.8 %staged.14 = (bf16[12,128,256]{2,1,0:T(8,128)(2,1)}, bf16[12,128,256]{2,1,0:T(8,128)(2,1)}, bf16[16,64,256]{2,1,0:T(8,128)(2,1)}, bf16[8,64,256]{2,1,0:T(8,128)(...) custom-call(s32[3]{0:T(128)} %pad_add_fusion.where_ref, ...), custom_call_target="tpu_custom_call" | custom-call | flops 3000000000 | bytes 10000000 | tf_op jit(solution)/shard_map/staged/pallas_call | solution.py:644
  278.8 1.5 collective-permute-start.22
  280.3 9.8 %attend_back.6 = (bf16[4,64,1024]{2,1,0:T(8,128)(2,1)}, bf16[4,64,1024]{2,1,0:T(8,128)(2,1)}, bf16[4,64,1024]{2,1,0:T(8,128)(2,1)}, f32[4,4,256]{2,1,0:T(4,128)}) custom-call(s32[1]{0:T(128)} %bitcast.refs_0_.me_ref, s32[1]{0:T(128)S(6)} %copy.26.refs_1_.len_ref, f32[16,4,256]{2,1,0:T(4,128)} %get-tuple-element.141.base_ref.refs_2_, ...), custom_call_target="tpu_custom_call" | custom-call | flops 9600000000 | bytes 4800000 | tf_op jit(solution)/shard_map/attend_back/pallas_call | solution.py:339
  290.2 2.6 collective-permute-done.22.refs_4_.refs_6_
  293.8 6.5 %staged.15 = (bf16[12,128,256]{2,1,0:T(8,128)(2,1)}, bf16[12,128,256]{2,1,0:T(8,128)(2,1)}, bf16[16,32,256]{2,1,0:T(8,128)(2,1)}, bf16[8,32,256]{2,1,0:T(8,128)(...) custom-call(s32[3]{0:T(128)} %pad_add_fusion.where_ref, ...), custom_call_target="tpu_custom_call" | custom-call | flops 3000000000 | bytes 10000000 | tf_op jit(solution)/shard_map/staged/pallas_call | solution.py:644
  300.3 2.5 collective-permute-start.26
  302.8 1.5 collective-permute-start.27
  304.3 1.5 collective-permute-start.28
  305.7 10.0 %attend_back.7 = (bf16[4,64,1024]{2,1,0:T(8,128)(2,1)}, bf16[4,64,1024]{2,1,0:T(8,128)(2,1)}, bf16[4,64,1024]{2,1,0:T(8,128)(2,1)}, f32[4,4,256]{2,1,0:T(4,128)}) custom-call(s32[1]{0:T(128)} %bitcast.refs_0_.me_ref, s32[1]{0:T(128)S(6)} %copy.26.refs_1_.len_ref, f32[16,4,256]{2,1,0:T(4,128)} %get-tuple-element.141.base_ref.refs_2_, ...), custom_call_target="tpu_custom_call" | custom-call | flops 9600000000 | bytes 4800000 | tf_op jit(solution)/shard_map/attend_back/pallas_call | solution.py:339
  315.8 6.2 %collective-permute-done.26.refs_4_.refs_6_ = bf16[16,32,256]{2,1,0:T(8,128)(2,1)S(1)} collective-permute-done((bf16[16,32,256]{2,1,0:T(8,128)(2,1)}, bf16[16,32,256]{2,1,0:T(8,128)(2,1)S(1)}, u32[]{:S(2)}, u32[]{:S(2)}) %collective-permute-start.26) | collective-permute-done | bytes 262176 | tf_op jit(solution)/shard_map/ppermute | solution.py:669
  323.2 6.8 %staged.16 = (bf16[12,128,256]{2,1,0:T(8,128)(2,1)}, bf16[12,128,256]{2,1,0:T(8,128)(2,1)}, bf16[16,32,256]{2,1,0:T(8,128)(2,1)}, bf16[8,32,256]{2,1,0:T(8,128)(...) custom-call(s32[3]{0:T(128)} %pad_add_fusion.where_ref, ...), custom_call_target="tpu_custom_call" | custom-call | flops 3000000000 | bytes 10000000 | tf_op jit(solution)/shard_map/staged/pallas_call | solution.py:644
  330.0 2.5 collective-permute-start.33
  333.5 15.1 %finish.1 = (f32[1024,1024]{1,0:T(8,128)}, f32[2,1024]{1,0:T(2,128)}) custom-call(s32[1]{0:T(128)} %bitcast.refs_0_.me_ref, bf16[1024,1024]{1,0:T(8,128)(2,1)} %bitcast.48, f32[1024,1024]{1,0:T(8,128)} %get-tuple-element.167.refs_2_, f32[1,1024]{1,0:T(1,128)} %get-tuple-element.263.refs_3_, ...), custom_call_target="tpu_custom_call" | custom-call | flops 6442450944 | bytes 34000000 | tf_op jit(solution)/shard_map/finish/pallas_call | solution.py:872
  348.7 1.6 collective-permute-start.35
  350.3 2.7 staged.17
  353.3 1.5 collective-permute-done.36.refs_21_
  354.9 6.8 %collective-permute-done.35.refs_10_.refs_12_ = bf16[14,64,256]{2,1,0:T(8,128)(2,1)S(1)} collective-permute-done((bf16[14,64,256]{2,1,0:T(8,128)(2,1)S(1)}, bf16[14,64,256]{2,1,0:T(8,128)(2,1)S(1)}, u32[]{:S(2)}, u32[]{:S(2)}) %collective-permute-start.35) | collective-permute-done | bytes 458784 | tf_op jit(solution)/shard_map/ppermute | solution.py:669
  362.7 4.3 staged.18
  367.0 1.6 collective-permute-start.41
  368.6 1.7 collective-permute-start.38
  370.3 1.5 collective-permute-start.39
  372.1 1.7 collective-permute-start.37
  373.7 15.9 %output.1.refs_17_ = bf16[1024,1024]{1,0:T(8,128)(2,1)} custom-call(s32[1]{0:T(128)} %bitcast.refs_0_.me_ref, s32[1]{0:T(128)S(6)} %copy.26.refs_1_.len_ref, f32[1024,1024]{1,0:T(8,128)} %get-tuple-element.145.refs_1_.refs_2_, bf16[1024,2048]{1,0:T(8,128)(2,1)} %get-tuple-element.150.refs_3_, bf16[1024,1024]{1,0:T(8,128)(2,1)} %get-tuple-element.153.refs_4_, ...), custom_call_target="tpu_custom_call" | custom-call | flops 8999999488 | bytes 20000000 | tf_op jit(solution)/shard_map/output/pallas_call | solution.py:526
  389.7 8.5 %collective-permute-done.37.refs_18_.refs_19_.refs_0_.refs_2_ = bf16[28,32,256]{2,1,0:T(8,128)(2,1)S(1)} collective-permute-done((bf16[28,32,256]{2,1,0:T(8,128)(2,1)}, bf16[28,32,256]{2,1,0:T(8,128)(2,1)S(1)}, u32[]{:S(2)}, u32[]{:S(2)}) %collective-permute-start.37) | collective-permute-done | bytes 458784 | tf_op jit(solution)/shard_map/ppermute | solution.py:669
  400.0 5.4 %staged.19 = (bf16[8,64,256]{2,1,0:T(8,128)(2,1)}, bf16[6,64,256]{2,1,0:T(8,128)(2,1)}, bf16[2,64,256]{2,1,0:T(8,128)(2,1)}, bf16[24,32,256]{2,1,0:T(8,128)(2,1)...) custom-call(s32[3]{0:T(128)} %pad_add_fusion.where_ref, ...), custom_call_target="tpu_custom_call" | custom-call | flops 3000000000 | bytes 10000000 | tf_op jit(solution)/shard_map/staged/pallas_call | solution.py:644
  405.4 3.2 collective-permute-start.42
  409.2 12.8 %collective-permute-done.43.refs_0_.refs_2_ = bf16[8,64,256]{2,1,0:T(8,128)(2,1)S(1)} collective-permute-done((bf16[8,64,256]{2,1,0:T(8,128)(2,1)}, bf16[8,64,256]{2,1,0:T(8,128)(2,1)S(1)}, u32[]{:S(2)}, u32[]{:S(2)}) %collective-permute-start.43) | collective-permute-done | bytes 262176 | tf_op jit(solution)/shard_map/ppermute | solution.py:669
  422.0 3.4 collective-permute-done.42.refs_4_.refs_5_.refs_6_
  426.1 2.6 staged.20
  429.2 12.7 %collective-permute-done.44.refs_8_.refs_10_ = bf16[16,32,256]{2,1,0:T(8,128)(2,1)S(1)} collective-permute-done((bf16[16,32,256]{2,1,0:T(8,128)(2,1)}, bf16[16,32,256]{2,1,0:T(8,128)(2,1)S(1)}, u32[]{:S(2)}, u32[]{:S(2)}) %collective-permute-start.44) | collective-permute-done | bytes 262176 | tf_op jit(solution)/shard_map/ppermute | solution.py:669
  442.6 3.9 staged.21
  (154 shorter events, 24.8 us)
Async XLA Ops:
  7.2 116.2 %all-gather.3.cloned.1.call-start = ((), (), s32[]{:S(2)}) async-start(), calls=%async_computation.1 | async-start | bytes 9437184 | tf_op jit(solution)/shard_map/all_gather | solution.py:986
  9.5 26.3 %collective-permute-start.5 = (bf16[128,4096]{1,0:T(8,128)(2,1)}, bf16[128,4096]{1,0:T(8,128)(2,1)S(1)}, u32[]{:S(2)}, u32[]{:S(2)}) collective-permute-start(bf16[128,4096]{1,0:T(8,128)(2,1)} %get-tuple-element.138.refs_0_.refs_5_.refs_6_.refs_4_), channel_id=1, source_target_pairs={{0,4},{1,5},{2,6},{3,7},{4,0},{5,1},{6,2},{7,3},{8,12},{9,13},{10,... | collective-permute-start | bytes 3145736 | tf_op jit(solution)/shard_map/ppermute | solution.py:885
  12.5 24.8 %collective-permute-start.4 = (bf16[128,4096]{1,0:T(8,128)(2,1)}, bf16[128,4096]{1,0:T(8,128)(2,1)S(1)}, u32[]{:S(2)}, u32[]{:S(2)}) collective-permute-start(bf16[128,4096]{1,0:T(8,128)(2,1)} %get-tuple-element.138.refs_0_.refs_5_.refs_6_.refs_4_), channel_id=1, source_target_pairs={{0,2},{1,3},{2,0},{3,1},{4,6},{5,7},{6,4},{7,5},{8,10},{9,11},{10,... | collective-permute-start | bytes 3145736 | tf_op jit(solution)/shard_map/ppermute | solution.py:885
  40.9 6.8 %copy-start.20 = (bf16[1,576]{1,0:T(2,128)(2,1)S(1)}, bf16[1,576]{1,0:T(2,128)(2,1)}, u32[]{:S(2)}) copy-start(bf16[1,576]{1,0:T(2,128)(2,1)} %get-tuple-element.137) | copy-start | bytes 3460
  40.9 23.9 %copy-start.4 = (bf16[128,4096]{1,0:T(8,128)(2,1)S(1)}, bf16[128,4096]{1,0:T(8,128)(2,1)}, u32[]{:S(2)}) copy-start(bf16[128,4096]{1,0:T(8,128)(2,1)} %get-tuple-element.138.refs_0_.refs_5_.refs_6_.refs_4_) | copy-start | bytes 3145732
  40.9 27.1 %copy-start.1 = (bf16[128,4096]{1,0:T(8,128)(2,1)S(1)}, bf16[128,4096]{1,0:T(8,128)(2,1)}, u32[]{:S(2)}) copy-start(bf16[128,4096]{1,0:T(8,128)(2,1)} %copy-done) | copy-start | bytes 3145732
  40.9 27.2 %copy-start.3 = (bf16[128,4096]{1,0:T(8,128)(2,1)S(1)}, bf16[128,4096]{1,0:T(8,128)(2,1)}, u32[]{:S(2)}) copy-start(bf16[128,4096]{1,0:T(8,128)(2,1)} %copy-done.2) | copy-start | bytes 3145732
  44.1 115.0 %all-gather.5.cloned.1.call-start = ((), (), s32[]{:S(2)}) async-start(), calls=%async_computation.2 | async-start | bytes 9437184 | tf_op jit(solution)/shard_map/all_gather | solution.py:986
  44.9 202.3 %reduce-scatter.2.cloned.1.call-start = ((), (), s32[]{:S(2)}) async-start(), calls=%async_computation.3 | async-start | bytes 9437184 | tf_op jit(solution)/shard_map/reduce_scatter | solution.py:1036
  44.9 29.6 %collective-permute-start.6 = (bf16[64,4096]{1,0:T(8,128)(2,1)}, bf16[64,4096]{1,0:T(8,128)(2,1)}, u32[]{:S(2)}, u32[]{:S(2)}) collective-permute-start(bf16[64,4096]{1,0:T(8,128)(2,1)} %get-tuple-element.139.refs_6_.refs_2_), channel_id=1, source_target_pairs={{0,4},{1,5},{2,6},{3,7},{4,0},{5,1},{6,2},{7,3},{8,12},{9,13},{10,... | collective-permute-start | bytes 1572872 | tf_op jit(solution)/shard_map/ppermute | solution.py:885
  46.2 28.2 %collective-permute-start.7 = (bf16[64,4096]{1,0:T(8,128)(2,1)}, bf16[64,4096]{1,0:T(8,128)(2,1)}, u32[]{:S(2)}, u32[]{:S(2)}) collective-permute-start(bf16[64,4096]{1,0:T(8,128)(2,1)} %get-tuple-element.140.refs_7_.refs_3_), channel_id=1, source_target_pairs={{0,2},{1,3},{2,0},{3,1},{4,6},{5,7},{6,4},{7,5},{8,10},{9,11},{10,... | collective-permute-start | bytes 1572872 | tf_op jit(solution)/shard_map/ppermute | solution.py:885
  47.7 17.0 %collective-permute-start.2 = (bf16[1,576]{1,0:T(2,128)(2,1)S(1)}, bf16[1,576]{1,0:T(2,128)(2,1)S(1)}, u32[]{:S(2)}, u32[]{:S(2)}) collective-permute-start(bf16[1,576]{1,0:T(2,128)(2,1)S(1)} %copy-done.20), channel_id=1, source_target_pairs={{0,6},{1,7},{2,4},{3,5},{4,2},{5,3},{6,0},{7,1},{8,14},{9,15},{10,... | collective-permute-start | bytes 3464 | tf_op jit(solution)/shard_map/ppermute | solution.py:885
  48.5 16.3 %collective-permute-start.1 = (bf16[1,576]{1,0:T(2,128)(2,1)S(1)}, bf16[1,576]{1,0:T(2,128)(2,1)S(1)}, u32[]{:S(2)}, u32[]{:S(2)}) collective-permute-start(bf16[1,576]{1,0:T(2,128)(2,1)S(1)} %copy-done.20), channel_id=1, source_target_pairs={{0,4},{1,5},{2,6},{3,7},{4,0},{5,1},{6,2},{7,3},{8,12},{9,13},{10,... | collective-permute-start | bytes 3464 | tf_op jit(solution)/shard_map/ppermute | solution.py:885
  49.7 15.1 %collective-permute-start = (bf16[1,576]{1,0:T(2,128)(2,1)S(1)}, bf16[1,576]{1,0:T(2,128)(2,1)S(1)}, u32[]{:S(2)}, u32[]{:S(2)}) collective-permute-start(bf16[1,576]{1,0:T(2,128)(2,1)S(1)} %copy-done.20), channel_id=1, source_target_pairs={{0,2},{1,3},{2,0},{3,1},{4,6},{5,7},{6,4},{7,5},{8,10},{9,11},{10,... | collective-permute-start | bytes 3464 | tf_op jit(solution)/shard_map/ppermute | solution.py:885
  64.7 12.8 %collective-permute-start.8 = (bf16[128,4096]{1,0:T(8,128)(2,1)S(1)}, bf16[128,4096]{1,0:T(8,128)(2,1)}, u32[]{:S(2)}, u32[]{:S(2)}) collective-permute-start(bf16[128,4096]{1,0:T(8,128)(2,1)S(1)} %copy-done.4), channel_id=1, source_target_pairs={{0,1},{1,0},{2,3},{3,2},{4,5},{5,4},{6,7},{7,6},{8,9},{9,8},{10,11... | collective-permute-start | bytes 3145736 | tf_op jit(solution)/shard_map/ppermute | solution.py:885
  64.8 2.5 collective-permute-start.3
  68.0 9.5 %collective-permute-start.10 = (bf16[128,4096]{1,0:T(8,128)(2,1)S(1)}, bf16[128,4096]{1,0:T(8,128)(2,1)}, u32[]{:S(2)}, u32[]{:S(2)}) collective-permute-start(bf16[128,4096]{1,0:T(8,128)(2,1)S(1)} %copy-done.1), channel_id=1, source_target_pairs={{0,1},{1,0},{2,3},{3,2},{4,5},{5,4},{6,7},{7,6},{8,9},{9,8},{10,11... | collective-permute-start | bytes 3145736 | tf_op jit(solution)/shard_map/ppermute | solution.py:885
  68.1 9.4 %collective-permute-start.9 = (bf16[128,4096]{1,0:T(8,128)(2,1)S(1)}, bf16[128,4096]{1,0:T(8,128)(2,1)}, u32[]{:S(2)}, u32[]{:S(2)}) collective-permute-start(bf16[128,4096]{1,0:T(8,128)(2,1)S(1)} %copy-done.3), channel_id=1, source_target_pairs={{0,1},{1,0},{2,3},{3,2},{4,5},{5,4},{6,7},{7,6},{8,9},{9,8},{10,11... | collective-permute-start | bytes 3145736 | tf_op jit(solution)/shard_map/ppermute | solution.py:885
  76.7 4.4 collective-permute-start.11
  179.7 21.4 %collective-permute-start.12 = (bf16[32,128,256]{2,1,0:T(8,128)(2,1)}, bf16[32,128,256]{2,1,0:T(8,128)(2,1)}, u32[]{:S(2)}, u32[]{:S(2)}) collective-permute-start(bf16[32,128,256]{2,1,0:T(8,128)(2,1)} %bitcast.100), channel_id=1, source_target_pairs={{0,1},{1,0},{2,3},{3,2},{4,5},{5,4},{6,7},{7,6},{8,9},{9,8},{10,11... | collective-permute-start | bytes 6291464 | tf_op jit(solution)/shard_map/ppermute | solution.py:885
  200.2 22.9 %collective-permute-start.13 = (bf16[32,128,256]{2,1,0:T(8,128)(2,1)}, bf16[32,128,256]{2,1,0:T(8,128)(2,1)S(1)}, u32[]{:S(2)}, u32[]{:S(2)}) collective-permute-start(bf16[32,128,256]{2,1,0:T(8,128)(2,1)} %bitcast.99), channel_id=1, source_target_pairs={{0,1},{1,0},{2,3},{3,2},{4,5},{5,4},{6,7},{7,6},{8,9},{9,8},{10,11... | collective-permute-start | bytes 6291464 | tf_op jit(solution)/shard_map/ppermute | solution.py:885
  205.8 34.4 %collective-permute-start.14 = (bf16[16,64,256]{2,1,0:T(8,128)(2,1)}, bf16[16,64,256]{2,1,0:T(8,128)(2,1)S(1)}, u32[]{:S(2)}, u32[]{:S(2)}) collective-permute-start(bf16[16,64,256]{2,1,0:T(8,128)(2,1)} %get-tuple-element.159.refs_14_), channel_id=1, source_target_pairs={{0,2},{1,3},{2,0},{3,1},{4,6},{5,7},{6,4},{7,5},{8,10},{9,11},{10,... | collective-permute-start | bytes 1572872 | tf_op jit(solution)/shard_map/ppermute | solution.py:885
  207.3 32.8 %collective-permute-start.15 = (bf16[16,64,256]{2,1,0:T(8,128)(2,1)}, bf16[16,64,256]{2,1,0:T(8,128)(2,1)S(1)}, u32[]{:S(2)}, u32[]{:S(2)}) collective-permute-start(bf16[16,64,256]{2,1,0:T(8,128)(2,1)} %get-tuple-element.160.refs_15_), channel_id=1, source_target_pairs={{0,4},{1,5},{2,6},{3,7},{4,0},{5,1},{6,2},{7,3},{8,12},{9,13},{10,... | collective-permute-start | bytes 1572872 | tf_op jit(solution)/shard_map/ppermute | solution.py:885
  228.8 18.3 %collective-permute-start.16 = (bf16[16,64,256]{2,1,0:T(8,128)(2,1)}, bf16[16,64,256]{2,1,0:T(8,128)(2,1)S(1)}, u32[]{:S(2)}, u32[]{:S(2)}) collective-permute-start(bf16[16,64,256]{2,1,0:T(8,128)(2,1)} %get-tuple-element.168.refs_9_), channel_id=1, source_target_pairs={{0,2},{1,3},{2,0},{3,1},{4,6},{5,7},{6,4},{7,5},{8,10},{9,11},{10,... | collective-permute-start | bytes 1572872 | tf_op jit(solution)/shard_map/ppermute | solution.py:885
  229.6 17.5 %collective-permute-start.17 = (bf16[16,64,256]{2,1,0:T(8,128)(2,1)}, bf16[16,64,256]{2,1,0:T(8,128)(2,1)S(1)}, u32[]{:S(2)}, u32[]{:S(2)}) collective-permute-start(bf16[16,64,256]{2,1,0:T(8,128)(2,1)} %get-tuple-element.169.refs_10_), channel_id=1, source_target_pairs={{0,4},{1,5},{2,6},{3,7},{4,0},{5,1},{6,2},{7,3},{8,12},{9,13},{10,... | collective-permute-start | bytes 1572872 | tf_op jit(solution)/shard_map/ppermute | solution.py:885
  230.3 36.1 %collective-permute-start.20 = (bf16[16,128,256]{2,1,0:T(8,128)(2,1)}, bf16[16,128,256]{2,1,0:T(8,128)(2,1)S(1)}, u32[]{:S(2)}, u32[]{:S(2)}) collective-permute-start(bf16[16,128,256]{2,1,0:T(8,128)(2,1)} %bitcast.101), channel_id=1, source_target_pairs={{0,1},{1,0},{2,3},{3,2},{4,5},{5,4},{6,7},{7,6},{8,9},{9,8},{10,11... | collective-permute-start | bytes 3145736 | tf_op jit(solution)/shard_map/ppermute | solution.py:885
  240.2 7.0 %copy-start.15 = (bf16[16,64,256]{2,1,0:T(8,128)(2,1)}, bf16[16,64,256]{2,1,0:T(8,128)(2,1)S(1)}, u32[]{:S(2)}) copy-start(bf16[16,64,256]{2,1,0:T(8,128)(2,1)S(1)} %collective-permute-done.14.refs_5_) | copy-start | bytes 1572868
  240.2 7.0 %copy-start.16 = (bf16[16,64,256]{2,1,0:T(8,128)(2,1)}, bf16[16,64,256]{2,1,0:T(8,128)(2,1)S(1)}, u32[]{:S(2)}) copy-start(bf16[16,64,256]{2,1,0:T(8,128)(2,1)S(1)} %collective-permute-done.15.refs_7_.refs_8_) | copy-start | bytes 1572868
  254.2 99.1 %all-reduce.2.cloned.1.call-start = ((), (), s32[]{:S(2)}) async-start(), calls=%async_computation.4 | async-start | bytes 2097152 | tf_op jit(solution)/shard_map/psum | solution.py:1050
  254.3 13.7 %collective-permute-start.18 = (bf16[16,64,256]{2,1,0:T(8,128)(2,1)}, bf16[16,64,256]{2,1,0:T(8,128)(2,1)S(1)}, u32[]{:S(2)}, u32[]{:S(2)}) collective-permute-start(bf16[16,64,256]{2,1,0:T(8,128)(2,1)} %get-tuple-element.178.refs_11_), channel_id=1, source_target_pairs={{0,4},{1,5},{2,6},{3,7},{4,0},{5,1},{6,2},{7,3},{8,12},{9,13},{10,... | collective-permute-start | bytes 1572872 | tf_op jit(solution)/shard_map/ppermute | solution.py:885
  255.8 13.4 %collective-permute-start.19 = (bf16[16,64,256]{2,1,0:T(8,128)(2,1)}, bf16[16,64,256]{2,1,0:T(8,128)(2,1)S(1)}, u32[]{:S(2)}, u32[]{:S(2)}) collective-permute-start(bf16[16,64,256]{2,1,0:T(8,128)(2,1)} %get-tuple-element.179.refs_12_), channel_id=1, source_target_pairs={{0,2},{1,3},{2,0},{3,1},{4,6},{5,7},{6,4},{7,5},{8,10},{9,11},{10,... | collective-permute-start | bytes 1572872 | tf_op jit(solution)/shard_map/ppermute | solution.py:885
  256.4 12.8 %collective-permute-start.21 = (bf16[12,128,256]{2,1,0:T(8,128)(2,1)}, bf16[12,128,256]{2,1,0:T(8,128)(2,1)S(1)}, u32[]{:S(2)}, u32[]{:S(2)}) collective-permute-start(bf16[12,128,256]{2,1,0:T(8,128)(2,1)} %get-tuple-element.176.refs_9_), channel_id=1, source_target_pairs={{0,1},{1,0},{2,3},{3,2},{4,5},{5,4},{6,7},{7,6},{8,9},{9,8},{10,11... | collective-permute-start | bytes 2359304 | tf_op jit(solution)/shard_map/ppermute | solution.py:885
  277.1 13.1 %collective-permute-start.23 = (bf16[14,64,256]{2,1,0:T(8,128)(2,1)}, bf16[14,64,256]{2,1,0:T(8,128)(2,1)S(1)}, u32[]{:S(2)}, u32[]{:S(2)}) collective-permute-start(bf16[14,64,256]{2,1,0:T(8,128)(2,1)} %get-tuple-element.190.refs_14_), channel_id=1, source_target_pairs={{0,2},{1,3},{2,0},{3,1},{4,6},{5,7},{6,4},{7,5},{8,10},{9,11},{10,... | collective-permute-start | bytes 1376264 | tf_op jit(solution)/shard_map/ppermute | solution.py:885
  277.7 12.4 %collective-permute-start.24 = (bf16[14,64,256]{2,1,0:T(8,128)(2,1)}, bf16[14,64,256]{2,1,0:T(8,128)(2,1)S(1)}, u32[]{:S(2)}, u32[]{:S(2)}) collective-permute-start(bf16[14,64,256]{2,1,0:T(8,128)(2,1)} %get-tuple-element.191.refs_15_), channel_id=1, source_target_pairs={{0,4},{1,5},{2,6},{3,7},{4,0},{5,1},{6,2},{7,3},{8,12},{9,13},{10,... | collective-permute-start | bytes 1376264 | tf_op jit(solution)/shard_map/ppermute | solution.py:885
  278.8 13.9 %collective-permute-start.22 = (bf16[16,64,256]{2,1,0:T(8,128)(2,1)}, bf16[16,64,256]{2,1,0:T(8,128)(2,1)S(1)}, u32[]{:S(2)}, u32[]{:S(2)}) collective-permute-start(bf16[16,64,256]{2,1,0:T(8,128)(2,1)} %get-tuple-element.187.refs_11_), channel_id=1, source_target_pairs={{0,8},{8,0},{16,24},{24,16},{1,9},{9,1},{17,25},{25,17},{2,10},{10... | collective-permute-start | bytes 1572872 | tf_op jit(solution)/shard_map/ppermute | solution.py:669
  280.3 12.4 %collective-permute-start.25 = (bf16[12,128,256]{2,1,0:T(8,128)(2,1)}, bf16[12,128,256]{2,1,0:T(8,128)(2,1)S(1)}, u32[]{:S(2)}, u32[]{:S(2)}) collective-permute-start(bf16[12,128,256]{2,1,0:T(8,128)(2,1)} %get-tuple-element.185.refs_9_), channel_id=1, source_target_pairs={{0,1},{1,0},{2,3},{3,2},{4,5},{5,4},{6,7},{7,6},{8,9},{9,8},{10,11... | collective-permute-start | bytes 2359304 | tf_op jit(solution)/shard_map/ppermute | solution.py:885
  300.3 21.6 %collective-permute-start.26 = (bf16[16,32,256]{2,1,0:T(8,128)(2,1)}, bf16[16,32,256]{2,1,0:T(8,128)(2,1)S(1)}, u32[]{:S(2)}, u32[]{:S(2)}) collective-permute-start(bf16[16,32,256]{2,1,0:T(8,128)(2,1)} %get-tuple-element.201.refs_11_), channel_id=1, source_target_pairs={{0,16},{8,24},{16,0},{24,8},{1,17},{9,25},{17,1},{25,9},{2,18},{10... | collective-permute-start | bytes 786440 | tf_op jit(solution)/shard_map/ppermute | solution.py:669
  302.8 19.2 %collective-permute-start.27 = (bf16[13,64,256]{2,1,0:T(8,128)(2,1)}, bf16[13,64,256]{2,1,0:T(8,128)(2,1)S(1)}, u32[]{:S(2)}, u32[]{:S(2)}) collective-permute-start(bf16[13,64,256]{2,1,0:T(8,128)(2,1)} %get-tuple-element.204.refs_14_), channel_id=1, source_target_pairs={{0,4},{1,5},{2,6},{3,7},{4,0},{5,1},{6,2},{7,3},{8,12},{9,13},{10,... | collective-permute-start | bytes 1277960 | tf_op jit(solution)/shard_map/ppermute | solution.py:885
  304.3 17.7 %collective-permute-start.28 = (bf16[13,64,256]{2,1,0:T(8,128)(2,1)}, bf16[13,64,256]{2,1,0:T(8,128)(2,1)S(1)}, u32[]{:S(2)}, u32[]{:S(2)}) collective-permute-start(bf16[13,64,256]{2,1,0:T(8,128)(2,1)} %get-tuple-element.205.refs_15_), channel_id=1, source_target_pairs={{0,2},{1,3},{2,0},{3,1},{4,6},{5,7},{6,4},{7,5},{8,10},{9,11},{10,... | collective-permute-start | bytes 1277960 | tf_op jit(solution)/shard_map/ppermute | solution.py:885
  305.7 16.2 %collective-permute-start.29 = (bf16[12,128,256]{2,1,0:T(8,128)(2,1)}, bf16[12,128,256]{2,1,0:T(8,128)(2,1)S(1)}, u32[]{:S(2)}, u32[]{:S(2)}) collective-permute-start(bf16[12,128,256]{2,1,0:T(8,128)(2,1)} %get-tuple-element.199.refs_9_), channel_id=1, source_target_pairs={{0,1},{1,0},{2,3},{3,2},{4,5},{5,4},{6,7},{7,6},{8,9},{9,8},{10,11... | collective-permute-start | bytes 2359304 | tf_op jit(solution)/shard_map/ppermute | solution.py:885
  330.0 18.7 %collective-permute-start.33 = (bf16[6,64,256]{2,1,0:T(8,128)(2,1)}, bf16[6,64,256]{2,1,0:T(8,128)(2,1)S(1)}, u32[]{:S(2)}, u32[]{:S(2)}) collective-permute-start(bf16[6,64,256]{2,1,0:T(8,128)(2,1)} %get-tuple-element.215.refs_34_), channel_id=1, source_target_pairs={{0,6},{1,7},{2,4},{3,5},{4,2},{5,3},{6,0},{7,1},{8,14},{9,15},{10,... | collective-permute-start | bytes 589832 | tf_op jit(solution)/shard_map/ppermute | solution.py:885
  332.4 20.6 %collective-permute-start.34 = (bf16[16,32,256]{2,1,0:T(8,128)(2,1)}, bf16[16,32,256]{2,1,0:T(8,128)(2,1)S(1)}, u32[]{:S(2)}, u32[]{:S(2)}) collective-permute-start(bf16[16,32,256]{2,1,0:T(8,128)(2,1)} %get-tuple-element.217.refs_26_), channel_id=1, source_target_pairs={{0,16},{8,24},{16,0},{24,8},{1,17},{9,25},{17,1},{25,9},{2,18},{10... | collective-permute-start | bytes 786440 | tf_op jit(solution)/shard_map/ppermute | solution.py:669
  332.4 22.5 %collective-permute-start.31 = (bf16[9,64,256]{2,1,0:T(8,128)(2,1)}, bf16[9,64,256]{2,1,0:T(8,128)(2,1)S(1)}, u32[]{:S(2)}, u32[]{:S(2)}) collective-permute-start(bf16[9,64,256]{2,1,0:T(8,128)(2,1)} %get-tuple-element.213.refs_33_), channel_id=1, source_target_pairs={{0,2},{1,3},{2,0},{3,1},{4,6},{5,7},{6,4},{7,5},{8,10},{9,11},{10,... | collective-permute-start | bytes 884744 | tf_op jit(solution)/shard_map/ppermute | solution.py:885
  333.0 21.9 %collective-permute-start.32 = (bf16[9,64,256]{2,1,0:T(8,128)(2,1)}, bf16[9,64,256]{2,1,0:T(8,128)(2,1)S(1)}, u32[]{:S(2)}, u32[]{:S(2)}) collective-permute-start(bf16[9,64,256]{2,1,0:T(8,128)(2,1)} %get-tuple-element.214.refs_32_), channel_id=1, source_target_pairs={{0,4},{1,5},{2,6},{3,7},{4,0},{5,1},{6,2},{7,3},{8,12},{9,13},{10,... | collective-permute-start | bytes 884744 | tf_op jit(solution)/shard_map/ppermute | solution.py:885
  333.5 28.2 %collective-permute-start.30 = (bf16[12,128,256]{2,1,0:T(8,128)(2,1)}, bf16[12,128,256]{2,1,0:T(8,128)(2,1)S(1)}, u32[]{:S(2)}, u32[]{:S(2)}) collective-permute-start(bf16[12,128,256]{2,1,0:T(8,128)(2,1)} %get-tuple-element.212.refs_24_), channel_id=1, source_target_pairs={{0,1},{1,0},{2,3},{3,2},{4,5},{5,4},{6,7},{7,6},{8,9},{9,8},{10,11... | collective-permute-start | bytes 2359304 | tf_op jit(solution)/shard_map/ppermute | solution.py:885
  333.5 15.1 %copy-start.19 = (bf16[14,64,256]{2,1,0:T(8,128)(2,1)S(1)}, bf16[14,64,256]{2,1,0:T(8,128)(2,1)}, u32[]{:S(2)}) copy-start(bf16[14,64,256]{2,1,0:T(8,128)(2,1)} %get-tuple-element.220.refs_29_) | copy-start | bytes 1376260
  348.7 4.4 copy-start.39
  348.7 13.0 %collective-permute-start.35 = (bf16[14,64,256]{2,1,0:T(8,128)(2,1)S(1)}, bf16[14,64,256]{2,1,0:T(8,128)(2,1)S(1)}, u32[]{:S(2)}, u32[]{:S(2)}) collective-permute-start(bf16[14,64,256]{2,1,0:T(8,128)(2,1)S(1)} %copy-done.19), channel_id=1, source_target_pairs={{0,8},{8,0},{16,24},{24,16},{1,9},{9,1},{17,25},{25,17},{2,10},{10... | collective-permute-start | bytes 1376264 | tf_op jit(solution)/shard_map/ppermute | solution.py:669
  353.1 8.6 %copy-start.32 = (bf16[16,32,256]{2,1,0:T(8,128)(2,1)}, bf16[16,32,256]{2,1,0:T(8,128)(2,1)S(1)}, u32[]{:S(2)}) copy-start(bf16[16,32,256]{2,1,0:T(8,128)(2,1)S(1)} %collective-permute-done.34.refs_6_.refs_8_) | copy-start | bytes 786436
  353.1 1.8 collective-permute-start.36
  354.9 6.8 %copy-start.35 = (bf16[4,128,256]{2,1,0:T(8,128)(2,1)}, bf16[4,128,256]{2,1,0:T(8,128)(2,1)S(1)}, u32[]{:S(2)}) copy-start(bf16[4,128,256]{2,1,0:T(8,128)(2,1)S(1)} %collective-permute-done.36.refs_21_) | copy-start | bytes 786436
  354.9 6.8 %copy-start.30 = (bf16[9,64,256]{2,1,0:T(8,128)(2,1)}, bf16[9,64,256]{2,1,0:T(8,128)(2,1)S(1)}, u32[]{:S(2)}) copy-start(bf16[9,64,256]{2,1,0:T(8,128)(2,1)S(1)} %collective-permute-done.31.refs_2_.refs_19_) | copy-start | bytes 884740
  354.9 6.8 %copy-start.31 = (bf16[9,64,256]{2,1,0:T(8,128)(2,1)}, bf16[9,64,256]{2,1,0:T(8,128)(2,1)S(1)}, u32[]{:S(2)}) copy-start(bf16[9,64,256]{2,1,0:T(8,128)(2,1)S(1)} %collective-permute-done.32.refs_3_.refs_16_) | copy-start | bytes 884740
  367.0 32.1 %collective-permute-start.41 = (bf16[28,64,256]{2,1,0:T(8,128)(2,1)}, bf16[28,64,256]{2,1,0:T(8,128)(2,1)S(1)}, u32[]{:S(2)}, u32[]{:S(2)}) collective-permute-start(bf16[28,64,256]{2,1,0:T(8,128)(2,1)} %get-tuple-element.235.refs_12_), channel_id=1, source_target_pairs={{0,8},{8,0},{16,24},{24,16},{1,9},{9,1},{17,25},{25,17},{2,10},{10... | collective-permute-start | bytes 2752520 | tf_op jit(solution)/shard_map/ppermute | solution.py:669
  368.6 21.1 %collective-permute-start.38 = (bf16[8,64,256]{2,1,0:T(8,128)(2,1)}, bf16[8,64,256]{2,1,0:T(8,128)(2,1)S(1)}, u32[]{:S(2)}, u32[]{:S(2)}) collective-permute-start(bf16[8,64,256]{2,1,0:T(8,128)(2,1)} %get-tuple-element.231.refs_8_), channel_id=1, source_target_pairs={{0,2},{1,3},{2,0},{3,1},{4,6},{5,7},{6,4},{7,5},{8,10},{9,11},{10,... | collective-permute-start | bytes 786440 | tf_op jit(solution)/shard_map/ppermute | solution.py:885
  370.3 19.4 %collective-permute-start.39 = (bf16[8,64,256]{2,1,0:T(8,128)(2,1)}, bf16[8,64,256]{2,1,0:T(8,128)(2,1)S(1)}, u32[]{:S(2)}, u32[]{:S(2)}) collective-permute-start(bf16[8,64,256]{2,1,0:T(8,128)(2,1)} %get-tuple-element.232.refs_9_), channel_id=1, source_target_pairs={{0,4},{1,5},{2,6},{3,7},{4,0},{5,1},{6,2},{7,3},{8,12},{9,13},{10,... | collective-permute-start | bytes 786440 | tf_op jit(solution)/shard_map/ppermute | solution.py:885
  371.8 17.9 %collective-permute-start.40 = (bf16[8,64,256]{2,1,0:T(8,128)(2,1)}, bf16[8,64,256]{2,1,0:T(8,128)(2,1)S(1)}, u32[]{:S(2)}, u32[]{:S(2)}) collective-permute-start(bf16[8,64,256]{2,1,0:T(8,128)(2,1)} %get-tuple-element.233.refs_10_), channel_id=1, source_target_pairs={{0,6},{1,7},{2,4},{3,5},{4,2},{5,3},{6,0},{7,1},{8,14},{9,15},{10,... | collective-permute-start | bytes 786440 | tf_op jit(solution)/shard_map/ppermute | solution.py:885
  372.1 26.1 %collective-permute-start.37 = (bf16[28,32,256]{2,1,0:T(8,128)(2,1)}, bf16[28,32,256]{2,1,0:T(8,128)(2,1)S(1)}, u32[]{:S(2)}, u32[]{:S(2)}) collective-permute-start(bf16[28,32,256]{2,1,0:T(8,128)(2,1)} %get-tuple-element.239.refs_16_), channel_id=1, source_target_pairs={{0,16},{8,24},{16,0},{24,8},{1,17},{9,25},{17,1},{25,9},{2,18},{10... | collective-permute-start | bytes 1376264 | tf_op jit(solution)/shard_map/ppermute | solution.py:669
  389.7 9.4 %copy-start.33 = (bf16[8,64,256]{2,1,0:T(8,128)(2,1)}, bf16[8,64,256]{2,1,0:T(8,128)(2,1)S(1)}, u32[]{:S(2)}) copy-start(bf16[8,64,256]{2,1,0:T(8,128)(2,1)S(1)} %collective-permute-done.38.refs_0_.refs_4_) | copy-start | bytes 786436
  389.7 9.4 %copy-start.34 = (bf16[8,64,256]{2,1,0:T(8,128)(2,1)}, bf16[8,64,256]{2,1,0:T(8,128)(2,1)S(1)}, u32[]{:S(2)}) copy-start(bf16[8,64,256]{2,1,0:T(8,128)(2,1)S(1)} %collective-permute-done.39.refs_1_.refs_5_) | copy-start | bytes 786436
  389.7 9.4 %copy-start.36 = (bf16[8,64,256]{2,1,0:T(8,128)(2,1)}, bf16[8,64,256]{2,1,0:T(8,128)(2,1)S(1)}, u32[]{:S(2)}) copy-start(bf16[8,64,256]{2,1,0:T(8,128)(2,1)S(1)} %collective-permute-done.40.refs_2_.refs_6_) | copy-start | bytes 786436
  405.4 20.0 %collective-permute-start.42 = (bf16[24,32,256]{2,1,0:T(8,128)(2,1)}, bf16[24,32,256]{2,1,0:T(8,128)(2,1)S(1)}, u32[]{:S(2)}, u32[]{:S(2)}) collective-permute-start(bf16[24,32,256]{2,1,0:T(8,128)(2,1)} %get-tuple-element.245), channel_id=1, source_target_pairs={{0,16},{8,24},{16,0},{24,8},{1,17},{9,25},{17,1},{25,9},{2,18},{10... | collective-permute-start | bytes 1179656 | tf_op jit(solution)/shard_map/ppermute | solution.py:669
  408.7 13.3 %collective-permute-start.43 = (bf16[8,64,256]{2,1,0:T(8,128)(2,1)}, bf16[8,64,256]{2,1,0:T(8,128)(2,1)S(1)}, u32[]{:S(2)}, u32[]{:S(2)}) collective-permute-start(bf16[8,64,256]{2,1,0:T(8,128)(2,1)} %get-tuple-element.248), channel_id=1, source_target_pairs={{0,8},{8,0},{16,24},{24,16},{1,9},{9,1},{17,25},{25,17},{2,10},{10... | collective-permute-start | bytes 786440 | tf_op jit(solution)/shard_map/ppermute | solution.py:669
  428.7 13.2 %collective-permute-start.44 = (bf16[16,32,256]{2,1,0:T(8,128)(2,1)}, bf16[16,32,256]{2,1,0:T(8,128)(2,1)S(1)}, u32[]{:S(2)}, u32[]{:S(2)}) collective-permute-start(bf16[16,32,256]{2,1,0:T(8,128)(2,1)} %get-tuple-element.251), channel_id=1, source_target_pairs={{0,16},{8,24},{16,0},{24,8},{1,17},{9,25},{17,1},{25,9},{2,18},{10... | collective-permute-start | bytes 786440 | tf_op jit(solution)/shard_map/ppermute | solution.py:669
  (25 other events, 33.1 us)
Sparse Core Ops, SparseCore 0:
  44.2 58.4 all-gather.2
  104.6 54.4 all-gather.4
  162.6 79.3 reduce-scatter.1
  257.2 63.0 all-reduce.1

commit v4 on v3

--- a/solution.py
+++ b/solution.py
@@ -190,7 +190,7 @@
 def project(n1t, parts):
     width, rows = n1t.shape
     cols = 3 * width
-    tile = 512
+    tile = 1024
     return pl.pallas_call(
         project_kernel, grid=(cols // tile,), name="project",
         in_specs=[resident((width, rows))] + [pl.BlockSpec((p.shape[0], tile), lambda i: (0, i)) for p in parts],
@@ -420,27 +420,18 @@
     n2 = n2_v[...]
     steps = 2 * len(chunks)
 
-    def products(t):
+    for t in range(steps):
         k, u = t // 2, t % 2
         offs = [block_of(me, 4 * u + j) for j in range(4)]
         wi = jnp.concatenate([w_v[:, k, :128, pl.ds(o, 128)].reshape(1024, 128) for o in offs], axis=1)
-        units = dot(n2, wi)
+        hid, slope = gelu_parts(dot(n2, wi))
+        hid = hid.astype(BF)
         if t == 0:
             for x in copies[early[0]:early[1]]:
                 x.wait()
+            og = og_v[...]
         wd = w_v[4 * u:4 * u + 4, k, 128:, :].reshape(512, 1024)
-        return offs, wi, units, dot(og_v[...], wd, NT)
-
-    ahead = products(0)
-    og = og_v[...]
-    for t in range(steps):
-        k, u = t // 2, t % 2
-        offs, wi, units, back = ahead
-        if t + 1 < steps:
-            ahead = products(t + 1)
-        hid, slope = gelu_parts(units)
-        hid = hid.astype(BF)
-        pre = (back * slope).astype(BF)
+        pre = (dot(og, wd, NT) * slope).astype(BF)
         hid_v[:, t * 512:(t + 1) * 512] = hid
         store(hid_v.at[:, t * 512:(t + 1) * 512], outs[1].at[:, t * 512:(t + 1) * 512])
         if t == 0:
@@ -1054,7 +1045,7 @@
         q1 = Piece(3, keep, got, False, "pairs")
         three = back(2, made)
         ((got, keep),), made = slot([f2, f3, wo, q0, q1], [project_back(n1t, three, "core")])
-        q2 = Piece(3, keep, got, True, "pairs")
+        q2 = Piece(3, keep, got, False, "pairs")
         three = back(3, made)
         ((got, keep),), made = slot([f2, f3, wo, q0, q1, q2], [project_back(n1t, three, "core")])
         q3 = Piece(3, keep, got, True, "pairs")
@@ -1065,7 +1056,7 @@
         _, made = slot([q3, q2, f2, f3, wo, q0, q1, vec], deps=(one,))
         outputs = output(me1, lengths, mid, [hid1, hid2, hid3], ffn_w, made)
         ((in_grad, down_grad),), made = slot([q3, vec, q2, q1], [], [feed_result(one, [f2, f3])], deps=(outputs,) + came(wo, q0))
-        _, made = slot([q3, vec], deps=came(q2, q1))
+        _, made = slot([q3, q2, vec], deps=came(q1))
         ((qkv_grad, out_g), tiny), _ = slot([], [project_result(wo, [q0, q1, q2, q3]), vector_result(vec)])
         in_grad, down_grad, qkv_grad, out_g = (v.array for v in (in_grad, down_grad, qkv_grad, out_g))
         tiny = [v.array[0] for v in tiny]

time: 460 us -> 460 us (level)
  waiting for transfers between devices: 109 us -> 115 us
    ppermute x36 -> x35, waiting for transfers between devices: 53.2 us -> 58.6 us  [flip(): return lax.ppermute(v, 'fsdp', [(i, i ^ k) for i in range(GROUPS)])]
    ppermute x36 -> x35, starting transfers between devices: 30.6 us -> 30.4 us  [flip(): return lax.ppermute(v, 'fsdp', [(i, i ^ k) for i in range(GROUPS)])]
    unnamed x80 -> x76, local copies, waits for them, and re-layouts: 9.96 us -> 9.76 us
  transfers between devices with their start and end apart: 49 -> 48, of which waited for: 18 -> 18; matrix products, arithmetic and copies ran while one was open for 0% -> 0% of each run, Pallas kernels for 55% -> 54%
where the time goes in v4:
time: 460 us; the launch traced here: 454 us
  Pallas kernels  269 us (58%)
  waiting for transfers between devices  115 us (25%)
  starting transfers between devices  42.9 us (9%)
  between operations  15.2 us (3%)
  local copies, waits for them, and re-layouts  11 us (2%)
    pallas_call x3, Pallas kernels, feed(): pl.pallas_call(functools.partial(feed_kernel, chunks, stacked, counts), n...  71.6 us
    ppermute x35, waiting for transfers between devices, flip(): return lax.ppermute(v, 'fsdp', [(i, i ^ k) for i in range(GROUPS)])  58.6 us
    pallas_call x11, Pallas kernels, staged(): pl.pallas_call(functools.partial(staged_kernel, steps, places, len(parts)...  54.3 us
    ppermute x9, waiting for transfers between devices, send(): return lax.ppermute(v, 'rep', [(i, i ^ k) for i in range(4)])  52.2 us
    pallas_call x4, Pallas kernels, attend_back(): pl.pallas_call(with_deps(attend_back_kernel, 9, len(deps)), name='attend_...  39.4 us
    ppermute x35, starting transfers between devices, flip(): return lax.ppermute(v, 'fsdp', [(i, i ^ k) for i in range(GROUPS)])  30.4 us
    pallas_call x1, Pallas kernels, attend(): pl.pallas_call(attend_kernel, name='attend', grid_spec=pltpu.PrefetchScal...  20.8 us
    pallas_call x1, Pallas kernels, output(): pl.pallas_call(with_deps(output_kernel, 5 + len(hids), len(deps)), grid=(...  15.9 us
  transfers between devices with their start and end apart: 48, of which 18 were waited for; matrix products, arithmetic and copies ran while one was open for 0% of the time, Pallas kernels for 54%

profile of v4, /device:TPU:0, one launch (start us, length us, event | category | flops | bytes accessed | tf_op | source)
XLA Modules:
  0.0 453.6 jit_solution(7835229285629359078)
XLA Ops:
  7.2 2.3 lead.1
  9.5 3.0 collective-permute-start.5
  12.5 1.5 collective-permute-start.4
  14.0 21.9 %collective-permute-done.5.b_ref.refs_2_.refs_7_.refs_8_.refs_6_ = bf16[128,4096]{1,0:T(8,128)(2,1)S(1)} collective-permute-done((bf16[128,4096]{1,0:T(8,128)(2,1)}, bf16[128,4096]{1,0:T(8,128)(2,1)S(1)}, u32[]{:S(2)}, u32[]{:S(2)}) %collective-permute-start.5) | collective-permute-done | bytes 1048608 | tf_op jit(solution)/shard_map/ppermute | solution.py:876
  35.9 1.5 collective-permute-done.4.a_ref.refs_1_.refs_6_.refs_7_.refs_5_
  38.3 2.5 halves.1
  40.9 3.2 pack.1
  46.2 1.5 collective-permute-start.7
  49.7 1.5 collective-permute-start
  51.9 12.9 %collective-permute-done.2 = bf16[1,576]{1,0:T(2,128)(2,1)S(1)} collective-permute-done((bf16[1,576]{1,0:T(2,128)(2,1)S(1)}, bf16[1,576]{1,0:T(2,128)(2,1)S(1)}, u32[]{:S(2)}, u32[]{:S(2)}) %collective-permute-start.2) | collective-permute-done | bytes 1184 | tf_op jit(solution)/shard_map/ppermute | solution.py:876
  65.4 2.0 collective-permute-done.3
  68.5 6.0 %prepare.1 = (bf16[1024,1024]{1,0:T(8,128)(2,1)}, bf16[1024,1024]{1,0:T(8,128)(2,1)}, f32[4,1024]{1,0:T(4,128)}, f32[16,4,256]{2,1,0:T(4,128)}) custom-call(s32[1]{0:T(128)} %bitcast.refs_0_.me_ref, s32[1]{0:T(128)S(6)} %copy.26.refs_1_.len_ref, bf16[1024,1024]{1,0:T(8,128)(2,1)} %bitcast.46, bf16[1024,1024]{1,0:T(8,128)(2,1)} %bitcast.64, ...), custom_call_target="tpu_custom_call" | custom-call | flops 1000000000 | bytes 8000000 | tf_op jit(solution)/shard_map/prepare/pallas_call | solution.py:106
  74.5 2.2 join.1.refs_3_.refs_8_.refs_9_.refs_7_
  77.5 3.7 collective-permute-done.11.refs_7_.refs_12_.refs_13_.refs_11_
  81.2 11.1 %project.1.q_ref.k_ref.v_ref.refs_3_.refs_4_.refs_5_ = bf16[48,64,1024]{2,1,0:T(8,128)(2,1)} custom-call(bf16[1024,1024]{1,0:T(8,128)(2,1)} %get-tuple-element.142.refs_2_.n1t_ref.refs_0_, bf16[128,4096]{1,0:T(8,128)(2,1)} %get-tuple-element.138.refs_0_.refs_5_.refs_6_.refs_4_, bf16[128,4096]{1,0:T(8,128)(2,1)} %copy-done.2, bf16[128,4096]{1,0:T(8,128)(2,1)} %copy-done, ...), custom_call_target="tpu_custom_call" | custom-call | flops 6442450944 | bytes 14000000 | tf_op jit(solution)/shard_map/project/pallas_call | solution.py:194
  92.3 20.8 %attend.1 = (bf16[16,64,1024]{2,1,0:T(8,128)(2,1)}, f32[16,1,1024]{2,1,0:T(1,128)}) custom-call(s32[1]{0:T(128)} %bitcast.refs_0_.me_ref, s32[1]{0:T(128)S(6)} %copy.26.refs_1_.len_ref, f32[16,4,256]{2,1,0:T(4,128)} %get-tuple-element.141.base_ref.refs_2_, bf16[48,64,1024]{2,1,0:T(8,128)(2,1)} %project.1.q_ref.k_ref.v_ref.refs_3_.refs_4_.refs_5_, ...), custom_call_target="tpu_custom_call" | custom-call | flops 30000001024 | bytes 10000000 | tf_op jit(solution)/shard_map/attend/pallas_call | solution.py:258
  113.1 9.6 %middle.1 = (f32[1024,1024]{1,0:T(8,128)}, bf16[1024,1024]{1,0:T(8,128)(2,1)}, bf16[1024,1024]{1,0:T(8,128)(2,1)}) custom-call(s32[1]{0:T(128)} %bitcast.refs_0_.me_ref, bf16[1024,1024]{1,0:T(8,128)(2,1)} %bitcast.55, bf16[1024,1024]{1,0:T(8,128)(2,1)} %bitcast.47, f32[1,1024]{1,0:T(1,128)} %get-tuple-element.265.refs_3_.refs_5_, ...), custom_call_target="tpu_custom_call" | custom-call | flops 2147483648 | bytes 14000000 | tf_op jit(solution)/shard_map/middle/pallas_call | solution.py:372
  122.7 33.4 %feed.3 = (f32[1024,1024]{1,0:T(8,128)}, bf16[1024,2048]{1,0:T(8,128)(2,1)}, bf16[8,2,256,1024]{3,2,1,0:T(8,128)(2,1)}) custom-call(s32[1]{0:T(128)} %bitcast.refs_0_.me_ref, bf16[1024,1024]{1,0:T(8,128)(2,1)} %get-tuple-element.146.n2_h, bf16[1024,1024]{1,0:T(8,128)(2,1)} %get-tuple-element.147.n2t_h, bf16[1024,1024]{1,0:T(8,128)(2,1)} %get-tuple-element.148.og_h.refs_3_, ...), custom_call_target="tpu_custom_call" | custom-call | flops 35999997952 | bytes 25000000 | tf_op jit(solution)/shard_map/feed/pallas_call | solution.py:476
  156.2 2.9 all-gather.5.cloned.1.call-done
  159.1 19.2 %feed.4 = (f32[1024,1024]{1,0:T(8,128)}, bf16[1024,1024]{1,0:T(8,128)(2,1)}, bf16[4,8,128,256]{3,2,1,0:T(8,128)(2,1)}, bf16[4,8,128,256]{3,2,1,0:T(8,128)(2,1)}) custom-call(s32[1]{0:T(128)} %bitcast.refs_0_.me_ref, bf16[1024,1024]{1,0:T(8,128)(2,1)} %get-tuple-element.146.n2_h, bf16[1024,1024]{1,0:T(8,128)(2,1)} %get-tuple-element.147.n2t_h, ...), custom_call_target="tpu_custom_call" | custom-call | flops 17999998976 | bytes 25000000 | tf_op jit(solution)/shard_map/feed/pallas_call | solution.py:476
  178.6 19.0 %feed.5 = (f32[1024,1024]{1,0:T(8,128)}, bf16[1024,1024]{1,0:T(8,128)(2,1)}, bf16[4,8,128,256]{3,2,1,0:T(8,128)(2,1)}, bf16[4,8,128,256]{3,2,1,0:T(8,128)(2,1)}) custom-call(s32[1]{0:T(128)} %bitcast.refs_0_.me_ref, bf16[1024,1024]{1,0:T(8,128)(2,1)} %get-tuple-element.146.n2_h, bf16[1024,1024]{1,0:T(8,128)(2,1)} %get-tuple-element.147.n2t_h, ...), custom_call_target="tpu_custom_call" | custom-call | flops 17999998976 | bytes 25000000 | tf_op jit(solution)/shard_map/feed/pallas_call | solution.py:476
  198.5 4.6 %staged.11 = (bf16[16,64,256]{2,1,0:T(8,128)(2,1)}, bf16[16,64,256]{2,1,0:T(8,128)(2,1)}, bf16[16,64,256]{2,1,0:T(8,128)(2,1)}, bf16[16,64,256]{2,1,0:T(8,128)(2,1)}) custom-call(s32[3]{0:T(128)} %pad_add_fusion.where_ref, bf16[32,128,256]{2,1,0:T(8,128)(2,1)} %bitcast.103, bf16[32,128,256]{2,1,0:T(8,128)(2,1)} %collective-permute-done.12.refs_1_, ...), custom_call_target="tpu_custom_call" | custom-call | flops 3000000000 | bytes 10000000 | tf_op jit(solution)/shard_map/staged/pallas_call | solution.py:635
  203.1 1.6 collective-permute-start.14
  205.4 14.8 %middle_back.1 = (f32[1024,1024]{1,0:T(8,128)}, bf16[1024,1024]{1,0:T(8,128)(2,1)}, bf16[4,4,128,256]{3,2,1,0:T(8,128)(2,1)}, bf16[4,4,128,256]{3,2,1,0:T(8,128)(2,1)}, f32[2,1024]{1,0:T(2,128)}) custom-call(s32[1]{0:T(128)} %bitcast.refs_0_.me_ref, f32[1024,1024]{1,0:T(8,128)} %get-tuple-element.145.refs_1_.refs_2_, ...), custom_call_target="tpu_custom_call" | custom-call | flops 4294967296 | bytes 24000000 | tf_op jit(solution)/shard_map/middle_back/pallas_call | solution.py:569
  221.5 4.4 staged.12
  227.6 9.8 %attend_back.4 = (bf16[4,64,1024]{2,1,0:T(8,128)(2,1)}, bf16[4,64,1024]{2,1,0:T(8,128)(2,1)}, bf16[4,64,1024]{2,1,0:T(8,128)(2,1)}, f32[4,4,256]{2,1,0:T(4,128)}) custom-call(s32[1]{0:T(128)} %bitcast.refs_0_.me_ref, s32[1]{0:T(128)S(6)} %copy.26.refs_1_.len_ref, f32[16,4,256]{2,1,0:T(4,128)} %get-tuple-element.141.base_ref.refs_2_, ...), custom_call_target="tpu_custom_call" | custom-call | flops 9600000000 | bytes 4800000 | tf_op jit(solution)/shard_map/attend_back/pallas_call | solution.py:339
  237.5 12.3 %collective-permute-done.16.refs_9_.refs_11_ = bf16[16,64,256]{2,1,0:T(8,128)(2,1)S(1)} collective-permute-done((bf16[16,64,256]{2,1,0:T(8,128)(2,1)}, bf16[16,64,256]{2,1,0:T(8,128)(2,1)S(1)}, u32[]{:S(2)}, u32[]{:S(2)}) %collective-permute-start.16) | collective-permute-done | bytes 524320 | tf_op jit(solution)/shard_map/ppermute | solution.py:876
  250.8 6.1 %staged.13 = (bf16[12,128,256]{2,1,0:T(8,128)(2,1)}, bf16[12,128,256]{2,1,0:T(8,128)(2,1)}, bf16[16,64,256]{2,1,0:T(8,128)(2,1)}, bf16[16,64,256]{2,1,0:T(8,128)(2,1)}) custom-call(s32[3]{0:T(128)} %pad_add_fusion.where_ref, bf16[1024,1024]{1,0:T(8,128)(2,1)} %get-tuple-element.142.refs_2_.n1t_ref.refs_0_, bf16[256,1024]{1,0:T(8,128)(2,1)} %bitcast.74, ...), custom_call_target="tpu_custom_call" | custom-call | flops 3000000000 | bytes 10000000 | tf_op jit(solution)/shard_map/staged/pallas_call | solution.py:635
  256.9 1.5 collective-permute-start.18
  259.1 9.8 %attend_back.5 = (bf16[4,64,1024]{2,1,0:T(8,128)(2,1)}, bf16[4,64,1024]{2,1,0:T(8,128)(2,1)}, bf16[4,64,1024]{2,1,0:T(8,128)(2,1)}, f32[4,4,256]{2,1,0:T(4,128)}) custom-call(s32[1]{0:T(128)} %bitcast.refs_0_.me_ref, s32[1]{0:T(128)S(6)} %copy.26.refs_1_.len_ref, f32[16,4,256]{2,1,0:T(4,128)} %get-tuple-element.141.base_ref.refs_2_, ...), custom_call_target="tpu_custom_call" | custom-call | flops 9600000000 | bytes 4800000 | tf_op jit(solution)/shard_map/attend_back/pallas_call | solution.py:339
  268.9 1.6 collective-permute-done.18.refs_6_.refs_12_
  270.5 1.3 collective-permute-done.19.refs_9_.refs_15_
  272.9 6.8 %staged.14 = (bf16[12,128,256]{2,1,0:T(8,128)(2,1)}, bf16[12,128,256]{2,1,0:T(8,128)(2,1)}, bf16[16,64,256]{2,1,0:T(8,128)(2,1)}, bf16[8,64,256]{2,1,0:T(8,128)(...) custom-call(s32[3]{0:T(128)} %pad_add_fusion.where_ref, ...), custom_call_target="tpu_custom_call" | custom-call | flops 3000000000 | bytes 10000000 | tf_op jit(solution)/shard_map/staged/pallas_call | solution.py:635
  281.4 1.5 collective-permute-start.22
  282.9 9.8 %attend_back.6 = (bf16[4,64,1024]{2,1,0:T(8,128)(2,1)}, bf16[4,64,1024]{2,1,0:T(8,128)(2,1)}, bf16[4,64,1024]{2,1,0:T(8,128)(2,1)}, f32[4,4,256]{2,1,0:T(4,128)}) custom-call(s32[1]{0:T(128)} %bitcast.refs_0_.me_ref, s32[1]{0:T(128)S(6)} %copy.26.refs_1_.len_ref, f32[16,4,256]{2,1,0:T(4,128)} %get-tuple-element.141.base_ref.refs_2_, ...), custom_call_target="tpu_custom_call" | custom-call | flops 9600000000 | bytes 4800000 | tf_op jit(solution)/shard_map/attend_back/pallas_call | solution.py:339
  292.7 2.7 collective-permute-done.22.refs_4_.refs_6_
  296.5 6.5 %staged.15 = (bf16[12,128,256]{2,1,0:T(8,128)(2,1)}, bf16[12,128,256]{2,1,0:T(8,128)(2,1)}, bf16[16,32,256]{2,1,0:T(8,128)(2,1)}, bf16[8,32,256]{2,1,0:T(8,128)(...) custom-call(s32[3]{0:T(128)} %pad_add_fusion.where_ref, ...), custom_call_target="tpu_custom_call" | custom-call | flops 3000000000 | bytes 10000000 | tf_op jit(solution)/shard_map/staged/pallas_call | solution.py:635
  303.0 2.5 collective-permute-start.26
  305.5 1.5 collective-permute-start.27
  306.9 1.5 collective-permute-start.28
  308.4 10.0 %attend_back.7 = (bf16[4,64,1024]{2,1,0:T(8,128)(2,1)}, bf16[4,64,1024]{2,1,0:T(8,128)(2,1)}, bf16[4,64,1024]{2,1,0:T(8,128)(2,1)}, f32[4,4,256]{2,1,0:T(4,128)}) custom-call(s32[1]{0:T(128)} %bitcast.refs_0_.me_ref, s32[1]{0:T(128)S(6)} %copy.26.refs_1_.len_ref, f32[16,4,256]{2,1,0:T(4,128)} %get-tuple-element.141.base_ref.refs_2_, ...), custom_call_target="tpu_custom_call" | custom-call | flops 9600000000 | bytes 4800000 | tf_op jit(solution)/shard_map/attend_back/pallas_call | solution.py:339
  318.4 6.3 %collective-permute-done.26.refs_4_.refs_6_ = bf16[16,32,256]{2,1,0:T(8,128)(2,1)S(1)} collective-permute-done((bf16[16,32,256]{2,1,0:T(8,128)(2,1)}, bf16[16,32,256]{2,1,0:T(8,128)(2,1)S(1)}, u32[]{:S(2)}, u32[]{:S(2)}) %collective-permute-start.26) | collective-permute-done | bytes 262176 | tf_op jit(solution)/shard_map/ppermute | solution.py:660
  325.9 6.8 %staged.16 = (bf16[12,128,256]{2,1,0:T(8,128)(2,1)}, bf16[12,128,256]{2,1,0:T(8,128)(2,1)}, bf16[16,32,256]{2,1,0:T(8,128)(2,1)}, bf16[8,32,256]{2,1,0:T(8,128)(...) custom-call(s32[3]{0:T(128)} %pad_add_fusion.where_ref, ...), custom_call_target="tpu_custom_call" | custom-call | flops 3000000000 | bytes 10000000 | tf_op jit(solution)/shard_map/staged/pallas_call | solution.py:635
  332.8 1.5 collective-permute-start.31
  334.3 1.5 collective-permute-start.32
  335.8 1.7 collective-permute-start.34
  337.5 15.1 %finish.1 = (f32[1024,1024]{1,0:T(8,128)}, f32[2,1024]{1,0:T(2,128)}) custom-call(s32[1]{0:T(128)} %bitcast.refs_0_.me_ref, bf16[1024,1024]{1,0:T(8,128)(2,1)} %bitcast.48, f32[1024,1024]{1,0:T(8,128)} %get-tuple-element.167.refs_2_, f32[1,1024]{1,0:T(1,128)} %get-tuple-element.263.refs_3_, ...), custom_call_target="tpu_custom_call" | custom-call | flops 6442450944 | bytes 34000000 | tf_op jit(solution)/shard_map/finish/pallas_call | solution.py:863
  352.6 2.7 staged.17
  355.9 1.4 collective-permute-done.35.refs_21_
  358.6 4.2 staged.18
  363.3 1.7 collective-permute-start.37
  364.9 1.5 collective-permute-start.38
  367.5 2.0 collective-permute-start.40
  369.6 15.9 %output.1.refs_21_ = bf16[1024,1024]{1,0:T(8,128)(2,1)} custom-call(s32[1]{0:T(128)} %bitcast.refs_0_.me_ref, s32[1]{0:T(128)S(6)} %copy.26.refs_1_.len_ref, f32[1024,1024]{1,0:T(8,128)} %get-tuple-element.145.refs_1_.refs_2_, bf16[1024,2048]{1,0:T(8,128)(2,1)} %get-tuple-element.150.refs_3_, bf16[1024,1024]{1,0:T(8,128)(2,1)} %get-tuple-element.153.refs_4_, ...), custom_call_target="tpu_custom_call" | custom-call | flops 8999999488 | bytes 20000000 | tf_op jit(solution)/shard_map/output/pallas_call | solution.py:517
  385.6 3.8 collective-permute-done.36.refs_22_.refs_23_.refs_0_.refs_2_
  389.3 5.8 %collective-permute-done.40.refs_14_.refs_17_.refs_19_ = bf16[22,64,256]{2,1,0:T(8,128)(2,1)S(1)} collective-permute-done((bf16[22,64,256]{2,1,0:T(8,128)(2,1)}, bf16[22,64,256]{2,1,0:T(8,128)(2,1)S(1)}, u32[]{:S(2)}, u32[]{:S(2)}) %collective-permute-start.40) | collective-permute-done | bytes 720928 | tf_op jit(solution)/shard_map/ppermute | solution.py:660
  396.0 5.5 %staged.19 = (bf16[14,64,256]{2,1,0:T(8,128)(2,1)}, bf16[6,64,256]{2,1,0:T(8,128)(2,1)}, bf16[2,64,256]{2,1,0:T(8,128)(2,1)}, bf16[6,64,256]{2,1,0:T(8,128)(2,1)...) custom-call(s32[3]{0:T(128)} %pad_add_fusion.where_ref, ...), custom_call_target="tpu_custom_call" | custom-call | flops 3000000000 | bytes 10000000 | tf_op jit(solution)/shard_map/staged/pallas_call | solution.py:635
  401.6 2.0 collective-permute-start.41
  403.6 11.4 %collective-permute-done.41.refs_6_.refs_4_ = bf16[12,32,256]{2,1,0:T(8,128)(2,1)S(1)} collective-permute-done((bf16[12,32,256]{2,1,0:T(8,128)(2,1)}, bf16[12,32,256]{2,1,0:T(8,128)(2,1)S(1)}, u32[]{:S(2)}, u32[]{:S(2)}) %collective-permute-start.41) | collective-permute-done | bytes 196640 | tf_op jit(solution)/shard_map/ppermute | solution.py:660
  415.0 2.1 collective-permute-done.42.refs_0_.refs_2_.refs_4_
  417.8 2.8 staged.20
  420.6 1.3 collective-permute-start.43
  422.0 20.2 %collective-permute-done.43.refs_6_.refs_8_.refs_10_ = bf16[28,32,256]{2,1,0:T(8,128)(2,1)S(1)} collective-permute-done((bf16[28,32,256]{2,1,0:T(8,128)(2,1)}, bf16[28,32,256]{2,1,0:T(8,128)(2,1)S(1)}, u32[]{:S(2)}, u32[]{:S(2)}) %collective-permute-start.43) | collective-permute-done | bytes 458784 | tf_op jit(solution)/shard_map/ppermute | solution.py:660
  442.9 3.9 staged.21
  (148 shorter events, 25.3 us)
Async XLA Ops:
  7.2 115.5 %all-gather.3.cloned.1.call-start = ((), (), s32[]{:S(2)}) async-start(), calls=%async_computation.1 | async-start | bytes 9437184 | tf_op jit(solution)/shard_map/all_gather | solution.py:977
  9.5 26.3 %collective-permute-start.5 = (bf16[128,4096]{1,0:T(8,128)(2,1)}, bf16[128,4096]{1,0:T(8,128)(2,1)S(1)}, u32[]{:S(2)}, u32[]{:S(2)}) collective-permute-start(bf16[128,4096]{1,0:T(8,128)(2,1)} %get-tuple-element.138.refs_0_.refs_5_.refs_6_.refs_4_), channel_id=1, source_target_pairs={{0,4},{1,5},{2,6},{3,7},{4,0},{5,1},{6,2},{7,3},{8,12},{9,13},{10,... | collective-permute-start | bytes 3145736 | tf_op jit(solution)/shard_map/ppermute | solution.py:876
  12.5 24.8 %collective-permute-start.4 = (bf16[128,4096]{1,0:T(8,128)(2,1)}, bf16[128,4096]{1,0:T(8,128)(2,1)S(1)}, u32[]{:S(2)}, u32[]{:S(2)}) collective-permute-start(bf16[128,4096]{1,0:T(8,128)(2,1)} %get-tuple-element.138.refs_0_.refs_5_.refs_6_.refs_4_), channel_id=1, source_target_pairs={{0,2},{1,3},{2,0},{3,1},{4,6},{5,7},{6,4},{7,5},{8,10},{9,11},{10,... | collective-permute-start | bytes 3145736 | tf_op jit(solution)/shard_map/ppermute | solution.py:876
  40.9 6.8 %copy-start.19 = (bf16[1,576]{1,0:T(2,128)(2,1)S(1)}, bf16[1,576]{1,0:T(2,128)(2,1)}, u32[]{:S(2)}) copy-start(bf16[1,576]{1,0:T(2,128)(2,1)} %get-tuple-element.137) | copy-start | bytes 3460
  40.9 23.8 %copy-start.4 = (bf16[128,4096]{1,0:T(8,128)(2,1)S(1)}, bf16[128,4096]{1,0:T(8,128)(2,1)}, u32[]{:S(2)}) copy-start(bf16[128,4096]{1,0:T(8,128)(2,1)} %get-tuple-element.138.refs_0_.refs_5_.refs_6_.refs_4_) | copy-start | bytes 3145732
  40.9 27.1 %copy-start.1 = (bf16[128,4096]{1,0:T(8,128)(2,1)S(1)}, bf16[128,4096]{1,0:T(8,128)(2,1)}, u32[]{:S(2)}) copy-start(bf16[128,4096]{1,0:T(8,128)(2,1)} %copy-done) | copy-start | bytes 3145732
  40.9 27.2 %copy-start.3 = (bf16[128,4096]{1,0:T(8,128)(2,1)S(1)}, bf16[128,4096]{1,0:T(8,128)(2,1)}, u32[]{:S(2)}) copy-start(bf16[128,4096]{1,0:T(8,128)(2,1)} %copy-done.2) | copy-start | bytes 3145732
  44.1 115.0 %all-gather.5.cloned.1.call-start = ((), (), s32[]{:S(2)}) async-start(), calls=%async_computation.2 | async-start | bytes 9437184 | tf_op jit(solution)/shard_map/all_gather | solution.py:977
  44.9 205.4 %reduce-scatter.2.cloned.1.call-start = ((), (), s32[]{:S(2)}) async-start(), calls=%async_computation.3 | async-start | bytes 9437184 | tf_op jit(solution)/shard_map/reduce_scatter | solution.py:1027
  44.9 29.5 %collective-permute-start.6 = (bf16[64,4096]{1,0:T(8,128)(2,1)}, bf16[64,4096]{1,0:T(8,128)(2,1)}, u32[]{:S(2)}, u32[]{:S(2)}) collective-permute-start(bf16[64,4096]{1,0:T(8,128)(2,1)} %get-tuple-element.139.refs_6_.refs_2_), channel_id=1, source_target_pairs={{0,4},{1,5},{2,6},{3,7},{4,0},{5,1},{6,2},{7,3},{8,12},{9,13},{10,... | collective-permute-start | bytes 1572872 | tf_op jit(solution)/shard_map/ppermute | solution.py:876
  46.2 28.3 %collective-permute-start.7 = (bf16[64,4096]{1,0:T(8,128)(2,1)}, bf16[64,4096]{1,0:T(8,128)(2,1)}, u32[]{:S(2)}, u32[]{:S(2)}) collective-permute-start(bf16[64,4096]{1,0:T(8,128)(2,1)} %get-tuple-element.140.refs_7_.refs_3_), channel_id=1, source_target_pairs={{0,2},{1,3},{2,0},{3,1},{4,6},{5,7},{6,4},{7,5},{8,10},{9,11},{10,... | collective-permute-start | bytes 1572872 | tf_op jit(solution)/shard_map/ppermute | solution.py:876
  47.7 17.0 %collective-permute-start.2 = (bf16[1,576]{1,0:T(2,128)(2,1)S(1)}, bf16[1,576]{1,0:T(2,128)(2,1)S(1)}, u32[]{:S(2)}, u32[]{:S(2)}) collective-permute-start(bf16[1,576]{1,0:T(2,128)(2,1)S(1)} %copy-done.19), channel_id=1, source_target_pairs={{0,6},{1,7},{2,4},{3,5},{4,2},{5,3},{6,0},{7,1},{8,14},{9,15},{10,... | collective-permute-start | bytes 3464 | tf_op jit(solution)/shard_map/ppermute | solution.py:876
  48.5 16.3 %collective-permute-start.1 = (bf16[1,576]{1,0:T(2,128)(2,1)S(1)}, bf16[1,576]{1,0:T(2,128)(2,1)S(1)}, u32[]{:S(2)}, u32[]{:S(2)}) collective-permute-start(bf16[1,576]{1,0:T(2,128)(2,1)S(1)} %copy-done.19), channel_id=1, source_target_pairs={{0,4},{1,5},{2,6},{3,7},{4,0},{5,1},{6,2},{7,3},{8,12},{9,13},{10,... | collective-permute-start | bytes 3464 | tf_op jit(solution)/shard_map/ppermute | solution.py:876
  49.7 15.1 %collective-permute-start = (bf16[1,576]{1,0:T(2,128)(2,1)S(1)}, bf16[1,576]{1,0:T(2,128)(2,1)S(1)}, u32[]{:S(2)}, u32[]{:S(2)}) collective-permute-start(bf16[1,576]{1,0:T(2,128)(2,1)S(1)} %copy-done.19), channel_id=1, source_target_pairs={{0,2},{1,3},{2,0},{3,1},{4,6},{5,7},{6,4},{7,5},{8,10},{9,11},{10,... | collective-permute-start | bytes 3464 | tf_op jit(solution)/shard_map/ppermute | solution.py:876
  64.7 12.8 %collective-permute-start.8 = (bf16[128,4096]{1,0:T(8,128)(2,1)S(1)}, bf16[128,4096]{1,0:T(8,128)(2,1)}, u32[]{:S(2)}, u32[]{:S(2)}) collective-permute-start(bf16[128,4096]{1,0:T(8,128)(2,1)S(1)} %copy-done.4), channel_id=1, source_target_pairs={{0,1},{1,0},{2,3},{3,2},{4,5},{5,4},{6,7},{7,6},{8,9},{9,8},{10,11... | collective-permute-start | bytes 3145736 | tf_op jit(solution)/shard_map/ppermute | solution.py:876
  64.8 2.5 collective-permute-start.3
  68.0 9.5 %collective-permute-start.10 = (bf16[128,4096]{1,0:T(8,128)(2,1)S(1)}, bf16[128,4096]{1,0:T(8,128)(2,1)}, u32[]{:S(2)}, u32[]{:S(2)}) collective-permute-start(bf16[128,4096]{1,0:T(8,128)(2,1)S(1)} %copy-done.1), channel_id=1, source_target_pairs={{0,1},{1,0},{2,3},{3,2},{4,5},{5,4},{6,7},{7,6},{8,9},{9,8},{10,11... | collective-permute-start | bytes 3145736 | tf_op jit(solution)/shard_map/ppermute | solution.py:876
  68.1 9.4 %collective-permute-start.9 = (bf16[128,4096]{1,0:T(8,128)(2,1)S(1)}, bf16[128,4096]{1,0:T(8,128)(2,1)}, u32[]{:S(2)}, u32[]{:S(2)}) collective-permute-start(bf16[128,4096]{1,0:T(8,128)(2,1)S(1)} %copy-done.3), channel_id=1, source_target_pairs={{0,1},{1,0},{2,3},{3,2},{4,5},{5,4},{6,7},{7,6},{8,9},{9,8},{10,11... | collective-permute-start | bytes 3145736 | tf_op jit(solution)/shard_map/ppermute | solution.py:876
  74.5 2.4 copy-start.20
  76.7 4.5 collective-permute-start.11
  178.3 20.2 %collective-permute-start.12 = (bf16[32,128,256]{2,1,0:T(8,128)(2,1)}, bf16[32,128,256]{2,1,0:T(8,128)(2,1)}, u32[]{:S(2)}, u32[]{:S(2)}) collective-permute-start(bf16[32,128,256]{2,1,0:T(8,128)(2,1)} %bitcast.100), channel_id=1, source_target_pairs={{0,1},{1,0},{2,3},{3,2},{4,5},{5,4},{6,7},{7,6},{8,9},{9,8},{10,11... | collective-permute-start | bytes 6291464 | tf_op jit(solution)/shard_map/ppermute | solution.py:876
  197.6 22.6 %collective-permute-start.13 = (bf16[32,128,256]{2,1,0:T(8,128)(2,1)}, bf16[32,128,256]{2,1,0:T(8,128)(2,1)S(1)}, u32[]{:S(2)}, u32[]{:S(2)}) collective-permute-start(bf16[32,128,256]{2,1,0:T(8,128)(2,1)} %bitcast.99), channel_id=1, source_target_pairs={{0,1},{1,0},{2,3},{3,2},{4,5},{5,4},{6,7},{7,6},{8,9},{9,8},{10,11... | collective-permute-start | bytes 6291464 | tf_op jit(solution)/shard_map/ppermute | solution.py:876
  203.1 34.3 %collective-permute-start.14 = (bf16[16,64,256]{2,1,0:T(8,128)(2,1)}, bf16[16,64,256]{2,1,0:T(8,128)(2,1)S(1)}, u32[]{:S(2)}, u32[]{:S(2)}) collective-permute-start(bf16[16,64,256]{2,1,0:T(8,128)(2,1)} %get-tuple-element.159.refs_14_), channel_id=1, source_target_pairs={{0,2},{1,3},{2,0},{3,1},{4,6},{5,7},{6,4},{7,5},{8,10},{9,11},{10,... | collective-permute-start | bytes 1572872 | tf_op jit(solution)/shard_map/ppermute | solution.py:876
  204.7 32.7 %collective-permute-start.15 = (bf16[16,64,256]{2,1,0:T(8,128)(2,1)}, bf16[16,64,256]{2,1,0:T(8,128)(2,1)S(1)}, u32[]{:S(2)}, u32[]{:S(2)}) collective-permute-start(bf16[16,64,256]{2,1,0:T(8,128)(2,1)} %get-tuple-element.160.refs_15_), channel_id=1, source_target_pairs={{0,4},{1,5},{2,6},{3,7},{4,0},{5,1},{6,2},{7,3},{8,12},{9,13},{10,... | collective-permute-start | bytes 1572872 | tf_op jit(solution)/shard_map/ppermute | solution.py:876
  225.9 23.9 %collective-permute-start.16 = (bf16[16,64,256]{2,1,0:T(8,128)(2,1)}, bf16[16,64,256]{2,1,0:T(8,128)(2,1)S(1)}, u32[]{:S(2)}, u32[]{:S(2)}) collective-permute-start(bf16[16,64,256]{2,1,0:T(8,128)(2,1)} %get-tuple-element.168.refs_9_), channel_id=1, source_target_pairs={{0,2},{1,3},{2,0},{3,1},{4,6},{5,7},{6,4},{7,5},{8,10},{9,11},{10,... | collective-permute-start | bytes 1572872 | tf_op jit(solution)/shard_map/ppermute | solution.py:876
  226.9 22.8 %collective-permute-start.17 = (bf16[16,64,256]{2,1,0:T(8,128)(2,1)}, bf16[16,64,256]{2,1,0:T(8,128)(2,1)S(1)}, u32[]{:S(2)}, u32[]{:S(2)}) collective-permute-start(bf16[16,64,256]{2,1,0:T(8,128)(2,1)} %get-tuple-element.169.refs_10_), channel_id=1, source_target_pairs={{0,4},{1,5},{2,6},{3,7},{4,0},{5,1},{6,2},{7,3},{8,12},{9,13},{10,... | collective-permute-start | bytes 1572872 | tf_op jit(solution)/shard_map/ppermute | solution.py:876
  227.6 41.2 %collective-permute-start.20 = (bf16[16,128,256]{2,1,0:T(8,128)(2,1)}, bf16[16,128,256]{2,1,0:T(8,128)(2,1)S(1)}, u32[]{:S(2)}, u32[]{:S(2)}) collective-permute-start(bf16[16,128,256]{2,1,0:T(8,128)(2,1)} %bitcast.101), channel_id=1, source_target_pairs={{0,1},{1,0},{2,3},{3,2},{4,5},{5,4},{6,7},{7,6},{8,9},{9,8},{10,11... | collective-permute-start | bytes 3145736 | tf_op jit(solution)/shard_map/ppermute | solution.py:876
  237.4 12.9 %copy-start.15 = (bf16[16,64,256]{2,1,0:T(8,128)(2,1)}, bf16[16,64,256]{2,1,0:T(8,128)(2,1)S(1)}, u32[]{:S(2)}) copy-start(bf16[16,64,256]{2,1,0:T(8,128)(2,1)S(1)} %collective-permute-done.14.refs_5_) | copy-start | bytes 1572868
  237.4 12.9 %copy-start.16 = (bf16[16,64,256]{2,1,0:T(8,128)(2,1)}, bf16[16,64,256]{2,1,0:T(8,128)(2,1)S(1)}, u32[]{:S(2)}) copy-start(bf16[16,64,256]{2,1,0:T(8,128)(2,1)S(1)} %collective-permute-done.15.refs_7_.refs_8_) | copy-start | bytes 1572868
  256.9 99.0 %all-reduce.2.cloned.1.call-start = ((), (), s32[]{:S(2)}) async-start(), calls=%async_computation.4 | async-start | bytes 2097152 | tf_op jit(solution)/shard_map/psum | solution.py:1041
  256.9 13.6 %collective-permute-start.18 = (bf16[16,64,256]{2,1,0:T(8,128)(2,1)}, bf16[16,64,256]{2,1,0:T(8,128)(2,1)S(1)}, u32[]{:S(2)}, u32[]{:S(2)}) collective-permute-start(bf16[16,64,256]{2,1,0:T(8,128)(2,1)} %get-tuple-element.178.refs_11_), channel_id=1, source_target_pairs={{0,4},{1,5},{2,6},{3,7},{4,0},{5,1},{6,2},{7,3},{8,12},{9,13},{10,... | collective-permute-start | bytes 1572872 | tf_op jit(solution)/shard_map/ppermute | solution.py:876
  258.5 13.4 %collective-permute-start.19 = (bf16[16,64,256]{2,1,0:T(8,128)(2,1)}, bf16[16,64,256]{2,1,0:T(8,128)(2,1)S(1)}, u32[]{:S(2)}, u32[]{:S(2)}) collective-permute-start(bf16[16,64,256]{2,1,0:T(8,128)(2,1)} %get-tuple-element.179.refs_12_), channel_id=1, source_target_pairs={{0,2},{1,3},{2,0},{3,1},{4,6},{5,7},{6,4},{7,5},{8,10},{9,11},{10,... | collective-permute-start | bytes 1572872 | tf_op jit(solution)/shard_map/ppermute | solution.py:876
  259.0 12.8 %collective-permute-start.21 = (bf16[12,128,256]{2,1,0:T(8,128)(2,1)}, bf16[12,128,256]{2,1,0:T(8,128)(2,1)S(1)}, u32[]{:S(2)}, u32[]{:S(2)}) collective-permute-start(bf16[12,128,256]{2,1,0:T(8,128)(2,1)} %get-tuple-element.176.refs_9_), channel_id=1, source_target_pairs={{0,1},{1,0},{2,3},{3,2},{4,5},{5,4},{6,7},{7,6},{8,9},{9,8},{10,11... | collective-permute-start | bytes 2359304 | tf_op jit(solution)/shard_map/ppermute | solution.py:876
  268.9 3.0 copy-start.12
  279.7 12.9 %collective-permute-start.23 = (bf16[14,64,256]{2,1,0:T(8,128)(2,1)}, bf16[14,64,256]{2,1,0:T(8,128)(2,1)S(1)}, u32[]{:S(2)}, u32[]{:S(2)}) collective-permute-start(bf16[14,64,256]{2,1,0:T(8,128)(2,1)} %get-tuple-element.190.refs_14_), channel_id=1, source_target_pairs={{0,2},{1,3},{2,0},{3,1},{4,6},{5,7},{6,4},{7,5},{8,10},{9,11},{10,... | collective-permute-start | bytes 1376264 | tf_op jit(solution)/shard_map/ppermute | solution.py:876
  280.3 12.4 %collective-permute-start.24 = (bf16[14,64,256]{2,1,0:T(8,128)(2,1)}, bf16[14,64,256]{2,1,0:T(8,128)(2,1)S(1)}, u32[]{:S(2)}, u32[]{:S(2)}) collective-permute-start(bf16[14,64,256]{2,1,0:T(8,128)(2,1)} %get-tuple-element.191.refs_15_), channel_id=1, source_target_pairs={{0,4},{1,5},{2,6},{3,7},{4,0},{5,1},{6,2},{7,3},{8,12},{9,13},{10,... | collective-permute-start | bytes 1376264 | tf_op jit(solution)/shard_map/ppermute | solution.py:876
  281.4 14.0 %collective-permute-start.22 = (bf16[16,64,256]{2,1,0:T(8,128)(2,1)}, bf16[16,64,256]{2,1,0:T(8,128)(2,1)S(1)}, u32[]{:S(2)}, u32[]{:S(2)}) collective-permute-start(bf16[16,64,256]{2,1,0:T(8,128)(2,1)} %get-tuple-element.187.refs_11_), channel_id=1, source_target_pairs={{0,8},{8,0},{16,24},{24,16},{1,9},{9,1},{17,25},{25,17},{2,10},{10... | collective-permute-start | bytes 1572872 | tf_op jit(solution)/shard_map/ppermute | solution.py:660
  282.9 12.5 %collective-permute-start.25 = (bf16[12,128,256]{2,1,0:T(8,128)(2,1)}, bf16[12,128,256]{2,1,0:T(8,128)(2,1)S(1)}, u32[]{:S(2)}, u32[]{:S(2)}) collective-permute-start(bf16[12,128,256]{2,1,0:T(8,128)(2,1)} %get-tuple-element.185.refs_9_), channel_id=1, source_target_pairs={{0,1},{1,0},{2,3},{3,2},{4,5},{5,4},{6,7},{7,6},{8,9},{9,8},{10,11... | collective-permute-start | bytes 2359304 | tf_op jit(solution)/shard_map/ppermute | solution.py:876
  292.7 2.7 copy-start.9
  292.7 2.7 copy-start.10
  303.0 21.7 %collective-permute-start.26 = (bf16[16,32,256]{2,1,0:T(8,128)(2,1)}, bf16[16,32,256]{2,1,0:T(8,128)(2,1)S(1)}, u32[]{:S(2)}, u32[]{:S(2)}) collective-permute-start(bf16[16,32,256]{2,1,0:T(8,128)(2,1)} %get-tuple-element.201.refs_11_), channel_id=1, source_target_pairs={{0,16},{8,24},{16,0},{24,8},{1,17},{9,25},{17,1},{25,9},{2,18},{10... | collective-permute-start | bytes 786440 | tf_op jit(solution)/shard_map/ppermute | solution.py:660
  305.5 19.2 %collective-permute-start.27 = (bf16[13,64,256]{2,1,0:T(8,128)(2,1)}, bf16[13,64,256]{2,1,0:T(8,128)(2,1)S(1)}, u32[]{:S(2)}, u32[]{:S(2)}) collective-permute-start(bf16[13,64,256]{2,1,0:T(8,128)(2,1)} %get-tuple-element.204.refs_14_), channel_id=1, source_target_pairs={{0,4},{1,5},{2,6},{3,7},{4,0},{5,1},{6,2},{7,3},{8,12},{9,13},{10,... | collective-permute-start | bytes 1277960 | tf_op jit(solution)/shard_map/ppermute | solution.py:876
  306.9 17.7 %collective-permute-start.28 = (bf16[13,64,256]{2,1,0:T(8,128)(2,1)}, bf16[13,64,256]{2,1,0:T(8,128)(2,1)S(1)}, u32[]{:S(2)}, u32[]{:S(2)}) collective-permute-start(bf16[13,64,256]{2,1,0:T(8,128)(2,1)} %get-tuple-element.205.refs_15_), channel_id=1, source_target_pairs={{0,2},{1,3},{2,0},{3,1},{4,6},{5,7},{6,4},{7,5},{8,10},{9,11},{10,... | collective-permute-start | bytes 1277960 | tf_op jit(solution)/shard_map/ppermute | solution.py:876
  308.4 16.3 %collective-permute-start.29 = (bf16[12,128,256]{2,1,0:T(8,128)(2,1)}, bf16[12,128,256]{2,1,0:T(8,128)(2,1)S(1)}, u32[]{:S(2)}, u32[]{:S(2)}) collective-permute-start(bf16[12,128,256]{2,1,0:T(8,128)(2,1)} %get-tuple-element.199.refs_9_), channel_id=1, source_target_pairs={{0,1},{1,0},{2,3},{3,2},{4,5},{5,4},{6,7},{7,6},{8,9},{9,8},{10,11... | collective-permute-start | bytes 2359304 | tf_op jit(solution)/shard_map/ppermute | solution.py:876
  332.7 22.6 %collective-permute-start.33 = (bf16[16,32,256]{2,1,0:T(8,128)(2,1)}, bf16[16,32,256]{2,1,0:T(8,128)(2,1)S(1)}, u32[]{:S(2)}, u32[]{:S(2)}) collective-permute-start(bf16[16,32,256]{2,1,0:T(8,128)(2,1)} %get-tuple-element.217.refs_26_), channel_id=1, source_target_pairs={{0,16},{8,24},{16,0},{24,8},{1,17},{9,25},{17,1},{25,9},{2,18},{10... | collective-permute-start | bytes 786440 | tf_op jit(solution)/shard_map/ppermute | solution.py:660
  332.8 24.5 %collective-permute-start.31 = (bf16[9,64,256]{2,1,0:T(8,128)(2,1)}, bf16[9,64,256]{2,1,0:T(8,128)(2,1)S(1)}, u32[]{:S(2)}, u32[]{:S(2)}) collective-permute-start(bf16[9,64,256]{2,1,0:T(8,128)(2,1)} %get-tuple-element.214.refs_33_), channel_id=1, source_target_pairs={{0,2},{1,3},{2,0},{3,1},{4,6},{5,7},{6,4},{7,5},{8,10},{9,11},{10,... | collective-permute-start | bytes 884744 | tf_op jit(solution)/shard_map/ppermute | solution.py:876
  334.3 23.0 %collective-permute-start.32 = (bf16[9,64,256]{2,1,0:T(8,128)(2,1)}, bf16[9,64,256]{2,1,0:T(8,128)(2,1)S(1)}, u32[]{:S(2)}, u32[]{:S(2)}) collective-permute-start(bf16[9,64,256]{2,1,0:T(8,128)(2,1)} %get-tuple-element.216.refs_32_), channel_id=1, source_target_pairs={{0,4},{1,5},{2,6},{3,7},{4,0},{5,1},{6,2},{7,3},{8,12},{9,13},{10,... | collective-permute-start | bytes 884744 | tf_op jit(solution)/shard_map/ppermute | solution.py:876
  335.8 21.5 %collective-permute-start.34 = (bf16[14,64,256]{2,1,0:T(8,128)(2,1)}, bf16[14,64,256]{2,1,0:T(8,128)(2,1)S(1)}, u32[]{:S(2)}, u32[]{:S(2)}) collective-permute-start(bf16[14,64,256]{2,1,0:T(8,128)(2,1)} %get-tuple-element.220.refs_29_), channel_id=1, source_target_pairs={{0,8},{8,0},{16,24},{24,16},{1,9},{9,1},{17,25},{25,17},{2,10},{10... | collective-permute-start | bytes 1376264 | tf_op jit(solution)/shard_map/ppermute | solution.py:660
  337.5 19.9 %collective-permute-start.30 = (bf16[12,128,256]{2,1,0:T(8,128)(2,1)}, bf16[12,128,256]{2,1,0:T(8,128)(2,1)S(1)}, u32[]{:S(2)}, u32[]{:S(2)}) collective-permute-start(bf16[12,128,256]{2,1,0:T(8,128)(2,1)} %get-tuple-element.212.refs_24_), channel_id=1, source_target_pairs={{0,1},{1,0},{2,3},{3,2},{4,5},{5,4},{6,7},{7,6},{8,9},{9,8},{10,11... | collective-permute-start | bytes 2359304 | tf_op jit(solution)/shard_map/ppermute | solution.py:876
  355.3 2.0 copy-start.34
  355.4 1.9 collective-permute-start.35
  362.8 22.7 %collective-permute-start.39 = (bf16[8,64,256]{2,1,0:T(8,128)(2,1)}, bf16[8,64,256]{2,1,0:T(8,128)(2,1)S(1)}, u32[]{:S(2)}, u32[]{:S(2)}) collective-permute-start(bf16[8,64,256]{2,1,0:T(8,128)(2,1)} %get-tuple-element.233.refs_10_), channel_id=1, source_target_pairs={{0,6},{1,7},{2,4},{3,5},{4,2},{5,3},{6,0},{7,1},{8,14},{9,15},{10,... | collective-permute-start | bytes 786440 | tf_op jit(solution)/shard_map/ppermute | solution.py:876
  363.3 22.3 %collective-permute-start.37 = (bf16[11,64,256]{2,1,0:T(8,128)(2,1)}, bf16[11,64,256]{2,1,0:T(8,128)(2,1)S(1)}, u32[]{:S(2)}, u32[]{:S(2)}) collective-permute-start(bf16[11,64,256]{2,1,0:T(8,128)(2,1)} %get-tuple-element.231.refs_8_), channel_id=1, source_target_pairs={{0,2},{1,3},{2,0},{3,1},{4,6},{5,7},{6,4},{7,5},{8,10},{9,11},{10,... | collective-permute-start | bytes 1081352 | tf_op jit(solution)/shard_map/ppermute | solution.py:876
  364.9 20.6 %collective-permute-start.38 = (bf16[11,64,256]{2,1,0:T(8,128)(2,1)}, bf16[11,64,256]{2,1,0:T(8,128)(2,1)S(1)}, u32[]{:S(2)}, u32[]{:S(2)}) collective-permute-start(bf16[11,64,256]{2,1,0:T(8,128)(2,1)} %get-tuple-element.232.refs_9_), channel_id=1, source_target_pairs={{0,4},{1,5},{2,6},{3,7},{4,0},{5,1},{6,2},{7,3},{8,12},{9,13},{10,... | collective-permute-start | bytes 1081352 | tf_op jit(solution)/shard_map/ppermute | solution.py:876
  366.4 23.0 %collective-permute-start.36 = (bf16[28,32,256]{2,1,0:T(8,128)(2,1)}, bf16[28,32,256]{2,1,0:T(8,128)(2,1)S(1)}, u32[]{:S(2)}, u32[]{:S(2)}) collective-permute-start(bf16[28,32,256]{2,1,0:T(8,128)(2,1)} %get-tuple-element.238.refs_15_), channel_id=1, source_target_pairs={{0,16},{8,24},{16,0},{24,8},{1,17},{9,25},{17,1},{25,9},{2,18},{10... | collective-permute-start | bytes 1376264 | tf_op jit(solution)/shard_map/ppermute | solution.py:660
  367.5 27.6 %collective-permute-start.40 = (bf16[22,64,256]{2,1,0:T(8,128)(2,1)}, bf16[22,64,256]{2,1,0:T(8,128)(2,1)S(1)}, u32[]{:S(2)}, u32[]{:S(2)}) collective-permute-start(bf16[22,64,256]{2,1,0:T(8,128)(2,1)} %get-tuple-element.235.refs_12_), channel_id=1, source_target_pairs={{0,8},{8,0},{16,24},{24,16},{1,9},{9,1},{17,25},{25,17},{2,10},{10... | collective-permute-start | bytes 2162696 | tf_op jit(solution)/shard_map/ppermute | solution.py:660
  385.5 9.6 %copy-start.35 = (bf16[8,64,256]{2,1,0:T(8,128)(2,1)}, bf16[8,64,256]{2,1,0:T(8,128)(2,1)S(1)}, u32[]{:S(2)}) copy-start(bf16[8,64,256]{2,1,0:T(8,128)(2,1)S(1)} %collective-permute-done.39.refs_2_.refs_6_) | copy-start | bytes 786436
  385.5 9.6 %copy-start.30 = (bf16[11,64,256]{2,1,0:T(8,128)(2,1)}, bf16[11,64,256]{2,1,0:T(8,128)(2,1)S(1)}, u32[]{:S(2)}) copy-start(bf16[11,64,256]{2,1,0:T(8,128)(2,1)S(1)} %collective-permute-done.37.refs_0_.refs_4_.refs_13_) | copy-start | bytes 1081348
  385.6 9.6 %copy-start.31 = (bf16[11,64,256]{2,1,0:T(8,128)(2,1)}, bf16[11,64,256]{2,1,0:T(8,128)(2,1)S(1)}, u32[]{:S(2)}) copy-start(bf16[11,64,256]{2,1,0:T(8,128)(2,1)S(1)} %collective-permute-done.38.refs_1_.refs_5_.refs_10_) | copy-start | bytes 1081348
  389.3 5.8 %copy-start.27 = (bf16[28,32,256]{2,1,0:T(8,128)(2,1)}, bf16[28,32,256]{2,1,0:T(8,128)(2,1)S(1)}, u32[]{:S(2)}) copy-start(bf16[28,32,256]{2,1,0:T(8,128)(2,1)S(1)} %collective-permute-done.36.refs_22_.refs_23_.refs_0_.refs_2_) | copy-start | bytes 1376260
  401.5 15.6 %collective-permute-start.42 = (bf16[14,64,256]{2,1,0:T(8,128)(2,1)}, bf16[14,64,256]{2,1,0:T(8,128)(2,1)S(1)}, u32[]{:S(2)}, u32[]{:S(2)}) collective-permute-start(bf16[14,64,256]{2,1,0:T(8,128)(2,1)} %get-tuple-element.246), channel_id=1, source_target_pairs={{0,8},{8,0},{16,24},{24,16},{1,9},{9,1},{17,25},{25,17},{2,10},{10... | collective-permute-start | bytes 1376264 | tf_op jit(solution)/shard_map/ppermute | solution.py:660
  401.6 13.4 %collective-permute-start.41 = (bf16[12,32,256]{2,1,0:T(8,128)(2,1)}, bf16[12,32,256]{2,1,0:T(8,128)(2,1)S(1)}, u32[]{:S(2)}, u32[]{:S(2)}) collective-permute-start(bf16[12,32,256]{2,1,0:T(8,128)(2,1)} %get-tuple-element.244), channel_id=1, source_target_pairs={{0,16},{8,24},{16,0},{24,8},{1,17},{9,25},{17,1},{25,9},{2,18},{10... | collective-permute-start | bytes 589832 | tf_op jit(solution)/shard_map/ppermute | solution.py:660
  415.0 2.1 copy-start.37
  420.6 21.5 %collective-permute-start.43 = (bf16[28,32,256]{2,1,0:T(8,128)(2,1)}, bf16[28,32,256]{2,1,0:T(8,128)(2,1)S(1)}, u32[]{:S(2)}, u32[]{:S(2)}) collective-permute-start(bf16[28,32,256]{2,1,0:T(8,128)(2,1)} %get-tuple-element.250), channel_id=1, source_target_pairs={{0,16},{8,24},{16,0},{24,8},{1,17},{9,25},{17,1},{25,9},{2,18},{10... | collective-permute-start | bytes 1376264 | tf_op jit(solution)/shard_map/ppermute | solution.py:660
  (22 other events, 21.6 us)
Sparse Core Ops, SparseCore 0:
  44.2 58.4 all-gather.2
  104.6 54.4 all-gather.4
  162.6 87.6 reduce-scatter.1
  259.9 63.1 all-reduce.1
